TPU v7x, 32 devices: a whole 2x2x4 slice. The times are simulated.
32 devices in a mesh: scene: 2 (over x), row: 8 (over z, y), col: 2 (over core).
Axes of the slice: x: 2, y: 2, z: 4, core: 2. Of those that a mesh axis runs over, the one named last changes fastest.
Arguments:
- camera_probe_field: bfloat16 [256, 64, 1024], P(('scene', 'row'), 'col'), parts along dimension 0, may hold values from -135 to 135
- echo_lookup_field: bfloat16 [256, 64, 1024], P(('scene', 'row'), 'col'), parts along dimension 0, may hold values from -135 to 135
- echo_content_field: bfloat16 [256, 64, 1024], P(('scene', 'row'), 'col'), parts along dimension 0, may hold values from -135 to 135
- upstream_sensitivity: bfloat16 [256, 64, 1024], P(('scene', 'row'), 'col'), parts along dimension 0, may hold values from -6 to 6
- sharpness_factor: float32 [16], replicated, may hold values from 1 to 6
- final_projector: bfloat16 [1024, 1024], replicated, may hold values from -0.1875 to 0.1875
- neighborhood_filter: float32 [9, 1024], replicated, may hold values from -2 to 2
Outputs:
- merged_result: bfloat16 [256, 64, 1024], P(('scene', 'row'), 'col'), parts along dimension 0
- probe_sensitivity: bfloat16 [256, 64, 1024], P(('scene', 'row'), 'col'), parts along dimension 0
- lookup_sensitivity: bfloat16 [256, 64, 1024], P(('scene', 'row'), 'col'), parts along dimension 0
- content_sensitivity: bfloat16 [256, 64, 1024], P(('scene', 'row'), 'col'), parts along dimension 0
- sharpness_sensitivity: float32 [32], P('scene'), parts along dimension 0
- neighborhood_sensitivity: float32 [18, 1024], P('scene'), parts along dimension 0
- projector_sensitivity: float32 [2048, 1024], P(('scene', 'row', 'col')), parts along dimension 0
There are 2 independent parts, one for each index of `scene`. A program takes and returns all parts, laid end to end along the dimension named above; an argument that names none is the same for every part. Nothing has to cross between parts.
All inputs are finite; a program needn't handle non-finite values.
Results may differ from a plain program's by a relative error of at most 0.0095.
Values may be sent and summed in bfloat16 or wider, within the bound.
No kernel may reach another device: no remote copies, remote signals or barrier semaphores. Data moves between devices by JAX's collectives and lax.ppermute only.
A program may use at most 128 MiB of HBM per device.

v0:
```python
import jax
import jax.numpy as jnp
from jax import lax
from jax.sharding import PartitionSpec as P

epsilon = 1e-06
inverse_root = 0.7071067811865476
density_root = 0.3989422804014327


def with_halo(cells, sides, width):
    for axis, dim in sides:
        count = lax.axis_size(axis)
        ends = count - 1
        head = lax.slice_in_dim(cells, 0, width, axis=dim)
        tail = lax.slice_in_dim(cells, cells.shape[dim] - width, cells.shape[dim], axis=dim)
        cells = jnp.concatenate(
            [
                lax.ppermute(tail, axis, [(i, (i + 1) % count) for i in range(ends)]),
                cells,
                lax.ppermute(head, axis, [((i + 1) % count, i) for i in range(ends)]),
            ],
            axis=dim,
        )
    return cells


def gelu_pair(field):
    cumul = 0.5 * (1.0 + lax.erf(field * inverse_root))
    return (field * cumul, cumul + field * jnp.exp(-0.5 * field * field) * density_root)


def stencil_apply(padded, neighborhood_filter):
    tile_rows = padded.shape[0] - 2
    tile_cols = padded.shape[1] - 2
    total = jnp.zeros((tile_rows, tile_cols, padded.shape[2]), jnp.float32)
    for shift_row in range(3):
        for shift_col in range(3):
            total = (
                total
                + neighborhood_filter[3 * shift_row + shift_col]
                * padded[shift_row : shift_row + tile_rows, shift_col : shift_col + tile_cols]
            )
    return total


def stencil_back(padded_slope, neighborhood_filter):
    tile_rows = padded_slope.shape[0] - 2
    tile_cols = padded_slope.shape[1] - 2
    total = jnp.zeros((tile_rows, tile_cols, padded_slope.shape[2]), jnp.float32)
    for shift_row in range(3):
        for shift_col in range(3):
            total = (
                total
                + neighborhood_filter[3 * shift_row + shift_col]
                * padded_slope[
                    2 - shift_row : 2 - shift_row + tile_rows,
                    2 - shift_col : 2 - shift_col + tile_cols,
                ]
            )
    return total


def stencil_weights(slope_mid, padded_field):
    tile_rows = slope_mid.shape[0]
    tile_cols = slope_mid.shape[1]
    taps = []
    for shift_row in range(3):
        for shift_col in range(3):
            window = padded_field[
                shift_row : shift_row + tile_rows, shift_col : shift_col + tile_cols
            ]
            taps.append(jnp.sum(slope_mid.astype(jnp.float32) * window, axis=(0, 1)))
    return jnp.stack(taps, axis=0)


def shards(
    camera_probe_field,
    echo_lookup_field,
    echo_content_field,
    upstream_sensitivity,
    sharpness_factor,
    final_projector,
    neighborhood_filter,
):
    tile_rows, tile_cols, width = camera_probe_field.shape
    per_group_layout = sharpness_factor.shape[0]
    head_size = width // per_group_layout
    token_count = tile_rows * tile_cols
    target_rim = with_halo(upstream_sensitivity, (("row", 0), ("col", 1)), 1)
    query_heads = camera_probe_field.reshape(token_count, per_group_layout, head_size)
    key_heads = echo_lookup_field.reshape(token_count, per_group_layout, head_size)
    value_heads = echo_content_field.reshape(token_count, per_group_layout, head_size)
    query_local = jnp.sum(jnp.square(query_heads.astype(jnp.float32)), axis=0)
    key_local = jnp.sum(jnp.square(key_heads.astype(jnp.float32)), axis=0)
    gram_local = jnp.einsum(
        "nhi,nhj->hij", query_heads, key_heads, preferred_element_type=jnp.float32
    )
    query_energy, key_energy, raw_gram = lax.psum(
        (query_local, key_local, gram_local), ("row", "col")
    )
    query_scale = lax.rsqrt(query_energy + epsilon)
    key_scale = lax.rsqrt(key_energy + epsilon)
    channel_similarity = query_scale[:, :, None] * raw_gram * key_scale[:, None, :]
    softmax_numerators = jnp.exp(sharpness_factor[:, None, None] * channel_similarity)
    attention = softmax_numerators / jnp.sum(softmax_numerators, axis=2, keepdims=True)
    attention_low = attention.astype(jnp.bfloat16)
    mixed_low = (
        jnp.einsum("nhj,hij->nhi", value_heads, attention_low, preferred_element_type=jnp.float32)
        .astype(jnp.bfloat16)
        .reshape(token_count, width)
    )
    projected = jnp.dot(mixed_low, final_projector, preferred_element_type=jnp.float32).reshape(
        tile_rows, tile_cols, width
    )
    projected_low = projected.astype(jnp.bfloat16)
    field_wide = with_halo(projected_low, (("row", 0), ("col", 1)), 2)
    stencil_wide = stencil_apply(field_wide, neighborhood_filter)
    activated_wide, slope_wide = gelu_pair(stencil_wide)
    activated = activated_wide[1:-1, 1:-1]
    slope_rim = (target_rim.astype(jnp.float32) * slope_wide).astype(jnp.bfloat16)
    field_rim = field_wide[1:-1, 1:-1]
    merged_result = (projected + activated).astype(jnp.bfloat16)
    stencil_local = stencil_weights(slope_rim[1:-1, 1:-1], field_rim)
    target_low = (
        upstream_sensitivity.astype(jnp.float32) + stencil_back(slope_rim, neighborhood_filter)
    ).astype(jnp.bfloat16)
    target_flat = target_low.reshape(token_count, width)
    mixed_grad_low = lax.dot_general(
        target_flat, final_projector, (((1,), (1,)), ((), ())), preferred_element_type=jnp.float32
    ).astype(jnp.bfloat16)
    grad_heads = mixed_grad_low.reshape(token_count, per_group_layout, head_size)
    attention_local = jnp.einsum(
        "nhi,nhj->hij", grad_heads, value_heads, preferred_element_type=jnp.float32
    )
    content_sensitivity = jnp.einsum(
        "nhi,hij->nhj", grad_heads, attention_low, preferred_element_type=jnp.float32
    ).astype(jnp.bfloat16)
    attention_grad, neighborhood_sensitivity = lax.psum(
        (attention_local, stencil_local), ("row", "col")
    )
    logit_sensitivity = attention * (
        attention_grad - jnp.sum(attention * attention_grad, axis=2, keepdims=True)
    )
    sharpness_sensitivity = jnp.sum(logit_sensitivity * channel_similarity, axis=(1, 2))
    similarity_sensitivity = sharpness_factor[:, None, None] * logit_sensitivity
    query_corr = jnp.sum(similarity_sensitivity * channel_similarity, axis=2)
    key_corr = jnp.sum(similarity_sensitivity * channel_similarity, axis=1)
    mixer_low = (query_scale[:, :, None] * similarity_sensitivity * key_scale[:, None, :]).astype(
        jnp.bfloat16
    )
    probe_sensitivity = (
        jnp.einsum("nhj,hij->nhi", key_heads, mixer_low, preferred_element_type=jnp.float32)
        - query_heads * (query_scale * query_scale * query_corr)[None]
    )
    lookup_sensitivity = (
        jnp.einsum("nhi,hij->nhj", query_heads, mixer_low, preferred_element_type=jnp.float32)
        - key_heads * (key_scale * key_scale * key_corr)[None]
    )
    projector_sensitivity = lax.psum_scatter(
        lax.dot_general(
            mixed_low, target_flat, (((0,), (0,)), ((), ())), preferred_element_type=jnp.float32
        ),
        ("row", "col"),
        scatter_dimension=0,
        tiled=True,
    )
    shape_tile = (tile_rows, tile_cols, width)
    return (
        merged_result,
        probe_sensitivity.astype(jnp.bfloat16).reshape(shape_tile),
        lookup_sensitivity.astype(jnp.bfloat16).reshape(shape_tile),
        content_sensitivity.reshape(shape_tile),
        sharpness_sensitivity,
        neighborhood_sensitivity,
        projector_sensitivity,
    )


def solution(mesh):
    placed = (
        P(("scene", "row"), "col", None),
        P(("scene", "row"), "col", None),
        P(("scene", "row"), "col", None),
        P(("scene", "row"), "col", None),
        P(),
        P(),
        P(),
    )
    return jax.shard_map(
        shards,
        mesh=mesh,
        in_specs=placed,
        out_specs=(
            P(("scene", "row"), "col", None),
            P(("scene", "row"), "col", None),
            P(("scene", "row"), "col", None),
            P(("scene", "row"), "col", None),
            P("scene"),
            P("scene", None),
            P(("scene", "row", "col"), None),
        ),
        check_vma=False,
    )
```

profile of v0, /device:TPU:0, one launch (start us, length us, event | category | flops | bytes accessed | tf_op | source)
XLA Modules:
  0.0 352.6 jit_solution(17960278457043749886)
XLA Ops:
  9.6 5.5 %collective-permute-start.4 = (bf16[1,32,1024]{2,1,0:T(8,128)(2,1)S(1)}, bf16[1,32,1024]{2,1,0:T(8,128)(2,1)S(1)}, u32[]{:S(2)}, u32[]{:S(2)}) collective-permute-start(bf16[1,32,1024]{2,1,0:T(8,128)(2,1)S(1)} %get-tuple-element.46), channel_id=1, source_target_pairs={{0,2},{2,4},{4,6},{6,8},{8,10},{10,12},{12,14},{1,3},{3,5},{5,7},{... | collective-permute-start | bytes 196616 | tf_op jit(solution)/shard_map/ppermute | solution.py:19
  15.1 4.1 %reshape.62 = bf16[512,16,64]{2,1,0:T(8,128)(2,1)} reshape(bf16[16,32,1024]{2,1,0:T(8,128)(2,1)} %param.7) | data formatting | bytes 2097152 | tf_op jit(solution)/shard_map/reshape | solution.py:91
  19.1 3.4 copy.26
  24.9 3.3 copy.27
  28.2 2.8 fusion.59
  33.0 59.6 %all-reduce = (f32[16,64]{1,0:T(8,128)S(1)}, f32[16,64]{1,0:T(8,128)S(1)}) all-reduce(f32[16,64]{1,0:T(8,128)S(1)} %reduce_sum.151, f32[16,64]{1,0:T(8,128)S(1)} %reduce_sum.149), channel_id=1, replica_groups=mesh['scene'=2,'row'=8,'col'=2] {'row','col'}, use_global_device_ids=true, to_apply=%region_4.0 | all-reduce | flops 2048 | bytes 16384 | tf_op jit(solution)/shard_map/psum | solution.py:99
  93.3 4.1 %reshape.64 = bf16[512,16,64]{2,1,0:T(8,128)(2,1)} reshape(bf16[16,32,1024]{2,1,0:T(8,128)(2,1)} %param.9) | data formatting | bytes 2097152 | tf_op jit(solution)/shard_map/reshape | solution.py:93
  100.6 22.4 %all-reduce.4.cloned.1.call-done = f32[16,64,64]{2,1,0:T(8,128)} async-done(((f32[16,64,64]{2,1,0:T(8,128)}), f32[16,64,64]{2,1,0:T(8,128)}) %all-reduce.4.cloned.1.call-update) | async-done | bytes 262160 | tf_op jit(solution)/shard_map/psum | solution.py:99
  127.0 3.9 %copy.29 = bf16[512,16,64]{2,1,0:T(8,128)(2,1)} copy(bf16[512,16,64]{0,2,1:T(8,128)(2,1)} %bitcast.53) | data formatting | bytes 2097152 | tf_op jit(solution)/shard_map/convert_element_type | solution.py:110
  130.9 4.1 %dot_general.31 = bf16[16,32,1024]{2,1,0:T(8,128)(2,1)} reshape(bf16[512,16,64]{2,1,0:T(8,128)(2,1)} %copy.29) | data formatting | bytes 2097152 | tf_op jit(solution)/shard_map/dot_general | solution.py:113
  135.0 3.9 %fusion.58 = (bf16[16,32,1024]{2,1,0:T(8,128)(2,1)S(1)}, f32[16,32,1024]{2,1,0:T(8,128)}) fusion(bf16[16,32,1024]{2,1,0:T(8,128)(2,1)} %dot_general.31, bf16[1024,1024]{1,0:T(8,128)(2,1)S(1)} %copy-done), kind=kOutput, calls=%fused_computation.85 | convolution fusion | flops 1074266112 | bytes 6291456 | tf_op jit(solution)/shard_map/dot_general | solution.py:113
  144.8 5.2 %collective-permute-done.1 = bf16[2,32,1024]{2,1,0:T(8,128)(2,1)S(1)} collective-permute-done((bf16[2,32,1024]{2,1,0:T(8,128)(2,1)S(1)}, bf16[2,32,1024]{2,1,0:T(8,128)(2,1)S(1)}, u32[]{:S(2)}, u32[]{:S(2)}) %collective-permute-start.1) | collective-permute-done | bytes 131104 | tf_op jit(solution)/shard_map/ppermute | solution.py:21
  152.9 3.0 collective-permute-start.6
  159.6 6.6 %fusion.6 = (bf16[18,34,1024]{2,1,0:T(8,128)(2,1)S(1)}, f32[18,34,1024]{2,1,0:T(8,128)}, f32[18,34,1024]{2,1,0:T(8,128)}) fusion(bf16[18,1,1024]{2,1,0:T(2,128)(2,1)S(1)} %collective-permute-done.7, bf16[18,32,1024]{2,1,0:T(8,128)(2,1)S(1)} %constant_dynamic-update-slice_fusion, bf16[18,1,1024]{2,1,0:T(2,128)(2,1)S(1)} %collective-permute-done.6, ...), kind=kLoop, calls=%fused_computation.17 | loop fusion | flops 26320896 | bytes 18837504 | tf_op jit(solution)/shard_map/convert_element_type | solution.py:121
  166.2 2.7 fusion.13
  174.4 2.7 fusion.60
  177.2 4.7 %fusion.61 = f32[1024,1024]{1,0:T(8,128)} fusion(bf16[512,1024]{0,1:T(8,128)(2,1)} %bitcast.54, bf16[512,1024]{1,0:T(8,128)(2,1)} %bitcast.56), kind=kOutput, calls=%fused_computation.88 | convolution fusion | flops 1073741824 | bytes 6291456 | tf_op jit(solution)/shard_map/dot_general | solution.py:161
  182.6 3.3 fusion.29
  186.0 3.8 %copy.40 = bf16[512,16,64]{2,1,0:T(8,128)(2,1)} copy(bf16[512,16,64]{0,2,1:T(8,128)(2,1)} %fusion.29) | data formatting | bytes 2097152 | tf_op jit(solution)/shard_map/convert_element_type | solution.py:138
  189.8 4.1 %reshape.69 = bf16[16,32,1024]{2,1,0:T(8,128)(2,1)} reshape(bf16[512,16,64]{2,1,0:T(8,128)(2,1)} %copy.40) | data formatting | bytes 2097152 | tf_op jit(solution)/shard_map/reshape | solution.py:173
  193.8 6.0 %fusion.22 = (f32[1024]{0:T(1024)S(1)}, f32[1024]{0:T(1024)S(1)}, f32[1024]{0:T(1024)S(1)}, f32[1024]{0:T(1024)S(1)}, f32[1024]{0:T(1024)S(1)}, /*index=5*/f32[1...) fusion(bf16[20,34,1024]{2,1,0:T(8,128)(2,1)} %copy-done.3, bf16[18,34,1024]{2,1,0:T(8,128)(2,1)} %copy-done.1, ...), kind=kLoop, calls=%fused_computation.35 | loop fusion | flops 15719424 | bytes 8687616 | tf_op jit(solution)/shard_map/reduce_sum | solution.py:73
  199.9 60.6 %psum.39 = f32[9,1024]{1,0:T(8,128)} all-reduce(f32[9,1024]{1,0:T(8,128)S(1)} %stack.39), channel_id=1, replica_groups=mesh['scene'=2,'row'=8,'col'=2] {'row','col'}, use_global_device_ids=true, to_apply=%region_20.0 | all-reduce | flops 9216 | bytes 73728 | tf_op jit(solution)/shard_map/psum | solution.py:139
  260.6 5.1 %fusion.24 = bf16[16,32,1024]{2,1,0:T(8,128)(2,1)} fusion(f32[16,32,1024]{2,1,0:T(8,128)} %get-tuple-element.57, f32[18,34,1024]{2,1,0:T(8,128)} %get-tuple-element.32, f32[18,34,1024]{2,1,0:T(8,128)} %get-tuple-element.33), kind=kLoop, calls=%fused_computation.38 | loop fusion | flops 1572864 | bytes 7340032 | tf_op jit(solution)/shard_map/convert_element_type | solution.py:123
  265.6 3.0 all-reduce.6.cloned.1.call-done
  268.6 8.9 %fusion.37 = (f32[16,64]{1,0:T(8,128)S(1)}, f32[16,64]{1,0:T(8,128)S(1)}, f32[16]{0:T(128)}) fusion(f32[16,64]{1,0:T(8,128)S(1)} %copy-done.17, f32[16,64,64]{2,1,0:T(8,128)} %all-reduce.4.cloned.1.call-done, f32[16,64]{1,0:T(8,128)S(1)} %copy-done.19, f32[16]{0:T(128)S(1)} %copy-done.28, f32[16,64,64]{2,1,0:T(8,128)} %all-reduce.6.cloned.1.call-done, ...), kind=kOutput, calls=%fused_computation.79 | output fusion | flops 1113135 | bytes 544896 | tf_op jit(solution)/shard_map/sub | solution.py:143
  277.6 9.9 %fusion.26 = bf16[512,16,64]{0,2,1:T(8,128)(2,1)} fusion(bf16[512,16,64]{0,2,1:T(8,128)(2,1)S(1)} %copy-done.7, bf16[512,16,64]{0,2,1:T(8,128)(2,1)} %copy.27, f32[16,64]{1,0:T(8,128)S(1)} %get-tuple-element.59, f32[16,64]{1,0:T(8,128)S(1)} %copy-done.17, f32[16,64]{1,0:T(8,128)S(1)} %copy-done.19, f32[16]{0:T(128)S(1)} %copy-done.28, ...), kind=kOutput, calls=%fused_computation.42 | convolution fusion | flops 70190144 | bytes 3686464 | tf_op jit(solution)/shard_map/nhj,hij->nhi/dot_general | solution.py:153
  287.5 3.9 %copy.34 = bf16[512,16,64]{2,1,0:T(8,128)(2,1)} copy(bf16[512,16,64]{0,2,1:T(8,128)(2,1)} %fusion.26) | data formatting | bytes 2097152 | tf_op jit(solution)/shard_map/convert_element_type | solution.py:171
  291.3 4.1 %reshape.67 = bf16[16,32,1024]{2,1,0:T(8,128)(2,1)} reshape(bf16[512,16,64]{2,1,0:T(8,128)(2,1)} %copy.34) | data formatting | bytes 2097152 | tf_op jit(solution)/shard_map/reshape | solution.py:171
  295.5 9.9 %fusion.25 = bf16[512,16,64]{0,2,1:T(8,128)(2,1)} fusion(bf16[512,16,64]{0,2,1:T(8,128)(2,1)} %copy.27, bf16[512,16,64]{0,2,1:T(8,128)(2,1)S(1)} %copy-done.7, f32[16,64]{1,0:T(8,128)S(1)} %get-tuple-element.58, f32[16,64]{1,0:T(8,128)S(1)} %copy-done.17, f32[16,64]{1,0:T(8,128)S(1)} %copy-done.19, f32[16]{0:T(128)S(1)} %copy-done.28, ...), kind=kOutput, calls=%fused_computation.40 | convolution fusion | flops 70190144 | bytes 3686464 | tf_op jit(solution)/shard_map/nhi,hij->nhj/dot_general | solution.py:157
  305.4 3.8 %copy.38 = bf16[512,16,64]{2,1,0:T(8,128)(2,1)} copy(bf16[512,16,64]{0,2,1:T(8,128)(2,1)} %fusion.25) | data formatting | bytes 2097152 | tf_op jit(solution)/shard_map/convert_element_type | solution.py:172
  309.3 4.1 %reshape.68 = bf16[16,32,1024]{2,1,0:T(8,128)(2,1)} reshape(bf16[512,16,64]{2,1,0:T(8,128)(2,1)} %copy.38) | data formatting | bytes 2097152 | tf_op jit(solution)/shard_map/reshape | solution.py:172
  313.4 32.7 %reduce-scatter.2.cloned.1.call-done = f32[64,1024]{1,0:T(8,128)} async-done(((f32[1024,1024]{1,0:T(8,128)}), f32[64,1024]{1,0:T(8,128)}) %reduce-scatter.2.cloned.1.call-update) | async-done | bytes 262160 | tf_op jit(solution)/shard_map/reduce_scatter | solution.py:160
  (101 shorter events, 33.0 us)
Async XLA Ops:
  7.2 127.8 %copy-start = (bf16[1024,1024]{1,0:T(8,128)(2,1)S(1)}, bf16[1024,1024]{1,0:T(8,128)(2,1)}, u32[]{:S(2)}) copy-start(bf16[1024,1024]{1,0:T(8,128)(2,1)} %param.12) | copy-start | bytes 6291460
  7.2 115.8 %all-reduce.4.cloned.1.call-start = ((), (), s32[]{:S(2)}) async-start(), calls=%async_computation.1 | async-start | bytes 1048576 | tf_op jit(solution)/shard_map/psum | solution.py:99
  8.3 134.6 %collective-permute-start.5 = (bf16[1,32,1024]{2,1,0:T(8,128)(2,1)S(1)}, bf16[1,32,1024]{2,1,0:T(8,128)(2,1)S(1)}, u32[]{:S(2)}, u32[]{:S(2)}) collective-permute-start(bf16[1,32,1024]{2,1,0:T(8,128)(2,1)S(1)} %get-tuple-element.45), channel_id=1, source_target_pairs={{2,0},{4,2},{6,4},{8,6},{10,8},{12,10},{14,12},{3,1},{5,3},{7,5},{... | collective-permute-start | bytes 196616 | tf_op jit(solution)/shard_map/ppermute | solution.py:21
  9.6 90.3 %collective-permute-start.4 = (bf16[1,32,1024]{2,1,0:T(8,128)(2,1)S(1)}, bf16[1,32,1024]{2,1,0:T(8,128)(2,1)S(1)}, u32[]{:S(2)}, u32[]{:S(2)}) collective-permute-start(bf16[1,32,1024]{2,1,0:T(8,128)(2,1)S(1)} %get-tuple-element.46), channel_id=1, source_target_pairs={{0,2},{2,4},{4,6},{6,8},{8,10},{10,12},{12,14},{1,3},{3,5},{5,7},{... | collective-permute-start | bytes 196616 | tf_op jit(solution)/shard_map/ppermute | solution.py:19
  19.1 3.4 copy-start.6
  28.2 2.9 copy-start.5
  28.2 64.4 %copy-start.24 = (f32[9,1024]{1,0:T(8,128)S(1)}, f32[9,1024]{1,0:T(8,128)}, u32[]{:S(2)}) copy-start(f32[9,1024]{1,0:T(8,128)} %param.13) | copy-start | bytes 110596
  31.1 237.6 %all-reduce.6.cloned.1.call-start = ((), (), s32[]{:S(2)}) async-start(), calls=%async_computation.2 | async-start | bytes 1048576 | tf_op jit(solution)/shard_map/psum | solution.py:139
  92.6 7.3 %copy-start.20 = (f32[16,64]{1,0:T(8,128)}, f32[16,64]{1,0:T(8,128)S(1)}, u32[]{:S(2)}) copy-start(f32[16,64]{1,0:T(8,128)S(1)} %get-tuple-element.29) | copy-start | bytes 12292
  92.6 7.3 %copy-start.22 = (f32[16,64]{1,0:T(8,128)}, f32[16,64]{1,0:T(8,128)S(1)}, u32[]{:S(2)}) copy-start(f32[16,64]{1,0:T(8,128)S(1)} %get-tuple-element.30) | copy-start | bytes 12292
  92.6 31.9 %copy-start.16 = (f32[16,64]{1,0:T(8,128)}, f32[16,64]{1,0:T(8,128)S(1)}, u32[]{:S(2)}) copy-start(f32[16,64]{1,0:T(8,128)S(1)} %add_rsqrt_fusion) | copy-start | bytes 12292
  93.3 31.2 %copy-start.18 = (f32[16,64]{1,0:T(8,128)}, f32[16,64]{1,0:T(8,128)S(1)}, u32[]{:S(2)}) copy-start(f32[16,64]{1,0:T(8,128)S(1)} %add_rsqrt_fusion.1) | copy-start | bytes 12292
  97.3 25.7 %copy-start.27 = (f32[16]{0:T(128)S(1)}, f32[16]{0:T(128)}, u32[]{:S(2)}) copy-start(f32[16]{0:T(128)} %param.11) | copy-start | bytes 196
  99.9 31.0 %copy-start.8 = (bf16[512,16,64]{0,2,1:T(8,128)(2,1)}, bf16[512,16,64]{0,2,1:T(8,128)(2,1)S(1)}, u32[]{:S(2)}) copy-start(bf16[512,16,64]{0,2,1:T(8,128)(2,1)S(1)} %copy.28) | copy-start | bytes 3145732
  124.5 6.4 %copy-start.25 = (f32[16,64]{1,0:T(8,128)}, f32[16,64]{1,0:T(8,128)S(1)}, u32[]{:S(2)}) copy-start(f32[16,64]{1,0:T(8,128)S(1)} %fusion.34) | copy-start | bytes 12292
  135.0 7.8 %copy-start.4 = (bf16[16,32,1024]{2,1,0:T(8,128)(2,1)S(1)}, bf16[16,32,1024]{2,1,0:T(8,128)(2,1)}, u32[]{:S(2)}) copy-start(bf16[16,32,1024]{2,1,0:T(8,128)(2,1)} %param.10) | copy-start | bytes 3145732
  135.0 7.8 %copy-start.9 = (bf16[18,32,1024]{2,1,0:T(8,128)(2,1)S(1)}, bf16[18,32,1024]{2,1,0:T(8,128)(2,1)}, u32[]{:S(2)}) copy-start(bf16[18,32,1024]{2,1,0:T(8,128)(2,1)} %constant_dynamic-update-slice_fusion.2) | copy-start | bytes 3538948
  139.0 5.9 %collective-permute-start = (bf16[2,32,1024]{2,1,0:T(8,128)(2,1)S(1)}, bf16[2,32,1024]{2,1,0:T(8,128)(2,1)S(1)}, u32[]{:S(2)}, u32[]{:S(2)}) collective-permute-start(bf16[2,32,1024]{2,1,0:T(8,128)(2,1)S(1)} %get-tuple-element.43), channel_id=1, source_target_pairs={{0,2},{2,4},{4,6},{6,8},{8,10},{10,12},{12,14},{1,3},{3,5},{5,7},{... | collective-permute-start | bytes 393224 | tf_op jit(solution)/shard_map/ppermute | solution.py:19
  141.5 8.6 %collective-permute-start.1 = (bf16[2,32,1024]{2,1,0:T(8,128)(2,1)S(1)}, bf16[2,32,1024]{2,1,0:T(8,128)(2,1)S(1)}, u32[]{:S(2)}, u32[]{:S(2)}) collective-permute-start(bf16[2,32,1024]{2,1,0:T(8,128)(2,1)S(1)} %get-tuple-element.44), channel_id=1, source_target_pairs={{2,0},{4,2},{6,4},{8,6},{10,8},{12,10},{14,12},{3,1},{5,3},{7,5},{... | collective-permute-start | bytes 393224 | tf_op jit(solution)/shard_map/ppermute | solution.py:21
  150.2 7.3 %collective-permute-start.2 = (bf16[20,2,1024]{2,1,0:T(2,128)(2,1)S(1)}, bf16[20,2,1024]{2,1,0:T(2,128)(2,1)S(1)}, u32[]{:S(2)}, u32[]{:S(2)}) collective-permute-start(bf16[20,2,1024]{2,1,0:T(2,128)(2,1)S(1)} %get-tuple-element.39), channel_id=1, source_target_pairs={{0,1},{2,3},{4,5},{6,7},{8,9},{10,11},{12,13},{14,15},{16,17},{18,... | collective-permute-start | bytes 245768 | tf_op jit(solution)/shard_map/ppermute | solution.py:19
  151.5 6.0 %collective-permute-start.3 = (bf16[20,2,1024]{2,1,0:T(2,128)(2,1)S(1)}, bf16[20,2,1024]{2,1,0:T(2,128)(2,1)S(1)}, u32[]{:S(2)}, u32[]{:S(2)}) collective-permute-start(bf16[20,2,1024]{2,1,0:T(2,128)(2,1)S(1)} %get-tuple-element.40), channel_id=1, source_target_pairs={{1,0},{3,2},{5,4},{7,6},{9,8},{11,10},{13,12},{15,14},{17,16},{19,... | collective-permute-start | bytes 245768 | tf_op jit(solution)/shard_map/ppermute | solution.py:21
  152.9 6.5 %collective-permute-start.6 = (bf16[18,1,1024]{2,1,0:T(2,128)(2,1)S(1)}, bf16[18,1,1024]{2,1,0:T(2,128)(2,1)S(1)}, u32[]{:S(2)}, u32[]{:S(2)}) collective-permute-start(bf16[18,1,1024]{2,1,0:T(2,128)(2,1)S(1)} %get-tuple-element.41), channel_id=1, source_target_pairs={{0,1},{2,3},{4,5},{6,7},{8,9},{10,11},{12,13},{14,15},{16,17},{18,... | collective-permute-start | bytes 110600 | tf_op jit(solution)/shard_map/ppermute | solution.py:19
  156.0 3.5 collective-permute-start.7
  158.4 7.7 %copy-start.2 = (bf16[20,34,1024]{2,1,0:T(8,128)(2,1)}, bf16[20,34,1024]{2,1,0:T(8,128)(2,1)S(1)}, u32[]{:S(2)}) copy-start(bf16[20,34,1024]{2,1,0:T(8,128)(2,1)S(1)} %get-tuple-element.37) | copy-start | bytes 4177924
  158.4 7.7 %copy-start.3 = (bf16[20,34,1024]{2,1,0:T(8,128)(2,1)}, bf16[20,34,1024]{2,1,0:T(8,128)(2,1)S(1)}, u32[]{:S(2)}) copy-start(bf16[20,34,1024]{2,1,0:T(8,128)(2,1)S(1)} %get-tuple-element.38) | copy-start | bytes 4177924
  158.4 1.1 copy-start.11
  158.4 1.1 copy-start.12
  166.2 2.7 copy-start.1
  177.1 168.9 %reduce-scatter.2.cloned.1.call-start = ((), (), s32[]{:S(2)}) async-start(), calls=%async_computation.3 | async-start | bytes 4456448 | tf_op jit(solution)/shard_map/reduce_scatter | solution.py:160
  265.6 11.9 %copy-start.21 = (f32[16,64]{1,0:T(8,128)S(1)}, f32[16,64]{1,0:T(8,128)}, u32[]{:S(2)}) copy-start(f32[16,64]{1,0:T(8,128)} %copy-done.20) | copy-start | bytes 12292
  265.6 11.9 %copy-start.23 = (f32[16,64]{1,0:T(8,128)S(1)}, f32[16,64]{1,0:T(8,128)}, u32[]{:S(2)}) copy-start(f32[16,64]{1,0:T(8,128)} %copy-done.22) | copy-start | bytes 12292
  265.6 11.9 %copy-start.7 = (bf16[512,16,64]{0,2,1:T(8,128)(2,1)S(1)}, bf16[512,16,64]{0,2,1:T(8,128)(2,1)}, u32[]{:S(2)}) copy-start(bf16[512,16,64]{0,2,1:T(8,128)(2,1)} %copy.26) | copy-start | bytes 3145732
  (8 other events, 7.0 us)
Sparse Core Ops, SparseCore 0:
  31.2 91.7 all-reduce.3
  177.3 91.3 all-reduce.5
  273.1 72.9 reduce-scatter.1
where the time goes:
time: 354 us; the launch traced here: 353 us
  blocking collectives  120 us (34%)
  waiting for transfers between devices  65.3 us (18%)
  local copies, waits for them, and re-layouts  58.3 us (16%)
  matrix products  42.2 us (12%)
  other arithmetic  34.5 us (10%)
  starting transfers between devices  17.8 us (5%)
  between operations  14.2 us (4%)
    psum x1, blocking collectives, shards(): lax.psum((attention_local, stencil_local), ('row', 'col'))  60.6 us
    psum x1, blocking collectives, shards(): lax.psum((query_local, key_local, gram_local), ('row', 'col'))  59.6 us
    reduce_scatter x1, waiting for transfers between devices, shards(): lax.psum_scatter(lax.dot_general(mixed_low, target_flat, (((0,), (0,)), (...  32.7 us
    psum x1, waiting for transfers between devices, shards(): lax.psum((query_local, key_local, gram_local), ('row', 'col'))  22.4 us
    ppermute x4, starting transfers between devices, with_halo(): lax.ppermute(tail, axis, [(i, (i + 1) % count) for i in range(ends)])  12.3 us
    dot_general x1, matrix products, shards(): jnp.einsum('nhi,hij->nhj', query_heads, mixer_low, preferred_element_type...  9.95 us
    dot_general x1, matrix products, shards(): jnp.einsum('nhj,hij->nhi', key_heads, mixer_low, preferred_element_type=j...  9.9 us
    sub x1, other arithmetic, shards(): attention_grad - jnp.sum(attention * attention_grad, axis=2, keepdims=True)  8.93 us
  transfers between devices with their start and end apart: 11, of which 5 were waited for; matrix products, arithmetic and copies ran while one was open for 33% of the time, Pallas kernels for 0%

commit v1 on v0

v1 whole, which is shorter than its diff:
```python
import functools

import jax
import jax.numpy as jnp
from jax import lax
from jax.experimental import pallas as pl
from jax.experimental.pallas import tpu as pltpu
from jax.sharding import PartitionSpec as P

epsilon = 1e-06
inverse_root = 0.7071067811865476
density_root = 0.3989422804014327
LANES = 128
GROUP = 256
RIM = 8
f32 = jnp.float32
bf16 = jnp.bfloat16
VMEM_LIMIT = 56 * 1024 * 1024


def whole(shape):
    return pl.BlockSpec(shape, lambda *_: (0,) * len(shape))


SCALAR = pl.BlockSpec(memory_space=pltpu.SMEM)


def params():
    return pltpu.CompilerParams(vmem_limit_bytes=VMEM_LIMIT)


def dot_tn(a, b):
    return lax.dot_general(a, b, (((0,), (0,)), ((), ())), preferred_element_type=f32)


def dot_nt(a, b):
    return lax.dot_general(a, b, (((1,), (1,)), ((), ())), preferred_element_type=f32)


def dot_nn(a, b):
    return jnp.dot(a, b, preferred_element_type=f32)


def lane_head(head_size):
    return lax.broadcasted_iota(jnp.int32, (head_size, LANES), 1) // head_size


def by_head(parts, owner):
    out = parts[0]
    for k in range(1, len(parts)):
        out = jnp.where(owner == k, parts[k], out)
    return out


def pack_diagonal(square, head_size):
    owner = lane_head(head_size)
    return by_head(
        [square[k * head_size : (k + 1) * head_size] for k in range(LANES // head_size)], owner
    )


def sum_in_head(values, owner, packed):
    sums = [jnp.sum(jnp.where(owner == k, values, 0.0), axis=1, keepdims=True) for k in range(packed)]
    return by_head([jnp.broadcast_to(s, values.shape) for s in sums], owner)


def gram_kernel(head_size, col_ref, q_ref, k_ref, mine_ref, other_ref):
    half = pl.program_id(0)
    span = q_ref.shape[1]
    rows = []
    for g in range(span // GROUP):
        at = pl.ds(g * GROUP, GROUP)
        square = dot_tn(q_ref[:, at], k_ref[:, at])
        for p in range(GROUP // LANES):
            cut = slice(p * LANES, (p + 1) * LANES)
            rows.append(pack_diagonal(square[cut, cut], head_size))
    for ref in (q_ref, k_ref):
        for p in range(span // LANES):
            x = ref[:, pl.ds(p * LANES, LANES)].astype(f32)
            rows.append(jnp.sum(x * x, axis=0, keepdims=True))

    def put(ref):
        at = 0
        for row in rows:
            ref[pl.ds(at, row.shape[0]), :] = row
            at += row.shape[0]

    @pl.when(half == col_ref[0])
    def _():
        put(mine_ref)

    @pl.when(half != col_ref[0])
    def _():
        put(other_ref)


def gram_call(col, q, k, head_size):
    tokens, width = q.shape
    span = width // 2
    lines = span // LANES * (head_size + 2)
    out = jax.ShapeDtypeStruct((lines, LANES), f32)
    return pl.pallas_call(
        functools.partial(gram_kernel, head_size),
        grid=(2,),
        in_specs=[
            SCALAR,
            pl.BlockSpec((tokens, span), lambda i: (0, i)),
            pl.BlockSpec((tokens, span), lambda i: (0, i)),
        ],
        out_specs=[whole((lines, LANES))] * 2,
        out_shape=[out, out],
        compiler_params=params(),
        name="gram",
    )(col, q, k)


def gelu_terms(u):
    cumul = 0.5 * (1.0 + lax.erf(u * inverse_root))
    return u * cumul, cumul + u * jnp.exp(-0.5 * u * u) * density_root


def attention_block(head_size, raw, q_line, k_line, sharp):
    packed = LANES // head_size
    owner = lane_head(head_size)
    row = lax.broadcasted_iota(jnp.int32, (head_size, LANES), 0)
    lane = lax.broadcasted_iota(jnp.int32, (head_size, LANES), 1)
    q_energy = by_head(
        [
            jnp.broadcast_to(
                jnp.sum(jnp.where(lane == row + k * head_size, q_line, 0.0), axis=1, keepdims=True),
                raw.shape,
            )
            for k in range(packed)
        ],
        owner,
    )
    q_scale = lax.rsqrt(q_energy + epsilon)
    k_scale = lax.rsqrt(k_line + epsilon)
    gram = q_scale * raw * k_scale
    heat = by_head([jnp.full(raw.shape, s, f32) for s in sharp], owner)
    numer = jnp.exp(heat * gram)
    attention = numer / sum_in_head(numer, owner, packed)
    return attention, gram, q_scale * k_scale


def middle_kernel(
    head_size,
    tile,
    col_ref,
    sharp_ref,
    own_ref,
    far_ref,
    v_ref,
    u_ref,
    side_ref,
    rim_ref,
    proj_ref,
    taps_ref,
    merged_ref,
    attn_ref,
    gram_ref,
    scale_ref,
    block_ref,
    mixed_ref,
    target_ref,
    grad_ref,
    mine_ref,
    other_ref,
    mixed_all,
    field_ref,
    slope_ref,
    projected_ref,
    upside_ref,
    tapsum_ref,
):
    step = pl.program_id(0)
    last = pl.num_programs(0) - 1
    tile_rows, tile_cols = tile
    tokens, width = v_ref.shape
    ring = tile_cols + RIM
    side = tile_rows * RIM
    packed = LANES // head_size
    blocks = width // LANES
    half_blocks = blocks // 2
    is_first = col_ref[0] == 0

    @pl.when(step == 0)
    def _():
        block_ref[...] = jnp.zeros(block_ref.shape, bf16)
        tapsum_ref[...] = jnp.zeros(tapsum_ref.shape, f32)
        owner = lane_head(head_size)
        for p in range(blocks):
            h, inner = divmod(p, half_blocks)

            def take(at, size):
                a = own_ref[pl.ds(at, size), :]
                b = far_ref[pl.ds(at, size), :]
                return jnp.where(is_first, a, b) if h == 0 else jnp.where(is_first, b, a)

            raw = take(inner * head_size, head_size)
            q_line = take(half_blocks * head_size + inner, 1)
            k_line = take(half_blocks * (head_size + 1) + inner, 1)
            attention, gram, scale = attention_block(
                head_size, raw, q_line, k_line, [sharp_ref[p * packed + k] for k in range(packed)]
            )
            at = pl.ds(p * head_size, head_size)
            attn_ref[at, :] = attention
            gram_ref[at, :] = gram
            scale_ref[at, :] = scale
            low = attention.astype(bf16)
            inside = (p * LANES) % GROUP
            for k in range(packed):
                block_ref[pl.ds(p * LANES + k * head_size, head_size), pl.ds(inside, LANES)] = jnp.where(
                    owner == k, low, jnp.zeros_like(low)
                )
        for g in range(width // GROUP):
            at = pl.ds(g * GROUP, GROUP)
            weights = block_ref[at, :]
            centre = dot_nt(v_ref[:, at], weights).astype(bf16)
            mixed_all[pl.ds(0, tokens), at] = centre
            mixed_ref[:, at] = centre
            mixed_all[pl.ds(tokens, side), at] = dot_nt(side_ref[pl.ds(0, side), at], weights).astype(bf16)
            mixed_all[pl.ds(tokens + side, 4 * ring), at] = dot_nt(
                rim_ref[pl.ds(0, 4 * ring), at], weights
            ).astype(bf16)

    chunk = pl.ds(pl.multiple_of(step * GROUP, GROUP), GROUP)
    projected_ref[...] = dot_nn(mixed_all[...], proj_ref[:, chunk])
    upside_ref[pl.ds(0, side), :] = side_ref[pl.ds(side, side), chunk].astype(f32)
    upside_ref[pl.ds(side, 2 * ring), :] = rim_ref[pl.ds(4 * ring, 2 * ring), chunk].astype(f32)

    def lanes_body(part, carry):
        lanes = pl.ds(pl.multiple_of(part * LANES, LANES), LANES)
        glob = pl.ds(pl.multiple_of(step * GROUP + part * LANES, LANES), LANES)
        taps = [taps_ref[pl.ds(t, 1), glob] for t in range(9)]

        def ring_row(r):
            if 0 <= r < tile_rows:
                return jnp.concatenate(
                    [
                        projected_ref[pl.ds(r * tile_cols, tile_cols), lanes],
                        projected_ref[pl.ds(tokens + r * RIM, RIM), lanes],
                    ],
                    axis=0,
                )
            k = r + 2 if r < 0 else r - tile_rows + 2
            return projected_ref[pl.ds(tokens + side + k * ring, ring), lanes]

        def up_row(r):
            if 0 <= r < tile_rows:
                return jnp.concatenate(
                    [
                        u_ref[pl.ds(r * tile_cols, tile_cols), glob].astype(f32),
                        upside_ref[pl.ds(r * RIM, RIM), lanes],
                    ],
                    axis=0,
                )
            k = 0 if r < 0 else 1
            return upside_ref[pl.ds(side + k * ring, ring), lanes]

        for r in range(-2, tile_rows + 2):
            field_ref[r + 2] = ring_row(r).astype(bf16).astype(f32)
        for r in range(-1, tile_rows + 1):
            near = [field_ref[r + 1 + a] for a in range(3)]
            sums = [sum(taps[3 * a + b] * near[a] for a in range(3)) for b in range(3)]
            total = pltpu.roll(sums[0], 1, 0) + sums[1] + pltpu.roll(sums[2], ring - 1, 0)
            active, slope = gelu_terms(total)
            slope_ref[r + 1] = (up_row(r) * slope).astype(bf16).astype(f32)
            if 0 <= r < tile_rows:
                at = pl.ds(r * tile_cols, tile_cols)
                merged_ref[at, glob] = (projected_ref[at, lanes] + active[:tile_cols]).astype(bf16)
        weights = [jnp.zeros((8, LANES), f32) for _ in range(9)]
        blank = jnp.zeros((RIM, LANES), f32)
        for r in range(tile_rows):
            near = [slope_ref[r + 2 - a] for a in range(3)]
            sums = [sum(taps[3 * a + b] * near[a] for a in range(3)) for b in range(3)]
            back = pltpu.roll(sums[0], ring - 1, 0) + sums[1] + pltpu.roll(sums[2], 1, 0)
            at = pl.ds(r * tile_cols, tile_cols)
            target_ref[at, glob] = (u_ref[at, glob].astype(f32) + back[:tile_cols]).astype(bf16)
            centre = jnp.concatenate([near[1][:tile_cols], blank], axis=0)
            shifted = [pltpu.roll(centre, ring - 1, 0), centre, pltpu.roll(centre, 1, 0)]
            for a in range(3):
                line = field_ref[r + 1 + a]
                for b in range(3):
                    product = shifted[b] * line
                    weights[3 * a + b] = weights[3 * a + b] + jnp.sum(
                        product.reshape(ring // 8, 8, LANES), axis=0
                    )
        for t in range(9):
            tapsum_ref[pl.ds(t, 1), glob] = jnp.sum(weights[t], axis=0, keepdims=True)
        return carry

    lax.fori_loop(0, GROUP // LANES, lanes_body, 0)

    @pl.when(step == last)
    def _():
        for g in range(width // GROUP):
            at = pl.ds(g * GROUP, GROUP)
            grad_ref[:, at] = dot_nt(target_ref[...], proj_ref[at, :]).astype(bf16)
        for g in range(width // GROUP):
            at = pl.ds(g * GROUP, GROUP)
            square = dot_tn(grad_ref[:, at], v_ref[:, at])
            for p in range(GROUP // LANES):
                cut = slice(p * LANES, (p + 1) * LANES)
                block = g * (GROUP // LANES) + p
                h, inner = divmod(block, half_blocks)
                packed_rows = pack_diagonal(square[cut, cut], head_size)
                tap_rows = tapsum_ref[:, pl.ds(block * LANES, LANES)]

                def put(ref, inner=inner, packed_rows=packed_rows, tap_rows=tap_rows):
                    ref[pl.ds(inner * head_size, head_size), :] = packed_rows
                    ref[pl.ds(half_blocks * head_size + inner * 16, 16), :] = tap_rows

                @pl.when(col_ref[0] == h)
                def _():
                    put(mine_ref)

                @pl.when(col_ref[0] != h)
                def _():
                    put(other_ref)


def middle_call(col, sharp, own, far, v, u, side, rim, proj, taps, tile, head_size):
    tokens, width = v.shape
    ring = tile[1] + RIM
    blocks = width // LANES
    grams = blocks * head_size
    lines = blocks // 2 * (head_size + 16)
    sds = jax.ShapeDtypeStruct
    outs = [
        sds((tokens, width), bf16),
        sds((grams, LANES), f32),
        sds((grams, LANES), f32),
        sds((grams, LANES), f32),
        sds((width, GROUP), bf16),
        sds((tokens, width), bf16),
        sds((tokens, width), bf16),
        sds((tokens, width), bf16),
        sds((lines, LANES), f32),
        sds((lines, LANES), f32),
    ]
    args = (col, sharp, own, far, v, u, side, rim, proj, taps)
    return pl.pallas_call(
        functools.partial(middle_kernel, head_size, tile),
        grid=(width // GROUP,),
        in_specs=[SCALAR, SCALAR] + [whole(x.shape) for x in args[2:]],
        out_specs=[whole(o.shape) for o in outs],
        out_shape=outs,
        scratch_shapes=[
            pltpu.VMEM((tokens + tile[0] * RIM + 4 * ring, width), bf16),
            pltpu.VMEM((tile[0] + 4, ring, LANES), f32),
            pltpu.VMEM((tile[0] + 2, ring, LANES), f32),
            pltpu.VMEM((tokens + tile[0] * RIM + 4 * ring, GROUP), f32),
            pltpu.VMEM((tile[0] * RIM + 2 * ring, GROUP), f32),
            pltpu.VMEM((16, width), f32),
        ],
        compiler_params=params(),
        name="middle",
    )(*args)


def projector_kernel(chunk, slots_ref, mixed_ref, target_ref, mine_ref, other_ref):
    step = pl.program_id(0)
    product = dot_tn(mixed_ref[...], target_ref[...])
    per = GROUP // chunk
    for k in range(per):
        piece = product[k * chunk : (k + 1) * chunk]
        far = slots_ref[0, step * per + k]
        at = pl.ds(pl.multiple_of(slots_ref[1, step * per + k] * chunk, chunk), chunk)

        @pl.when(far == 0)
        def _():
            mine_ref[at, :] = piece

        @pl.when(far != 0)
        def _():
            other_ref[at, :] = piece.astype(bf16)


def projector_call(slots, mixed, target, chunk):
    tokens, width = mixed.shape
    sds = jax.ShapeDtypeStruct
    outs = [sds((width // 2, width), f32), sds((width // 2, width), bf16)]
    return pl.pallas_call(
        functools.partial(projector_kernel, chunk),
        grid=(width // GROUP,),
        in_specs=[SCALAR, pl.BlockSpec((tokens, GROUP), lambda i: (0, i)), whole(target.shape)],
        out_specs=[whole(o.shape) for o in outs],
        out_shape=outs,
        compiler_params=params(),
        name="projector",
    )(slots, mixed, target)


def content_kernel(grad_ref, block_ref, out_ref):
    out_ref[...] = dot_nn(grad_ref[...], block_ref[...]).astype(bf16)


def content_call(grad, block):
    tokens, width = grad.shape
    return pl.pallas_call(
        content_kernel,
        grid=(width // GROUP,),
        in_specs=[
            pl.BlockSpec((tokens, GROUP), lambda i: (0, i)),
            pl.BlockSpec((GROUP, GROUP), lambda i: (i, 0)),
        ],
        out_specs=pl.BlockSpec((tokens, GROUP), lambda i: (0, i)),
        out_shape=jax.ShapeDtypeStruct((tokens, width), bf16),
        compiler_params=params(),
        name="content",
    )(grad, block)


def final_kernel(
    head_size,
    col_ref,
    sharp_ref,
    own_ref,
    far_ref,
    energy_own_ref,
    energy_far_ref,
    attn_ref,
    gram_ref,
    scale_ref,
    q_ref,
    k_ref,
    dq_ref,
    dk_ref,
    heat_ref,
    taps_ref,
    mixer_ref,
):
    step = pl.program_id(0)
    steps = pl.num_programs(0)
    packed = LANES // head_size
    per = GROUP // LANES
    half_blocks = steps * per // 2
    mine = (step // (steps // 2)) == col_ref[0]
    owner = lane_head(head_size)
    row = lax.broadcasted_iota(jnp.int32, (head_size, LANES), 0)
    lane = lax.broadcasted_iota(jnp.int32, (head_size, LANES), 1)
    mixer_ref[...] = jnp.zeros(mixer_ref.shape, bf16)
    q_terms, k_terms = [], []
    for p in range(per):
        block = step * per + p
        inner = lax.rem(block, half_blocks)

        def take(own, far, at, size):
            return jnp.where(mine, own[pl.ds(at, size), :], far[pl.ds(at, size), :])

        grad = take(own_ref, far_ref, pl.multiple_of(inner * head_size, head_size), head_size)
        taps_ref[:, pl.ds(p * LANES, LANES)] = take(
            own_ref, far_ref, pl.multiple_of(half_blocks * head_size + inner * 16, 16), 16
        )[:9]
        q_line = take(energy_own_ref, energy_far_ref, half_blocks * head_size + inner, 1)
        k_line = take(energy_own_ref, energy_far_ref, half_blocks * (head_size + 1) + inner, 1)
        at = pl.ds(pl.multiple_of(block * head_size, head_size), head_size)
        attention, gram, scale = attn_ref[at, :], gram_ref[at, :], scale_ref[at, :]
        scores = attention * (grad - sum_in_head(attention * grad, owner, packed))
        heated = scores * gram
        heat = by_head(
            [jnp.full(scores.shape, sharp_ref[block * packed + k], f32) for k in range(packed)], owner
        )
        for k in range(packed):
            heat_ref[block * packed + k] = jnp.sum(jnp.where(owner == k, heated, 0.0))
        gram_grad = heat * scores
        corr = gram_grad * gram
        k_corr = jnp.sum(corr, axis=0, keepdims=True)
        columns = sum_in_head(corr, owner, packed)
        q_corr = jnp.sum(jnp.where(lane == row + owner * head_size, columns, 0.0), axis=0, keepdims=True)
        q_scale = lax.rsqrt(q_line + epsilon)
        k_scale = lax.rsqrt(k_line + epsilon)
        q_terms.append(q_scale * q_scale * q_corr)
        k_terms.append(k_scale * k_scale * k_corr)
        low = (scale * gram_grad).astype(bf16)
        for k in range(packed):
            mixer_ref[pl.ds(p * LANES + k * head_size, head_size), pl.ds(p * LANES, LANES)] = jnp.where(
                owner == k, low, jnp.zeros_like(low)
            )
    q, k = q_ref[...], k_ref[...]
    mixer = mixer_ref[...]
    dq_ref[...] = (dot_nt(k, mixer) - q.astype(f32) * jnp.concatenate(q_terms, axis=1)).astype(bf16)
    dk_ref[...] = (dot_nn(q, mixer) - k.astype(f32) * jnp.concatenate(k_terms, axis=1)).astype(bf16)


def final_call(col, sharp, own, far, energy_own, energy_far, attn, gram, scale, q, k, head_size):
    tokens, width = q.shape
    sds = jax.ShapeDtypeStruct
    token_block = pl.BlockSpec((tokens, GROUP), lambda i: (0, i))
    args = (col, sharp, own, far, energy_own, energy_far, attn, gram, scale, q, k)
    return pl.pallas_call(
        functools.partial(final_kernel, head_size),
        grid=(width // GROUP,),
        in_specs=[SCALAR, SCALAR] + [whole(x.shape) for x in args[2:9]] + [token_block] * 2,
        out_specs=[
            token_block,
            token_block,
            SCALAR,
            pl.BlockSpec((9, GROUP), lambda i: (0, i)),
        ],
        out_shape=[
            sds((tokens, width), bf16),
            sds((tokens, width), bf16),
            sds(sharp.shape, f32),
            sds((9, width), f32),
        ],
        scratch_shapes=[pltpu.VMEM((GROUP, GROUP), bf16)],
        compiler_params=params(),
        name="final",
    )(*args)


def swap(x, axis, bit):
    return lax.ppermute(x, axis, [(i, i ^ bit) for i in range(lax.axis_size(axis))])


def row_bits():
    bits, bit = [], 1
    while bit < lax.axis_size("row"):
        bits.append(bit)
        bit *= 2
    return bits


def sum_halves(mine, other):
    total = mine + swap(other, "col", 1)
    for bit in row_bits():
        total = total + swap(total, "row", bit)
    return total, swap(total, "col", 1)


def halo(v, u):
    tile_rows, tile_cols, width = v.shape
    rows, cols = lax.axis_size("row"), lax.axis_size("col")
    down = [(i, i + 1) for i in range(rows - 1)]
    up = [(i + 1, i) for i in range(rows - 1)]
    above = lax.ppermute(jnp.concatenate([v[-2:], u[-1:]]), "row", down)
    below = lax.ppermute(jnp.concatenate([v[:2], u[:1]]), "row", up)
    rim = jnp.concatenate([above[:2], below[:2], above[2:], below[2:]])
    first = lax.axis_index("col") == 0
    edge = jnp.concatenate(
        [jnp.where(first, x[:, -2:], x[:, :2]) for x in (v, u, rim)]
    )
    got = swap(edge, "col", 1)
    none = jnp.zeros((got.shape[0], RIM - 2, width), got.dtype)
    side = jnp.where(
        first,
        jnp.concatenate([got, none], axis=1),
        jnp.concatenate([none, got], axis=1),
    )
    rim = jnp.concatenate([rim, side[2 * tile_rows :]], axis=1)
    return (
        side[: 2 * tile_rows].reshape(2 * tile_rows * RIM, width),
        rim.reshape(6 * (tile_cols + RIM), width),
    )


def projector_sum(mine, other):
    total = mine + swap(other, "col", 1).astype(f32)
    for bit in row_bits():
        half = total.shape[0] // 2
        total = total[:half] + swap(total[half:].astype(bf16), "row", bit).astype(f32)
    return total


def projector_slots():
    rows, cols = lax.axis_size("row"), lax.axis_size("col")
    piece = jnp.arange(rows * cols, dtype=jnp.int32)
    away = (piece // cols) ^ lax.axis_index("row")
    place = jnp.zeros_like(piece)
    for bit in row_bits():
        place = 2 * place + (away // bit) % 2
    return jnp.stack([(piece % cols) ^ lax.axis_index("col"), place])


def shards(q, k, v, u, sharp, proj, taps):
    tile = v.shape[:2]
    width = v.shape[2]
    tokens = tile[0] * tile[1]
    head_size = width // sharp.shape[0]
    flat = lambda x: x.reshape(tokens, width)
    col = lax.axis_index("col").astype(jnp.int32).reshape(1)
    q2, k2, v2, u2 = flat(q), flat(k), flat(v), flat(u)
    energy_own, energy_far = sum_halves(*gram_call(col, q2, k2, head_size))
    side, rim = halo(v, u)
    (merged, attn, gram, scale, block, mixed, target, grad, mine, other) = middle_call(
        col, sharp, energy_own, energy_far, v2, u2, side, rim, proj, taps, tile, head_size
    )
    own, far = sum_halves(mine, other)
    chunk = width // (lax.axis_size("row") * lax.axis_size("col"))
    projector = projector_sum(*projector_call(projector_slots(), mixed, target, chunk))
    content = content_call(grad, block)
    dq, dk, heat, tap_sums = final_call(
        col, sharp, own, far, energy_own, energy_far, attn, gram, scale, q2, k2, head_size
    )
    full = lambda x: x.reshape(tile + (width,))
    return full(merged), full(dq), full(dk), full(content), heat, tap_sums, projector


def solution(mesh):
    field = P(("scene", "row"), "col", None)
    return jax.shard_map(
        shards,
        mesh=mesh,
        in_specs=(field, field, field, field, P(), P(), P()),
        out_specs=(
            field,
            field,
            field,
            field,
            P("scene"),
            P("scene", None),
            P(("scene", "row", "col"), None),
        ),
        check_vma=False,
    )
```

time: 354 us -> 117 us (0.33)
  blocking collectives: 120 us -> 0 us
  local copies, waits for them, and re-layouts: 58.3 us -> 6.83 us
  matrix products: 42.2 us -> 0 us
  Pallas kernels: 0 us -> 36 us
  other arithmetic: 34.5 us -> 4.71 us
  waiting for transfers between devices: 65.3 us -> 45.2 us
  between operations: 14.2 us -> 0.96 us
  starting transfers between devices: 17.8 us -> 22.4 us
    psum x2 -> x0, blocking collectives: 120 us -> none  [the longest x1 60.6 us: shards(): lax.psum((attention_local, stencil_local), ('row', 'col'))]
    dot_general x9 -> x0, matrix products: 42.2 us -> none  [the longest x1 9.95 us: shards(): jnp.einsum('nhi,hij->nhj', query_heads, mixer_low, preferred_element_type...]
    ppermute x8 -> x17, waiting for transfers between devices: 7.2 us -> 45.2 us  [the longest x15 42 us: swap(): lax.ppermute(x, axis, [(i, i ^ bit) for i in range(lax.axis_size(axis))])]
    pallas_call x0 -> x5, Pallas kernels: none -> 36 us  [the longest x1 18.9 us: middle_call(): pl.pallas_call(functools.partial(middle_kernel, head_size, tile), grid=(w...]
    reduce_scatter x1 -> x0, waiting for transfers between devices: 32.7 us -> none  [shards(): lax.psum_scatter(lax.dot_general(mixed_low, target_flat, (((0,), (0,)), (...]
    reshape x9 -> x0, local copies, waits for them, and re-layouts: 32 us -> none  [the longest x2 7.45 us: shards(): camera_probe_field.reshape(token_count, per_group_layout, head_size)]
    psum x2 -> x0, waiting for transfers between devices: 25.4 us -> none  [the longest x1 22.4 us: shards(): lax.psum((query_local, key_local, gram_local), ('row', 'col'))]
    convert_element_type x5 -> x0, local copies, waits for them, and re-layouts: 17.6 us -> none  [the longest x1 3.87 us: shards(): probe_sensitivity.astype(jnp.bfloat16).reshape(shape_tile)]
  transfers between devices with their start and end apart: 11 -> 17, of which waited for: 5 -> 9; matrix products, arithmetic and copies ran while one was open for 33% -> 6% of each run, Pallas kernels for 0% -> 8%
where the time goes in v1:
time: 117 us; the launch traced here: 116 us
  waiting for transfers between devices  45.2 us (39%)
  Pallas kernels  36 us (31%)
  starting transfers between devices  22.4 us (19%)
  local copies, waits for them, and re-layouts  6.83 us (6%)
  other arithmetic  4.71 us (4%)
    ppermute x15, waiting for transfers between devices, swap(): lax.ppermute(x, axis, [(i, i ^ bit) for i in range(lax.axis_size(axis))])  42 us
    pallas_call x1, Pallas kernels, middle_call(): pl.pallas_call(functools.partial(middle_kernel, head_size, tile), grid=(w...  18.9 us
    ppermute x15, starting transfers between devices, swap(): lax.ppermute(x, axis, [(i, i ^ bit) for i in range(lax.axis_size(axis))])  16.6 us
    pallas_call x1, Pallas kernels, projector_call(): pl.pallas_call(functools.partial(projector_kernel, chunk), grid=(width //...  5.61 us
    pallas_call x1, Pallas kernels, final_call(): pl.pallas_call(functools.partial(final_kernel, head_size), grid=(width //...  4.99 us
    ppermute x1, starting transfers between devices, halo(): above = lax.ppermute(jnp.concatenate([v[-2:], u[-1:]]), 'row', down)  4.47 us
    pallas_call x1, Pallas kernels, content_call(): pl.pallas_call(content_kernel, grid=(width // GROUP,), in_specs=[pl.Block...  3.88 us
    ppermute x1, waiting for transfers between devices, halo(): below = lax.ppermute(jnp.concatenate([v[:2], u[:1]]), 'row', up)  3.19 us
  transfers between devices with their start and end apart: 17, of which 9 were waited for; matrix products, arithmetic and copies ran while one was open for 6% of the time, Pallas kernels for 8%

profile of v1, /device:TPU:0, one launch (start us, length us, event | category | flops | bytes accessed | tf_op | source)
XLA Modules:
  0.0 116.0 jit_solution(12461808978904062376)
XLA Ops:
  0.6 2.7 %gram.1 = (f32[264,128]{1,0:T(8,128)}, f32[264,128]{1,0:T(8,128)}) custom-call(s32[1]{0:T(128)} %bitcast.col_ref, bf16[512,1024]{1,0:T(8,128)(2,1)} %bitcast.13, bf16[512,1024]{1,0:T(8,128)(2,1)} %bitcast.15), custom_call_target="tpu_custom_call" | custom-call | tf_op jit(solution)/shard_map/gram/pallas_call | solution.py:102
  3.7 1.0 fusion.9
  4.7 0.9 fusion.10
  5.7 4.5 %collective-permute-start.5 = (bf16[3,32,1024]{2,1,0:T(8,128)(2,1)S(1)}, bf16[3,32,1024]{2,1,0:T(8,128)(2,1)S(1)}, u32[]{:S(2)}, u32[]{:S(2)}) collective-permute-start(bf16[3,32,1024]{2,1,0:T(8,128)(2,1)S(1)} %pad_maximum_fusion.1), channel_id=1, source_target_pairs={{0,2},{2,4},{4,6},{6,8},{8,10},{10,12},{12,14},{1,3},{3,5},{5,7},{... | collective-permute-start | bytes 589832 | tf_op jit(solution)/shard_map/ppermute | solution.py:538
  10.2 1.3 %collective-permute-start.6 = (bf16[3,32,1024]{2,1,0:T(8,128)(2,1)S(1)}, bf16[3,32,1024]{2,1,0:T(8,128)(2,1)S(1)}, u32[]{:S(2)}, u32[]{:S(2)}) collective-permute-start(bf16[3,32,1024]{2,1,0:T(8,128)(2,1)S(1)} %pad_maximum_fusion.2), channel_id=1, source_target_pairs={{2,0},{4,2},{6,4},{8,6},{10,8},{12,10},{14,12},{3,1},{5,3},{7,5},{... | collective-permute-start | bytes 589832 | tf_op jit(solution)/shard_map/ppermute | solution.py:539
  11.5 1.1 fusion.7
  12.6 1.1 fusion.8
  13.8 2.7 %collective-permute-start.1 = (f32[264,128]{1,0:T(8,128)S(1)}, f32[264,128]{1,0:T(8,128)S(1)}, u32[]{:S(2)}, u32[]{:S(2)}) collective-permute-start(f32[264,128]{1,0:T(8,128)S(1)} %add.132), channel_id=1, source_target_pairs={{0,2},{2,0},{4,6},{6,4},{8,10},{10,8},{12,14},{14,12},{1,3},{3,1},... | collective-permute-start | bytes 405512 | tf_op jit(solution)/shard_map/ppermute | solution.py:515
  16.6 3.2 %collective-permute-done.6 = bf16[3,32,1024]{2,1,0:T(8,128)(2,1)S(1)} collective-permute-done((bf16[3,32,1024]{2,1,0:T(8,128)(2,1)S(1)}, bf16[3,32,1024]{2,1,0:T(8,128)(2,1)S(1)}, u32[]{:S(2)}, u32[]{:S(2)}) %collective-permute-start.6) | collective-permute-done | bytes 196640 | tf_op jit(solution)/shard_map/ppermute | solution.py:539
  19.8 2.1 %collective-permute-done.1 = f32[264,128]{1,0:T(8,128)S(1)} collective-permute-done((f32[264,128]{1,0:T(8,128)S(1)}, f32[264,128]{1,0:T(8,128)S(1)}, u32[]{:S(2)}, u32[]{:S(2)}) %collective-permute-start.1) | collective-permute-done | bytes 135200 | tf_op jit(solution)/shard_map/ppermute | solution.py:515
  22.0 3.5 %collective-permute-start.2 = (f32[264,128]{1,0:T(8,128)S(1)}, f32[264,128]{1,0:T(8,128)S(1)}, u32[]{:S(2)}, u32[]{:S(2)}) collective-permute-start(f32[264,128]{1,0:T(8,128)S(1)} %add.133), channel_id=1, source_target_pairs={{0,4},{2,6},{4,0},{6,2},{8,12},{10,14},{12,8},{14,10},{1,5},{3,7},... | collective-permute-start | bytes 405512 | tf_op jit(solution)/shard_map/ppermute | solution.py:515
  25.7 3.6 %collective-permute-done.2 = f32[264,128]{1,0:T(8,128)S(1)} collective-permute-done((f32[264,128]{1,0:T(8,128)S(1)}, f32[264,128]{1,0:T(8,128)S(1)}, u32[]{:S(2)}, u32[]{:S(2)}) %collective-permute-start.2) | collective-permute-done | bytes 135200 | tf_op jit(solution)/shard_map/ppermute | solution.py:515
  29.3 2.8 %collective-permute-start.3 = (f32[264,128]{1,0:T(8,128)S(1)}, f32[264,128]{1,0:T(8,128)S(1)}, u32[]{:S(2)}, u32[]{:S(2)}) collective-permute-start(f32[264,128]{1,0:T(8,128)S(1)} %add.134), channel_id=1, source_target_pairs={{0,8},{2,10},{4,12},{6,14},{8,0},{10,2},{12,4},{14,6},{1,9},{3,11}... | collective-permute-start | bytes 405512 | tf_op jit(solution)/shard_map/ppermute | solution.py:515
  32.8 5.4 %collective-permute-done.3 = f32[264,128]{1,0:T(8,128)S(1)} collective-permute-done((f32[264,128]{1,0:T(8,128)S(1)}, f32[264,128]{1,0:T(8,128)S(1)}, u32[]{:S(2)}, u32[]{:S(2)}) %collective-permute-start.3) | collective-permute-done | bytes 135200 | tf_op jit(solution)/shard_map/ppermute | solution.py:515
  38.5 1.1 copy.40
  39.6 0.8 pad_maximum_fusion
  40.4 0.7 copy-done.2
  41.1 18.9 %middle.1 = (bf16[512,1024]{1,0:T(8,128)(2,1)}, f32[512,128]{1,0:T(8,128)}, f32[512,128]{1,0:T(8,128)}, f32[512,128]{1,0:T(8,128)}, bf16[1024,256]{1,0:T(8,128)(...) custom-call(s32[1]{0:T(128)} %bitcast.col_ref, ...), custom_call_target="tpu_custom_call" | custom-call | tf_op jit(solution)/shard_map/middle/pallas_call | solution.py:343
  60.0 5.6 %projector.1 = (f32[512,1024]{1,0:T(8,128)}, bf16[512,1024]{1,0:T(8,128)(2,1)}) custom-call(s32[2,16]{1,0:T(2,128)} %pad_add_fusion.slots_ref, bf16[512,1024]{1,0:T(8,128)(2,1)} %get-tuple-element.39.mixed_ref, bf16[512,1024]{1,0:T(8,128)(2,1)} %get-tuple-element.40.target_ref), custom_call_target="tpu_custom_call" | custom-call | tf_op jit(solution)/shard_map/projector/pallas_call | solution.py:384
  66.1 2.5 %collective-permute-done.13 = bf16[512,1024]{1,0:T(8,128)(2,1)S(1)} collective-permute-done((bf16[512,1024]{1,0:T(8,128)(2,1)}, bf16[512,1024]{1,0:T(8,128)(2,1)S(1)}, u32[]{:S(2)}, u32[]{:S(2)}) %collective-permute-start.13) | collective-permute-done | bytes 1048608 | tf_op jit(solution)/shard_map/ppermute | solution.py:515
  68.6 2.0 %convert_add_fusion = f32[512,1024]{1,0:T(8,128)S(1)} fusion(f32[512,1024]{1,0:T(8,128)} %get-tuple-element.41, bf16[512,1024]{1,0:T(8,128)(2,1)S(1)} %collective-permute-done.13), kind=kLoop, calls=%fused_computation | loop fusion | flops 1048576 | bytes 5242880 | tf_op jit(solution)/shard_map/add | solution.py:560
  70.6 0.7 collective-permute-start.14
  71.4 1.3 %collective-permute-done.8 = f32[320,128]{1,0:T(8,128)S(1)} collective-permute-done((f32[320,128]{1,0:T(8,128)S(1)}, f32[320,128]{1,0:T(8,128)S(1)}, u32[]{:S(2)}, u32[]{:S(2)}) %collective-permute-start.8) | collective-permute-done | bytes 163872 | tf_op jit(solution)/shard_map/ppermute | solution.py:515
  72.7 1.5 %collective-permute-start.9 = (f32[320,128]{1,0:T(8,128)S(1)}, f32[320,128]{1,0:T(8,128)S(1)}, u32[]{:S(2)}, u32[]{:S(2)}) collective-permute-start(f32[320,128]{1,0:T(8,128)S(1)} %add.136), channel_id=1, source_target_pairs={{0,2},{2,0},{4,6},{6,4},{8,10},{10,8},{12,14},{14,12},{1,3},{3,1},... | collective-permute-start | bytes 491528 | tf_op jit(solution)/shard_map/ppermute | solution.py:515
  74.2 14.2 %collective-permute-done.9 = f32[320,128]{1,0:T(8,128)S(1)} collective-permute-done((f32[320,128]{1,0:T(8,128)S(1)}, f32[320,128]{1,0:T(8,128)S(1)}, u32[]{:S(2)}, u32[]{:S(2)}) %collective-permute-start.9) | collective-permute-done | bytes 163872 | tf_op jit(solution)/shard_map/ppermute | solution.py:515
  89.2 1.6 %collective-permute-start.15 = (bf16[128,1024]{1,0:T(8,128)(2,1)S(1)}, bf16[128,1024]{1,0:T(8,128)(2,1)S(1)}, u32[]{:S(2)}, u32[]{:S(2)}) collective-permute-start(bf16[128,1024]{1,0:T(8,128)(2,1)S(1)} %slice.110), channel_id=1, source_target_pairs={{0,4},{2,6},{4,0},{6,2},{8,12},{10,14},{12,8},{14,10},{1,5},{3,7},... | collective-permute-start | bytes 786440 | tf_op jit(solution)/shard_map/ppermute | solution.py:515
  90.8 4.8 %collective-permute-done.10 = f32[320,128]{1,0:T(8,128)S(1)} collective-permute-done((f32[320,128]{1,0:T(8,128)S(1)}, f32[320,128]{1,0:T(8,128)S(1)}, u32[]{:S(2)}, u32[]{:S(2)}) %collective-permute-start.10) | collective-permute-done | bytes 163872 | tf_op jit(solution)/shard_map/ppermute | solution.py:515
  95.7 1.9 %collective-permute-start.11 = (f32[320,128]{1,0:T(8,128)S(1)}, f32[320,128]{1,0:T(8,128)S(1)}, u32[]{:S(2)}, u32[]{:S(2)}) collective-permute-start(f32[320,128]{1,0:T(8,128)S(1)} %add.138), channel_id=1, source_target_pairs={{0,8},{2,10},{4,12},{6,14},{8,0},{10,2},{12,4},{14,6},{1,9},{3,11}... | collective-permute-start | bytes 491528 | tf_op jit(solution)/shard_map/ppermute | solution.py:515
  97.6 7.9 %collective-permute-done.11 = f32[320,128]{1,0:T(8,128)S(1)} collective-permute-done((f32[320,128]{1,0:T(8,128)S(1)}, f32[320,128]{1,0:T(8,128)S(1)}, u32[]{:S(2)}, u32[]{:S(2)}) %collective-permute-start.11) | collective-permute-done | bytes 163872 | tf_op jit(solution)/shard_map/ppermute | solution.py:515
  105.8 3.9 %content.1 = bf16[512,1024]{1,0:T(8,128)(2,1)} custom-call(bf16[512,1024]{1,0:T(8,128)(2,1)} %get-tuple-element.35.grad_ref, bf16[1024,256]{1,0:T(8,128)(2,1)} %get-tuple-element.36.block_ref), custom_call_target="tpu_custom_call" | custom-call | tf_op jit(solution)/shard_map/content/pallas_call | solution.py:401
  110.3 5.0 %final.1 = (bf16[512,1024]{1,0:T(8,128)(2,1)}, bf16[512,1024]{1,0:T(8,128)(2,1)}, f32[16]{0:T(128)}, f32[9,1024]{1,0:T(8,128)}) custom-call(s32[1]{0:T(128)} %bitcast.col_ref, f32[16]{0:T(128)} %sharp_ref.3, f32[320,128]{1,0:T(8,128)} %copy-done.1, f32[320,128]{1,0:T(8,128)} %copy-done.3, f32[264,128]{1,0:T(8,128)} %copy-done, f32[264,128]{1,0:T(8,128)} %copy-done.2, ...), custom_call_target="tpu_custom_call" | custom-call | tf_op jit(solution)/shard_map/final/pallas_call | solution.py:492
  115.3 0.7 slice_add_fusion.2
  (58 shorter events, 4.0 us)
Async XLA Ops:
  3.3 10.5 %copy-start.5 = (f32[264,128]{1,0:T(8,128)S(1)}, f32[264,128]{1,0:T(8,128)}, u32[]{:S(2)}) copy-start(f32[264,128]{1,0:T(8,128)} %get-tuple-element.25) | copy-start | bytes 405508
  3.3 10.5 %collective-permute-start = (f32[264,128]{1,0:T(8,128)}, f32[264,128]{1,0:T(8,128)S(1)}, u32[]{:S(2)}, u32[]{:S(2)}) collective-permute-start(f32[264,128]{1,0:T(8,128)} %get-tuple-element.26), channel_id=1, source_target_pairs={{0,1},{1,0},{2,3},{3,2},{4,5},{5,4},{6,7},{7,6},{8,9},{9,8},{10,11... | collective-permute-start | bytes 405512 | tf_op jit(solution)/shard_map/ppermute | solution.py:515
  5.7 10.9 %collective-permute-start.5 = (bf16[3,32,1024]{2,1,0:T(8,128)(2,1)S(1)}, bf16[3,32,1024]{2,1,0:T(8,128)(2,1)S(1)}, u32[]{:S(2)}, u32[]{:S(2)}) collective-permute-start(bf16[3,32,1024]{2,1,0:T(8,128)(2,1)S(1)} %pad_maximum_fusion.1), channel_id=1, source_target_pairs={{0,2},{2,4},{4,6},{6,8},{8,10},{10,12},{12,14},{1,3},{3,5},{5,7},{... | collective-permute-start | bytes 589832 | tf_op jit(solution)/shard_map/ppermute | solution.py:538
  10.2 9.6 %collective-permute-start.6 = (bf16[3,32,1024]{2,1,0:T(8,128)(2,1)S(1)}, bf16[3,32,1024]{2,1,0:T(8,128)(2,1)S(1)}, u32[]{:S(2)}, u32[]{:S(2)}) collective-permute-start(bf16[3,32,1024]{2,1,0:T(8,128)(2,1)S(1)} %pad_maximum_fusion.2), channel_id=1, source_target_pairs={{2,0},{4,2},{6,4},{8,6},{10,8},{12,10},{14,12},{3,1},{5,3},{7,5},{... | collective-permute-start | bytes 589832 | tf_op jit(solution)/shard_map/ppermute | solution.py:539
  13.8 8.2 %collective-permute-start.1 = (f32[264,128]{1,0:T(8,128)S(1)}, f32[264,128]{1,0:T(8,128)S(1)}, u32[]{:S(2)}, u32[]{:S(2)}) collective-permute-start(f32[264,128]{1,0:T(8,128)S(1)} %add.132), channel_id=1, source_target_pairs={{0,2},{2,0},{4,6},{6,4},{8,10},{10,8},{12,14},{14,12},{1,3},{3,1},... | collective-permute-start | bytes 405512 | tf_op jit(solution)/shard_map/ppermute | solution.py:515
  22.0 7.3 %collective-permute-start.2 = (f32[264,128]{1,0:T(8,128)S(1)}, f32[264,128]{1,0:T(8,128)S(1)}, u32[]{:S(2)}, u32[]{:S(2)}) collective-permute-start(f32[264,128]{1,0:T(8,128)S(1)} %add.133), channel_id=1, source_target_pairs={{0,4},{2,6},{4,0},{6,2},{8,12},{10,14},{12,8},{14,10},{1,5},{3,7},... | collective-permute-start | bytes 405512 | tf_op jit(solution)/shard_map/ppermute | solution.py:515
  25.6 12.7 %collective-permute-start.7 = (bf16[38,2,1024]{2,0,1:T(8,128)(2,1)S(1)}, bf16[38,2,1024]{2,0,1:T(8,128)(2,1)S(1)}, u32[]{:S(2)}, u32[]{:S(2)}) collective-permute-start(bf16[38,2,1024]{2,0,1:T(8,128)(2,1)S(1)} %pad_maximum_fusion.3), channel_id=1, source_target_pairs={{0,1},{1,0},{2,3},{3,2},{4,5},{5,4},{6,7},{7,6},{8,9},{9,8},{10,11... | collective-permute-start | bytes 466952 | tf_op jit(solution)/shard_map/ppermute | solution.py:515
  29.3 8.9 %collective-permute-start.3 = (f32[264,128]{1,0:T(8,128)S(1)}, f32[264,128]{1,0:T(8,128)S(1)}, u32[]{:S(2)}, u32[]{:S(2)}) collective-permute-start(f32[264,128]{1,0:T(8,128)S(1)} %add.134), channel_id=1, source_target_pairs={{0,8},{2,10},{4,12},{6,14},{8,0},{10,2},{12,4},{14,6},{1,9},{3,11}... | collective-permute-start | bytes 405512 | tf_op jit(solution)/shard_map/ppermute | solution.py:515
  38.2 2.2 %copy-start = (f32[264,128]{1,0:T(8,128)}, f32[264,128]{1,0:T(8,128)S(1)}, u32[]{:S(2)}) copy-start(f32[264,128]{1,0:T(8,128)S(1)} %add.135.own_ref.energy_own_ref) | copy-start | bytes 405508
  38.2 2.2 %collective-permute-start.4 = (f32[264,128]{1,0:T(8,128)S(1)}, f32[264,128]{1,0:T(8,128)S(1)}, u32[]{:S(2)}, u32[]{:S(2)}) collective-permute-start(f32[264,128]{1,0:T(8,128)S(1)} %add.135.own_ref.energy_own_ref), channel_id=1, source_target_pairs={{0,1},{1,0},{2,3},{3,2},{4,5},{5,4},{6,7},{7,6},{8,9},{9,8},{10,11... | collective-permute-start | bytes 405512 | tf_op jit(solution)/shard_map/ppermute | solution.py:515
  40.4 0.7 copy-start.2
  65.6 3.0 %collective-permute-start.13 = (bf16[512,1024]{1,0:T(8,128)(2,1)}, bf16[512,1024]{1,0:T(8,128)(2,1)S(1)}, u32[]{:S(2)}, u32[]{:S(2)}) collective-permute-start(bf16[512,1024]{1,0:T(8,128)(2,1)} %get-tuple-element.42), channel_id=1, source_target_pairs={{0,1},{1,0},{2,3},{3,2},{4,5},{5,4},{6,7},{7,6},{8,9},{9,8},{10,11... | collective-permute-start | bytes 3145736 | tf_op jit(solution)/shard_map/ppermute | solution.py:515
  68.6 2.7 %copy-start.6 = (f32[320,128]{1,0:T(8,128)S(1)}, f32[320,128]{1,0:T(8,128)}, u32[]{:S(2)}) copy-start(f32[320,128]{1,0:T(8,128)} %get-tuple-element.29) | copy-start | bytes 491524
  68.6 4.1 %copy-start.4 = (f32[320,128]{1,0:T(8,128)S(1)}, f32[320,128]{1,0:T(8,128)}, u32[]{:S(2)}) copy-start(f32[320,128]{1,0:T(8,128)} %get-tuple-element.28) | copy-start | bytes 491524
  70.6 18.4 %collective-permute-start.14 = (bf16[256,1024]{1,0:T(8,128)(2,1)S(1)}, bf16[256,1024]{1,0:T(8,128)(2,1)S(1)}, u32[]{:S(2)}, u32[]{:S(2)}) collective-permute-start(bf16[256,1024]{1,0:T(8,128)(2,1)S(1)} %slice.109), channel_id=1, source_target_pairs={{0,2},{2,0},{4,6},{6,4},{8,10},{10,8},{12,14},{14,12},{1,3},{3,1},... | collective-permute-start | bytes 1572872 | tf_op jit(solution)/shard_map/ppermute | solution.py:515
  71.3 1.4 %collective-permute-start.8 = (f32[320,128]{1,0:T(8,128)S(1)}, f32[320,128]{1,0:T(8,128)S(1)}, u32[]{:S(2)}, u32[]{:S(2)}) collective-permute-start(f32[320,128]{1,0:T(8,128)S(1)} %copy-done.6), channel_id=1, source_target_pairs={{0,1},{1,0},{2,3},{3,2},{4,5},{5,4},{6,7},{7,6},{8,9},{9,8},{10,11... | collective-permute-start | bytes 491528 | tf_op jit(solution)/shard_map/ppermute | solution.py:515
  72.7 15.7 %collective-permute-start.9 = (f32[320,128]{1,0:T(8,128)S(1)}, f32[320,128]{1,0:T(8,128)S(1)}, u32[]{:S(2)}, u32[]{:S(2)}) collective-permute-start(f32[320,128]{1,0:T(8,128)S(1)} %add.136), channel_id=1, source_target_pairs={{0,2},{2,0},{4,6},{6,4},{8,10},{10,8},{12,14},{14,12},{1,3},{3,1},... | collective-permute-start | bytes 491528 | tf_op jit(solution)/shard_map/ppermute | solution.py:515
  88.5 7.2 %collective-permute-start.10 = (f32[320,128]{1,0:T(8,128)S(1)}, f32[320,128]{1,0:T(8,128)S(1)}, u32[]{:S(2)}, u32[]{:S(2)}) collective-permute-start(f32[320,128]{1,0:T(8,128)S(1)} %add.137), channel_id=1, source_target_pairs={{0,4},{2,6},{4,0},{6,2},{8,12},{10,14},{12,8},{14,10},{1,5},{3,7},... | collective-permute-start | bytes 491528 | tf_op jit(solution)/shard_map/ppermute | solution.py:515
  89.2 16.4 %collective-permute-start.15 = (bf16[128,1024]{1,0:T(8,128)(2,1)S(1)}, bf16[128,1024]{1,0:T(8,128)(2,1)S(1)}, u32[]{:S(2)}, u32[]{:S(2)}) collective-permute-start(bf16[128,1024]{1,0:T(8,128)(2,1)S(1)} %slice.110), channel_id=1, source_target_pairs={{0,4},{2,6},{4,0},{6,2},{8,12},{10,14},{12,8},{14,10},{1,5},{3,7},... | collective-permute-start | bytes 786440 | tf_op jit(solution)/shard_map/ppermute | solution.py:515
  95.7 9.8 %collective-permute-start.11 = (f32[320,128]{1,0:T(8,128)S(1)}, f32[320,128]{1,0:T(8,128)S(1)}, u32[]{:S(2)}, u32[]{:S(2)}) collective-permute-start(f32[320,128]{1,0:T(8,128)S(1)} %add.138), channel_id=1, source_target_pairs={{0,8},{2,10},{4,12},{6,14},{8,0},{10,2},{12,4},{14,6},{1,9},{3,11}... | collective-permute-start | bytes 491528 | tf_op jit(solution)/shard_map/ppermute | solution.py:515
  105.5 4.2 %copy-start.1 = (f32[320,128]{1,0:T(8,128)}, f32[320,128]{1,0:T(8,128)S(1)}, u32[]{:S(2)}) copy-start(f32[320,128]{1,0:T(8,128)S(1)} %add.139.own_ref) | copy-start | bytes 491524
  105.5 4.1 %collective-permute-start.12 = (f32[320,128]{1,0:T(8,128)S(1)}, f32[320,128]{1,0:T(8,128)S(1)}, u32[]{:S(2)}, u32[]{:S(2)}) collective-permute-start(f32[320,128]{1,0:T(8,128)S(1)} %add.139.own_ref), channel_id=1, source_target_pairs={{0,1},{1,0},{2,3},{3,2},{4,5},{5,4},{6,7},{7,6},{8,9},{9,8},{10,11... | collective-permute-start | bytes 491528 | tf_op jit(solution)/shard_map/ppermute | solution.py:515
  105.7 9.6 %collective-permute-start.16 = (bf16[64,1024]{1,0:T(8,128)(2,1)S(1)}, bf16[64,1024]{1,0:T(8,128)(2,1)S(1)}, u32[]{:S(2)}, u32[]{:S(2)}) collective-permute-start(bf16[64,1024]{1,0:T(8,128)(2,1)S(1)} %slice.111), channel_id=1, source_target_pairs={{0,8},{2,10},{4,12},{6,14},{8,0},{10,2},{12,4},{14,6},{1,9},{3,11}... | collective-permute-start | bytes 393224 | tf_op jit(solution)/shard_map/ppermute | solution.py:515
  109.6 0.7 copy-start.3

commit v2 on v1

v2 whole, which is shorter than its diff:
```python
import functools

import jax
import jax.numpy as jnp
from jax import lax
from jax.experimental import pallas as pl
from jax.experimental.pallas import tpu as pltpu
from jax.sharding import PartitionSpec as P

epsilon = 1e-06
inverse_root = 0.7071067811865476
density_root = 0.3989422804014327
LANES = 128
GROUP = 256
RIM = 8
f32 = jnp.float32
bf16 = jnp.bfloat16
VMEM_LIMIT = 24 * 1024 * 1024


def whole(shape):
    return pl.BlockSpec(shape, lambda *_: (0,) * len(shape))


SCALAR = pl.BlockSpec(memory_space=pltpu.SMEM)
LOCAL = pl.BlockSpec(memory_space=pltpu.VMEM)


def params(limit=VMEM_LIMIT):
    return pltpu.CompilerParams(vmem_limit_bytes=limit)


def cost(microseconds):
    return pl.CostEstimate(flops=0, bytes_accessed=int(microseconds * 3.6e6), transcendentals=0)


def pad_lines(lines, count):
    blank = jnp.zeros((count - len(lines), LANES), f32)
    return jnp.concatenate(lines + [blank], axis=0) if count > len(lines) else jnp.concatenate(lines, axis=0)


def dot_tn(a, b):
    return lax.dot_general(a, b, (((0,), (0,)), ((), ())), preferred_element_type=f32)


def dot_nt(a, b):
    return lax.dot_general(a, b, (((1,), (1,)), ((), ())), preferred_element_type=f32)


def dot_nn(a, b):
    return jnp.dot(a, b, preferred_element_type=f32)


def lane_head(head_size):
    return lax.broadcasted_iota(jnp.int32, (head_size, LANES), 1) // head_size


def by_head(parts, owner):
    out = parts[0]
    for k in range(1, len(parts)):
        out = jnp.where(owner == k, parts[k], out)
    return out


def pack_diagonal(square, head_size):
    owner = lane_head(head_size)
    return by_head(
        [square[k * head_size : (k + 1) * head_size] for k in range(LANES // head_size)], owner
    )


def sum_in_head(values, owner, packed):
    sums = [jnp.sum(jnp.where(owner == k, values, 0.0), axis=1, keepdims=True) for k in range(packed)]
    return by_head([jnp.broadcast_to(s, values.shape) for s in sums], owner)


def edges_kernel(here_ref, v_head, v_tail, u_head, u_tail, twin_ref, next_ref):
    even = lax.rem(here_ref[1], 2) == 0

    def put(tail_ref, head_ref):
        tail_ref[:2] = v_tail[...]
        tail_ref[2:] = u_tail[...]
        head_ref[:2] = v_head[...]
        head_ref[2:] = u_head[...]

    @pl.when(even)
    def _():
        put(twin_ref, next_ref)

    @pl.when(jnp.logical_not(even))
    def _():
        put(next_ref, twin_ref)


def edges_call(here, v, u):
    rows, cols, width = v.shape
    out = jax.ShapeDtypeStruct((3, cols, width), bf16)
    return pl.pallas_call(
        edges_kernel,
        grid=(1,),
        in_specs=[
            SCALAR,
            pl.BlockSpec((2, cols, width), lambda i: (0, 0, 0)),
            pl.BlockSpec((2, cols, width), lambda i: (rows // 2 - 1, 0, 0)),
            pl.BlockSpec((1, cols, width), lambda i: (0, 0, 0)),
            pl.BlockSpec((1, cols, width), lambda i: (rows - 1, 0, 0)),
        ],
        out_specs=[LOCAL, LOCAL],
        out_shape=[out, out],
        compiler_params=params(),
        cost_estimate=cost(1),
        name="edges",
    )(here, v, v, u, u)


def gram_kernel(head_size, col_ref, q_ref, k_ref, mine_ref, other_ref):
    half = pl.program_id(0)
    per = GROUP // LANES
    energy = mine_ref.shape[0] - 16
    values = []
    for g in range(q_ref.shape[1] // GROUP):
        at = pl.ds(g * GROUP, GROUP)
        square = dot_tn(q_ref[:, at], k_ref[:, at])
        for p in range(per):
            cut = slice(p * LANES, (p + 1) * LANES)
            block = g * per + p
            values.append((block * head_size, pack_diagonal(square[cut, cut], head_size)))
            for line, ref in ((energy, q_ref), (energy + 8, k_ref)):
                x = ref[:, pl.ds(block * LANES, LANES)].astype(f32)
                values.append((line + block, jnp.sum(x * x, axis=0, keepdims=True)))

    def put(ref):
        for at, value in values:
            ref[pl.ds(at, value.shape[0]), :] = value

    @pl.when(half == 0)
    def _():
        mine_ref[pl.ds(energy, 16), :] = jnp.zeros((16, LANES), f32)
        other_ref[pl.ds(energy, 16), :] = jnp.zeros((16, LANES), f32)

    @pl.when(half == col_ref[0])
    def _():
        put(mine_ref)

    @pl.when(half != col_ref[0])
    def _():
        put(other_ref)


def gram_call(col, q, k, head_size):
    tokens, width = q.shape
    lines = width // 2 // LANES * head_size + 16
    out = jax.ShapeDtypeStruct((lines, LANES), f32)
    return pl.pallas_call(
        functools.partial(gram_kernel, head_size),
        grid=(2,),
        in_specs=[
            SCALAR,
            pl.BlockSpec((tokens, width // 2), lambda i: (0, i)),
            pl.BlockSpec((tokens, width // 2), lambda i: (0, i)),
        ],
        out_specs=[LOCAL, LOCAL],
        out_shape=[out, out],
        compiler_params=params(60 * 1024 * 1024),
        cost_estimate=cost(2.5),
        name="gram",
    )(col, q, k)


def gelu_terms(u):
    cumul = 0.5 * (1.0 + lax.erf(u * inverse_root))
    return u * cumul, cumul + u * jnp.exp(-0.5 * u * u) * density_root


def attention_block(head_size, raw, q_line, k_line, sharp):
    packed = LANES // head_size
    owner = lane_head(head_size)
    row = lax.broadcasted_iota(jnp.int32, (head_size, LANES), 0)
    lane = lax.broadcasted_iota(jnp.int32, (head_size, LANES), 1)
    q_energy = by_head(
        [
            jnp.broadcast_to(
                jnp.sum(jnp.where(lane == row + k * head_size, q_line, 0.0), axis=1, keepdims=True),
                raw.shape,
            )
            for k in range(packed)
        ],
        owner,
    )
    q_scale = lax.rsqrt(q_energy + epsilon)
    k_scale = lax.rsqrt(k_line + epsilon)
    gram = q_scale * raw * k_scale
    heat = by_head([jnp.full(raw.shape, s, f32) for s in sharp], owner)
    numer = jnp.exp(heat * gram)
    attention = numer / sum_in_head(numer, owner, packed)
    return attention, gram, q_scale * k_scale


def attention_phase(
    head_size, col_ref, sharp_ref, own_ref, far_ref, attn_ref, gram_ref, scale_ref, block_ref
):
    packed = LANES // head_size
    blocks = attn_ref.shape[0] // head_size
    half_blocks = blocks // 2
    is_first = col_ref[0] == 0
    block_ref[...] = jnp.zeros(block_ref.shape, bf16)
    owner = lane_head(head_size)
    for p in range(blocks):
        h, inner = divmod(p, half_blocks)

        def take(at, size):
            a = own_ref[pl.ds(at, size), :]
            b = far_ref[pl.ds(at, size), :]
            return jnp.where(is_first, a, b) if h == 0 else jnp.where(is_first, b, a)

        raw = take(inner * head_size, head_size)
        q_line = take(half_blocks * head_size + inner, 1)
        k_line = take(half_blocks * head_size + 8 + inner, 1)
        attention, gram, scale = attention_block(
            head_size, raw, q_line, k_line, [sharp_ref[p * packed + k] for k in range(packed)]
        )
        at = pl.ds(p * head_size, head_size)
        attn_ref[at, :] = attention
        gram_ref[at, :] = gram
        scale_ref[at, :] = scale
        low = attention.astype(bf16)
        inside = (p * LANES) % GROUP
        for k in range(packed):
            block_ref[pl.ds(p * LANES + k * head_size, head_size), pl.ds(inside, LANES)] = jnp.where(
                owner == k, low, jnp.zeros_like(low)
            )


def keep_side(col_ref, shape):
    place = lax.rem(lax.broadcasted_iota(jnp.int32, shape, 0), RIM)
    second = col_ref[0].astype(f32)
    right = jnp.where(place < 2, 1.0, 0.0)
    left = jnp.where(place >= RIM - 2, 1.0, 0.0)
    return right + second * (left - right)


def stencil_chunk(
    step, tile, col_ref, u_ref, side_ref, twin_ref, next_ref, corner_ref, mixed_all, proj, taps_ref,
    merged_ref, target_ref, tapsum_ref, field_ref, slope_ref, projected_ref, upside_ref,
    first_channel,
):
    tile_rows, tile_cols = tile
    tokens = tile_rows * tile_cols
    ring = tile_cols + RIM
    side = tile_rows * RIM
    chunk = pl.ds(pl.multiple_of(first_channel + step * GROUP, GROUP), GROUP)
    here = pl.ds(pl.multiple_of(step * GROUP, GROUP), GROUP)
    projected_ref[...] = dot_nn(mixed_all[...], proj[:, chunk])
    for at, size, ref, start in (
        (0, side, side_ref, side),
        (side, tile_cols, twin_ref, 2 * tile_cols),
        (side + tile_cols, tile_cols, next_ref, 2 * tile_cols),
        (side + 2 * tile_cols, 2 * RIM, corner_ref, 4 * RIM),
    ):
        piece = ref[pl.ds(start, size), chunk].astype(f32)
        if ref is side_ref or ref is corner_ref:
            piece = piece * keep_side(col_ref, piece.shape)
        upside_ref[pl.ds(at, size), :] = piece

    def lanes_body(part, carry):
        lanes = pl.ds(pl.multiple_of(part * LANES, LANES), LANES)
        glob = pl.ds(pl.multiple_of(first_channel + step * GROUP + part * LANES, LANES), LANES)
        away = pl.ds(pl.multiple_of(step * GROUP + part * LANES, LANES), LANES)
        taps = [taps_ref[pl.ds(t, 1), glob] for t in range(9)]
        rim = tokens + side
        from_next = 1 - lax.rem(col_ref[1], 2)

        def ring_row(r):
            if 0 <= r < tile_rows:
                pieces = (r * tile_cols, tokens + r * RIM)
            else:
                k = r + 2 if r < 0 else r - tile_rows
                k = k + 2 * (from_next if r < 0 else 1 - from_next)
                pieces = (
                    pl.multiple_of(rim + k * tile_cols, RIM),
                    pl.multiple_of(rim + 4 * tile_cols + k * RIM, RIM),
                )
            return jnp.concatenate(
                [
                    projected_ref[pl.ds(pieces[0], tile_cols), lanes],
                    projected_ref[pl.ds(pieces[1], RIM), lanes],
                ],
                axis=0,
            )

        def up_row(r):
            if 0 <= r < tile_rows:
                return jnp.concatenate(
                    [
                        u_ref[pl.ds(r * tile_cols, tile_cols), glob].astype(f32),
                        upside_ref[pl.ds(r * RIM, RIM), lanes],
                    ],
                    axis=0,
                )
            k = from_next if r < 0 else 1 - from_next
            pieces = (
                pl.multiple_of(side + k * tile_cols, RIM),
                pl.multiple_of(side + 2 * tile_cols + k * RIM, RIM),
            )
            return jnp.concatenate(
                [
                    upside_ref[pl.ds(pieces[0], tile_cols), lanes],
                    upside_ref[pl.ds(pieces[1], RIM), lanes],
                ],
                axis=0,
            )

        for r in range(-2, tile_rows + 2):
            field_ref[r + 2] = ring_row(r).astype(bf16).astype(f32)
        for r in range(-1, tile_rows + 1):
            near = [field_ref[r + 1 + a] for a in range(3)]
            sums = [sum(taps[3 * a + b] * near[a] for a in range(3)) for b in range(3)]
            total = pltpu.roll(sums[0], 1, 0) + sums[1] + pltpu.roll(sums[2], ring - 1, 0)
            active, slope = gelu_terms(total)
            slope_ref[r + 1] = (up_row(r) * slope).astype(bf16).astype(f32)
            if 0 <= r < tile_rows:
                at = pl.ds(r * tile_cols, tile_cols)
                merged_ref[at, lanes] = (projected_ref[at, lanes] + active[:tile_cols]).astype(bf16)
        weights = [jnp.zeros((8, LANES), f32) for _ in range(9)]
        blank = jnp.zeros((RIM, LANES), f32)
        for r in range(tile_rows):
            near = [slope_ref[r + 2 - a] for a in range(3)]
            sums = [sum(taps[3 * a + b] * near[a] for a in range(3)) for b in range(3)]
            back = pltpu.roll(sums[0], ring - 1, 0) + sums[1] + pltpu.roll(sums[2], 1, 0)
            at = pl.ds(r * tile_cols, tile_cols)
            target_ref[at, away] = (u_ref[at, glob].astype(f32) + back[:tile_cols]).astype(bf16)
            centre = jnp.concatenate([near[1][:tile_cols], blank], axis=0)
            shifted = [pltpu.roll(centre, ring - 1, 0), centre, pltpu.roll(centre, 1, 0)]
            for a in range(3):
                line = field_ref[r + 1 + a]
                for b in range(3):
                    product = shifted[b] * line
                    weights[3 * a + b] = weights[3 * a + b] + jnp.sum(
                        product.reshape(ring // 8, 8, LANES), axis=0
                    )
        for t in range(9):
            tapsum_ref[pl.ds(t, 1), away] = jnp.sum(weights[t], axis=0, keepdims=True)
        return carry

    lax.fori_loop(0, GROUP // LANES, lanes_body, 0)


def spread_product(piece_rows, cols, order, here_ref, mixed_all, target_ref, mine_ref, other_ref):
    tokens = target_ref.shape[0]
    axis, bit = order[0]
    apart = bit if axis == "col" else bit * cols
    index = {"col": here_ref[0], "row": here_ref[1]}
    flipped = (index[axis] // bit) % 2 == 1
    per = GROUP // piece_rows
    for g in range(mixed_all.shape[1] // GROUP):
        product = dot_tn(mixed_all[pl.ds(0, tokens), pl.ds(g * GROUP, GROUP)], target_ref[...])
        for k in range(per):
            if k & apart:
                continue
            owner = g * per + k
            a, b = (product[x * piece_rows : (x + 1) * piece_rows] for x in (k, k | apart))
            away = {"col": (owner % cols) ^ index["col"], "row": (owner // cols) ^ index["row"]}
            place = 0
            for name, digit in order[1:]:
                place = 2 * place + (away[name] // digit) % 2
            at = pl.ds(pl.multiple_of(place * piece_rows, piece_rows), piece_rows)
            mine_ref[at, :] = jnp.where(flipped, b, a)
            other_ref[at, :] = jnp.where(flipped, a, b).astype(bf16)


def front_kernel(
    head_size, tile, piece_rows, cols, order,
    col_ref, sharp_ref, own_ref, far_ref, v_ref, u_ref, side_ref, twin_ref, next_ref,
    corner_ref, proj_ref, taps_ref,
    merged_ref, attn_ref, gram_ref, scale_ref, block_ref, mixed_all, target_ref, tapsum_ref,
    mine_ref, other_ref,
    field_ref, slope_ref, projected_ref, upside_ref,
):
    step = pl.program_id(0)
    tile_rows, tile_cols = tile
    tokens, width = v_ref.shape
    side = tile_rows * RIM
    two = 2 * tile_cols

    @pl.when(step == 0)
    def _():
        tapsum_ref[...] = jnp.zeros(tapsum_ref.shape, f32)
        attention_phase(
            head_size, col_ref, sharp_ref, own_ref, far_ref, attn_ref, gram_ref, scale_ref, block_ref
        )
        for g in range(width // GROUP):
            at = pl.ds(g * GROUP, GROUP)
            weights = block_ref[at, :]
            mixed_all[pl.ds(0, tokens), at] = dot_nt(v_ref[:, at], weights).astype(bf16)
            around = [(side_ref, side), (twin_ref, two), (next_ref, two), (corner_ref, 4 * RIM)]
            value = dot_nt(
                jnp.concatenate([ref[pl.ds(0, size), at] for ref, size in around], axis=0), weights
            )
            start = 0
            for ref, size in around:
                piece = value[start : start + size]
                if ref is side_ref or ref is corner_ref:
                    piece = piece * keep_side(col_ref, piece.shape)
                mixed_all[pl.ds(tokens + start, size), at] = piece.astype(bf16)
                start += size

    stencil_chunk(
        step, tile, col_ref, u_ref, side_ref, twin_ref, next_ref, corner_ref, mixed_all, proj_ref,
        taps_ref, merged_ref, target_ref, tapsum_ref, field_ref, slope_ref, projected_ref, upside_ref, 0,
    )

    @pl.when(step == pl.num_programs(0) - 1)
    def _():
        spread_product(piece_rows, cols, order, col_ref, mixed_all, target_ref, mine_ref, other_ref)


def back_kernel(
    head_size, tile, first_channel,
    col_ref, u_ref, v_ref, side_ref, twin_ref, next_ref, corner_ref, mixed_all, proj_ref, taps_ref,
    front_target, front_taps, merged_before,
    merged_ref, target_ref, grad_ref, mine_ref, other_ref,
    field_ref, slope_ref, projected_ref, upside_ref, tapsum_ref, whole_ref,
):
    step = pl.program_id(0)
    last = pl.num_programs(0) - 1
    tokens, width = v_ref.shape
    blocks = width // LANES
    half_blocks = blocks // 2

    @pl.when(step == 0)
    def _():
        tapsum_ref[...] = jnp.zeros(tapsum_ref.shape, f32)

    stencil_chunk(
        step, tile, col_ref, u_ref, side_ref, twin_ref, next_ref, corner_ref, mixed_all, proj_ref,
        taps_ref, merged_ref, target_ref, tapsum_ref, field_ref, slope_ref, projected_ref, upside_ref,
        first_channel,
    )

    @pl.when(step == last)
    def _():
        whole_ref[:, pl.ds(0, first_channel)] = front_target[...]
        whole_ref[:, pl.ds(first_channel, width - first_channel)] = target_ref[...]
        grad_ref[...] = dot_nt(whole_ref[...], proj_ref[...]).astype(bf16)
        for g in range(width // GROUP):
            at = pl.ds(g * GROUP, GROUP)
            square = dot_tn(grad_ref[:, at], v_ref[:, at])
            for p in range(GROUP // LANES):
                cut = slice(p * LANES, (p + 1) * LANES)
                block = g * (GROUP // LANES) + p
                h, inner = divmod(block, half_blocks)
                packed_rows = pack_diagonal(square[cut, cut], head_size)
                if block * LANES < first_channel:
                    tap_rows = front_taps[:, pl.ds(block * LANES, LANES)]
                else:
                    tap_rows = tapsum_ref[:, pl.ds(block * LANES - first_channel, LANES)]

                def put(ref, inner=inner, packed_rows=packed_rows, tap_rows=tap_rows):
                    ref[pl.ds(inner * head_size, head_size), :] = packed_rows.astype(ref.dtype)
                    ref[pl.ds(half_blocks * head_size + inner * 16, 16), :] = tap_rows.astype(ref.dtype)

                @pl.when(col_ref[0] == h)
                def _():
                    put(mine_ref)

                @pl.when(col_ref[0] != h)
                def _():
                    put(other_ref)


def stencil_scratch(tile):
    ring = tile[1] + RIM
    return [
        pltpu.VMEM((tile[0] + 4, ring, LANES), f32),
        pltpu.VMEM((tile[0] + 2, ring, LANES), f32),
        pltpu.VMEM(((tile[0] + 4) * ring, GROUP), f32),
        pltpu.VMEM(((tile[0] + 2) * ring, GROUP), f32),
    ]


def front_call(col, sharp, own, far, v, u, halo, proj, taps, tile, head_size, piece_rows, cols, order):
    tokens, width = v.shape
    ring = tile[1] + RIM
    span = width // 2
    grams = width // LANES * head_size
    sds = jax.ShapeDtypeStruct
    outs = [
        sds((tokens, width), bf16),
        sds((grams, LANES), f32),
        sds((grams, LANES), f32),
        sds((grams, LANES), f32),
        sds((width, GROUP), bf16),
        sds(((tile[0] + 4) * ring, width), bf16),
        sds((tokens, span), bf16),
        sds((16, span), f32),
        sds((width // 2, span), f32),
        sds((width // 2, span), bf16),
    ]
    args = (col, sharp, own, far, v, u, *halo, proj, taps)
    return pl.pallas_call(
        functools.partial(front_kernel, head_size, tile, piece_rows, cols, order),
        grid=(span // GROUP,),
        in_specs=[SCALAR] * 2 + [LOCAL] * (len(args) - 2),
        out_specs=[pl.BlockSpec((tokens, GROUP), lambda i: (0, i))] + [LOCAL] * (len(outs) - 1),
        out_shape=outs,
        scratch_shapes=stencil_scratch(tile),
        compiler_params=params(),
        cost_estimate=cost(10),
        name="front",
    )(*args)


def back_call(col, u, v, halo, mixed_all, proj, taps, target, tapsum, merged, tile, head_size):
    tokens, width = v.shape
    span = width // 2
    lines = width // LANES // 2 * (head_size + 16)
    sds = jax.ShapeDtypeStruct
    outs = [
        sds((tokens, width), bf16),
        sds((tokens, span), bf16),
        sds((tokens, width), bf16),
        sds((lines, LANES), f32),
        sds((lines, LANES), bf16),
    ]
    args = (col, u, v, *halo, mixed_all, proj, taps, target, tapsum, merged)
    first = span // GROUP
    return pl.pallas_call(
        functools.partial(back_kernel, head_size, tile, span),
        grid=(span // GROUP,),
        in_specs=[SCALAR] + [LOCAL] * (len(args) - 2) + [pl.BlockSpec(memory_space=pl.ANY)],
        out_specs=[pl.BlockSpec((tokens, GROUP), lambda i: (0, i + first))] + [LOCAL] * (len(outs) - 1),
        out_shape=outs,
        input_output_aliases={len(args) - 1: 0},
        scratch_shapes=stencil_scratch(tile)
        + [pltpu.VMEM((16, span), f32), pltpu.VMEM((tokens, width), bf16)],
        compiler_params=params(),
        cost_estimate=cost(10),
        name="back",
    )(*args)


def projector_kernel(
    piece_rows, cols, order, here_ref, mixed_all, target_ref, after_ref, mine_ref, other_ref
):
    spread_product(piece_rows, cols, order, here_ref, mixed_all, target_ref, mine_ref, other_ref)


def projector_call(here, mixed_all, target, after, piece_rows, cols, order):
    width, span = mixed_all.shape[1], target.shape[1]
    sds = jax.ShapeDtypeStruct
    return pl.pallas_call(
        functools.partial(projector_kernel, piece_rows, cols, order),
        in_specs=[SCALAR, LOCAL, LOCAL, pl.BlockSpec(memory_space=pl.ANY)],
        out_specs=[LOCAL, LOCAL],
        out_shape=[sds((width // 2, span), f32), sds((width // 2, span), bf16)],
        compiler_params=params(),
        cost_estimate=cost(2),
        name="projector",
    )(here, mixed_all, target, after)


def content_kernel(grad_ref, block_ref, after_ref, out_ref):
    span = out_ref.shape[1]
    for g in range(span // GROUP):
        at = pl.ds(pl.multiple_of(pl.program_id(0) * span + g * GROUP, GROUP), GROUP)
        out_ref[:, pl.ds(g * GROUP, GROUP)] = dot_nn(grad_ref[:, at], block_ref[at, :]).astype(bf16)


def content_call(grad, block, after):
    tokens, width = grad.shape
    return pl.pallas_call(
        content_kernel,
        grid=(2,),
        in_specs=[LOCAL] * 2 + [pl.BlockSpec(memory_space=pl.ANY)],
        out_specs=pl.BlockSpec((tokens, width // 2), lambda i: (0, i)),
        out_shape=jax.ShapeDtypeStruct((tokens, width), bf16),
        compiler_params=params(),
        cost_estimate=cost(2),
        name="content",
    )(grad, block, after)


def final_kernel(
    head_size,
    col_ref,
    sharp_ref,
    own_ref,
    far_ref,
    energy_own_ref,
    energy_far_ref,
    attn_ref,
    gram_ref,
    scale_ref,
    q_ref,
    k_ref,
    dq_ref,
    dk_ref,
    heat_ref,
    taps_ref,
    mixer_ref,
):
    step = pl.program_id(0)
    steps = pl.num_programs(0)
    packed = LANES // head_size
    per = GROUP // LANES
    half_blocks = steps * per // 2
    mine = (step // (steps // 2)) == col_ref[0]
    owner = lane_head(head_size)
    row = lax.broadcasted_iota(jnp.int32, (head_size, LANES), 0)
    lane = lax.broadcasted_iota(jnp.int32, (head_size, LANES), 1)
    mixer_ref[...] = jnp.zeros(mixer_ref.shape, bf16)
    q_terms, k_terms = [], []
    for p in range(per):
        block = step * per + p
        inner = lax.rem(block, half_blocks)

        def take(own, far, at, size):
            return jnp.where(mine, own[pl.ds(at, size), :], far[pl.ds(at, size), :])

        grad = take(own_ref, far_ref, pl.multiple_of(inner * head_size, head_size), head_size)
        taps_ref[:, pl.ds(p * LANES, LANES)] = take(
            own_ref, far_ref, pl.multiple_of(half_blocks * head_size + inner * 16, 16), 16
        )[:9]
        q_line = take(energy_own_ref, energy_far_ref, half_blocks * head_size + inner, 1)
        k_line = take(energy_own_ref, energy_far_ref, half_blocks * head_size + 8 + inner, 1)
        at = pl.ds(pl.multiple_of(block * head_size, head_size), head_size)
        attention, gram, scale = attn_ref[at, :], gram_ref[at, :], scale_ref[at, :]
        scores = attention * (grad - sum_in_head(attention * grad, owner, packed))
        heated = scores * gram
        heat = by_head(
            [jnp.full(scores.shape, sharp_ref[block * packed + k], f32) for k in range(packed)], owner
        )
        for k in range(packed):
            heat_ref[block * packed + k] = jnp.sum(jnp.where(owner == k, heated, 0.0))
        gram_grad = heat * scores
        corr = gram_grad * gram
        k_corr = jnp.sum(corr, axis=0, keepdims=True)
        columns = sum_in_head(corr, owner, packed)
        q_corr = jnp.sum(jnp.where(lane == row + owner * head_size, columns, 0.0), axis=0, keepdims=True)
        q_scale = lax.rsqrt(q_line + epsilon)
        k_scale = lax.rsqrt(k_line + epsilon)
        q_terms.append(q_scale * q_scale * q_corr)
        k_terms.append(k_scale * k_scale * k_corr)
        low = (scale * gram_grad).astype(bf16)
        for k in range(packed):
            mixer_ref[pl.ds(p * LANES + k * head_size, head_size), pl.ds(p * LANES, LANES)] = jnp.where(
                owner == k, low, jnp.zeros_like(low)
            )
    here = pl.ds(pl.multiple_of(step * GROUP, GROUP), GROUP)
    q, k = q_ref[:, here], k_ref[:, here]
    mixer = mixer_ref[...]
    dq_ref[...] = (dot_nt(k, mixer) - q.astype(f32) * jnp.concatenate(q_terms, axis=1)).astype(bf16)
    dk_ref[...] = (dot_nn(q, mixer) - k.astype(f32) * jnp.concatenate(k_terms, axis=1)).astype(bf16)


def final_call(col, sharp, own, far, energy_own, energy_far, attn, gram, scale, q, k, head_size):
    tokens, width = q.shape
    sds = jax.ShapeDtypeStruct
    token_block = pl.BlockSpec((tokens, GROUP), lambda i: (0, i))
    args = (col, sharp, own, far, energy_own, energy_far, attn, gram, scale, q, k)
    return pl.pallas_call(
        functools.partial(final_kernel, head_size),
        grid=(width // GROUP,),
        in_specs=[SCALAR, SCALAR] + [LOCAL] * 9,
        out_specs=[
            token_block,
            token_block,
            SCALAR,
            pl.BlockSpec((9, GROUP), lambda i: (0, i)),
        ],
        out_shape=[
            sds((tokens, width), bf16),
            sds((tokens, width), bf16),
            sds(sharp.shape, f32),
            sds((9, width), f32),
        ],
        scratch_shapes=[pltpu.VMEM((GROUP, GROUP), bf16)],
        compiler_params=params(),
        cost_estimate=cost(5),
        name="final",
    )(*args)


def swap(x, axis, bit):
    return lax.ppermute(x, axis, [(i, i ^ bit) for i in range(lax.axis_size(axis))])


def row_bits():
    bits, bit = [], 1
    while bit < lax.axis_size("row"):
        bits.append(bit)
        bit *= 2
    return bits


def halve(total):
    half = total.shape[0] // 2
    return total[:half], total[half:].astype(bf16)


def add_low(total, got):
    return total + got.astype(f32)


def add_step(total, axis, bit):
    low = total.astype(bf16)
    return low.astype(f32) + swap(low, axis, bit).astype(f32)


def scatter_step(total, group):
    count = 2 ** len(group)
    rows = total.shape[0] // count
    out = total[:rows]
    for k in range(1, count):
        mask = sum(bit for i, bit in enumerate(group) if (k >> (len(group) - 1 - i)) & 1)
        out = add_low(out, swap(total[k * rows : (k + 1) * rows].astype(bf16), "row", mask))
    return out


def scatter_both(first, second, group):
    early, late = group
    quarter, half = first.shape[0] // 4, second.shape[0] // 2
    pieces = [first[k * quarter : (k + 1) * quarter] for k in range(4)]
    joint = swap(jnp.concatenate([pieces[1], second[half:]]).astype(bf16), "row", late)
    first = add_low(pieces[0], swap(pieces[2].astype(bf16), "row", early))
    first = add_low(first, swap(pieces[3].astype(bf16), "row", early | late))
    return add_low(first, joint[:quarter]), add_low(second[:half], joint[quarter:])


def tie(*values):
    return lax.optimization_barrier(values)


def shards(q, k, v, u, sharp, proj, taps):
    tile = v.shape[:2]
    width = v.shape[2]
    tokens = tile[0] * tile[1]
    head_size = width // sharp.shape[0]
    rows, cols = lax.axis_size("row"), lax.axis_size("col")
    flat = lambda x: x.reshape(tokens, width)
    here = jnp.stack([lax.axis_index("col"), lax.axis_index("row")]).astype(jnp.int32)
    q2, k2, v2, u2 = flat(q), flat(k), flat(v), flat(u)
    bits = row_bits()
    early = [("row", bits[0]), ("col", 1)] + [("row", bit) for bit in bits[1:]]
    late = [("col", 1)] + [("row", bit) for bit in bits]
    piece_rows = width // (rows * cols)

    mine, other = gram_call(here, q2, k2, head_size)
    to_twin, to_next = edges_call(here, v, u)
    total = add_low(mine, swap(other, "col", 1))
    start = jnp.where(lax.axis_index("col") == 0, v.shape[1] - RIM, 0)
    edge = lambda x: lax.dynamic_slice_in_dim(x, start, RIM, axis=1)
    pairs_next = [(j, j + 1) for j in range(1, rows - 1, 2)]
    pairs_next = pairs_next + [(b, a) for a, b in pairs_next]
    side = swap(jnp.concatenate([edge(v), edge(u)]), "col", 1)
    for i, bit in enumerate(bits):
        total = total + swap(total, "row", bit)
        if i == 1:
            from_twin = swap(to_twin, "row", 1)
            total, from_twin = tie(total, from_twin)
        if i == 2:
            from_next = lax.ppermute(to_next, "row", pairs_next)
            total, from_next = tie(total, from_next)
    corner = swap(
        edge(jnp.concatenate([from_twin[:2], from_next[:2], from_twin[2:], from_next[2:]])), "col", 1
    )
    around = tuple(x.reshape(-1, width) for x in (side, from_twin, from_next, corner))
    energy_own, energy_far = total, swap(total, "col", 1)

    (merged, attn, gram, scale, block, mixed_all, front_target, front_taps, mine, other) = front_call(
        here, sharp, energy_own, energy_far, v2, u2, around, proj, taps, tile, head_size, piece_rows, cols, early
    )
    halves = [swap(x, "row", bits[0]) for x in jnp.split(other, 2)]
    first = halves[:1]
    front_mine = mine
    merged, target, grad, mine, other = back_call(
        here, u2, v2, around, mixed_all, proj, taps, front_target, front_taps, merged, tile, head_size
    )

    mine, other, *first = tie(mine, other, *first)
    after = swap(other, "col", 1)
    total = add_low(mine, after)
    turns = bits[1:2] + bits[:1] + bits[2:]
    back_mine, back_other = projector_call(here, mixed_all, target, after, piece_rows, cols, late)
    front_sum = add_low(front_mine, jnp.concatenate([*first, *halves[1:]]))
    back_sum = add_low(back_mine, swap(back_other, "col", 1))
    total = add_step(total, "row", turns[0])
    total, back_sum = tie(total, back_sum)
    total = add_step(total, "row", turns[1])
    total, front_sum = tie(total, front_sum)
    for bit in turns[2:]:
        total = add_step(total, "row", bit)
    front_sum, leaves = halve(front_sum)
    front_sum = add_low(front_sum, swap(leaves, "col", 1))
    back_sum = scatter_step(back_sum, bits[:2])
    front_sum = scatter_step(front_sum, bits[1:2])
    total, back_sum = tie(total, back_sum)
    for bit in bits[2:-1]:
        front_sum, back_sum = scatter_step(front_sum, [bit]), scatter_step(back_sum, [bit])
    far = swap(total, "col", 1)
    kept, leaves = zip(halve(front_sum), halve(back_sum))
    got = swap(jnp.concatenate(leaves), "row", bits[-1])
    dq, dk, heat, tap_sums = final_call(
        here, sharp, total, far, energy_own, energy_far, attn, gram, scale, q2, k2, head_size
    )
    content = content_call(grad, block, tap_sums)
    content, *kept = tie(content, *kept)
    front_sum, back_sum = (add_low(x, y) for x, y in zip(kept, jnp.split(got, 2)))
    projector = jnp.concatenate([front_sum, back_sum], axis=1)
    full = lambda x: x.reshape(tile + (width,))
    return full(merged), full(dq), full(dk), full(content), heat, tap_sums, projector


def solution(mesh):
    field = P(("scene", "row"), "col", None)
    return jax.shard_map(
        shards,
        mesh=mesh,
        in_specs=(field, field, field, field, P(), P(), P()),
        out_specs=(
            field,
            field,
            field,
            field,
            P("scene"),
            P("scene", None),
            P(("scene", "row", "col"), None),
        ),
        check_vma=False,
    )
```

time: 117 us -> 86.7 us (0.74)
  waiting for transfers between devices: 45.2 us -> 32.4 us
  Pallas kernels: 36 us -> 26.6 us
  local copies, waits for them, and re-layouts: 6.83 us -> 1.11 us
  other arithmetic: 4.71 us -> 2.13 us
    ppermute x15 -> x22, waiting for transfers between devices: 42 us -> 32.4 us  [swap(): lax.ppermute(x, axis, [(i, i ^ bit) for i in range(lax.axis_size(axis))])]
    pallas_call x3 -> x5, Pallas kernels: 28.3 us -> 20.3 us  [the longest x1 8.84 us: back_call(): pl.pallas_call(functools.partial(back_kernel, head_size, tile, span), gri...]
    ppermute x15 -> x22, starting transfers between devices: 16.6 us -> 22.6 us  [swap(): lax.ppermute(x, axis, [(i, i ^ bit) for i in range(lax.axis_size(axis))])]
    slice x15 -> x12, local copies, waits for them, and re-layouts: 5.49 us -> 0.15 us  [the longest x6 0.07 us: halve(): return (total[:half], total[half:].astype(bf16))]
    ppermute x2 -> x1, starting transfers between devices: 5.76 us -> 0.66 us  [shards(): from_next = lax.ppermute(to_next, 'row', pairs_next)]
    ppermute x2 -> x1, waiting for transfers between devices: 3.2 us -> 0.01 us  [shards(): from_next = lax.ppermute(to_next, 'row', pairs_next)]
    add x13, other arithmetic: 3.1 us -> 0.66 us  [the longest x7 0.54 us: add_low(): return total + got.astype(f32)]
    pallas_call x1, Pallas kernels: 4.99 us -> 3.53 us  [final_call(): pl.pallas_call(functools.partial(final_kernel, head_size), grid=(width //...]
  transfers between devices with their start and end apart: 17 -> 23, of which waited for: 9 -> 10; matrix products, arithmetic and copies ran while one was open for 6% -> 1% of each run, Pallas kernels for 8% -> 18%
where the time goes in v2:
time: 86.7 us; the launch traced here: 86.6 us
  waiting for transfers between devices  32.4 us (37%)
  Pallas kernels  26.6 us (31%)
  starting transfers between devices  23.3 us (27%)
  other arithmetic  2.13 us (2%)
  local copies, waits for them, and re-layouts  1.11 us (1%)
  between operations  1.05 us (1%)
    ppermute x22, waiting for transfers between devices, swap(): lax.ppermute(x, axis, [(i, i ^ bit) for i in range(lax.axis_size(axis))])  32.4 us
    ppermute x22, starting transfers between devices, swap(): lax.ppermute(x, axis, [(i, i ^ bit) for i in range(lax.axis_size(axis))])  22.6 us
    pallas_call x1, Pallas kernels, back_call(): pl.pallas_call(functools.partial(back_kernel, head_size, tile, span), gri...  8.84 us
    pallas_call x1, Pallas kernels, front_call(): pl.pallas_call(functools.partial(front_kernel, head_size, tile, piece_row...  8.2 us
    pallas_call x1, Pallas kernels, final_call(): pl.pallas_call(functools.partial(final_kernel, head_size), grid=(width //...  3.53 us
    pallas_call x1, Pallas kernels, gram_call(): pl.pallas_call(functools.partial(gram_kernel, head_size), grid=(2,), in_s...  2.73 us
  transfers between devices with their start and end apart: 23, of which 10 were waited for; matrix products, arithmetic and copies ran while one was open for 1% of the time, Pallas kernels for 18%

profile of v2, /device:TPU:0, one launch (start us, length us, event | category | flops | bytes accessed | tf_op | source)
XLA Modules:
  0.0 86.6 jit_solution(15547255299629760389)
XLA Ops:
  0.7 0.6 pad_add_fusion.col_ref.here_ref
  1.2 2.7 %gram.1 = (f32[272,128]{1,0:T(8,128)}, f32[272,128]{1,0:T(8,128)}) custom-call(s32[2]{0:T(128)} %pad_add_fusion.col_ref.here_ref, bf16[512,1024]{1,0:T(8,128)(2,1)} %bitcast.18, bf16[512,1024]{1,0:T(8,128)(2,1)} %bitcast.20), custom_call_target="tpu_custom_call" | custom-call | bytes 9000000 | tf_op jit(solution)/shard_map/gram/pallas_call | solution.py:154
  4.4 0.6 edges.1
  5.0 2.6 %collective-permute-start.4 = (bf16[3,32,1024]{2,1,0:T(8,128)(2,1)S(1)}, bf16[3,32,1024]{2,1,0:T(8,128)(2,1)S(1)}, u32[]{:S(2)}, u32[]{:S(2)}) collective-permute-start(bf16[3,32,1024]{2,1,0:T(8,128)(2,1)S(1)} %get-tuple-element.50), channel_id=1, source_target_pairs={{0,2},{2,0},{4,6},{6,4},{8,10},{10,8},{12,14},{14,12},{1,3},{3,1},... | collective-permute-start | bytes 589832 | tf_op jit(solution)/shard_map/ppermute | solution.py:685
  7.8 0.8 collective-permute-start.2
  8.7 7.4 %collective-permute-done.2 = f32[272,128]{1,0:T(8,128)S(1)} collective-permute-done((f32[272,128]{1,0:T(8,128)S(1)}, f32[272,128]{1,0:T(8,128)S(1)}, u32[]{:S(2)}, u32[]{:S(2)}) %collective-permute-start.2) | collective-permute-done | bytes 139296 | tf_op jit(solution)/shard_map/ppermute | solution.py:685
  16.2 1.9 %collective-permute-start.3 = (f32[272,128]{1,0:T(8,128)S(1)}, f32[272,128]{1,0:T(8,128)S(1)}, u32[]{:S(2)}, u32[]{:S(2)}) collective-permute-start(f32[272,128]{1,0:T(8,128)S(1)} %add.55), channel_id=1, source_target_pairs={{0,4},{2,6},{4,0},{6,2},{8,12},{10,14},{12,8},{14,10},{1,5},{3,7},... | collective-permute-start | bytes 417800 | tf_op jit(solution)/shard_map/ppermute | solution.py:685
  18.1 0.7 collective-permute-start.6
  18.7 3.0 %collective-permute-done.3 = f32[272,128]{1,0:T(8,128)S(1)} collective-permute-done((f32[272,128]{1,0:T(8,128)S(1)}, f32[272,128]{1,0:T(8,128)S(1)}, u32[]{:S(2)}, u32[]{:S(2)}) %collective-permute-start.3) | collective-permute-done | bytes 139296 | tf_op jit(solution)/shard_map/ppermute | solution.py:685
  21.8 2.7 %collective-permute-start.5 = (f32[272,128]{1,0:T(8,128)S(1)}, f32[272,128]{1,0:T(8,128)S(1)}, u32[]{:S(2)}, u32[]{:S(2)}) collective-permute-start(f32[272,128]{1,0:T(8,128)S(1)} %add.56), channel_id=1, source_target_pairs={{0,8},{2,10},{4,12},{6,14},{8,0},{10,2},{12,4},{14,6},{1,9},{3,11}... | collective-permute-start | bytes 417800 | tf_op jit(solution)/shard_map/ppermute | solution.py:685
  24.5 8.5 %collective-permute-done.5 = f32[272,128]{1,0:T(8,128)S(1)} collective-permute-done((f32[272,128]{1,0:T(8,128)S(1)}, f32[272,128]{1,0:T(8,128)S(1)}, u32[]{:S(2)}, u32[]{:S(2)}) %collective-permute-start.5) | collective-permute-done | bytes 139296 | tf_op jit(solution)/shard_map/ppermute | solution.py:685
  33.7 0.9 %collective-permute-done.7 = bf16[6,8,1024]{2,1,0:T(8,128)(2,1)S(1)} collective-permute-done((bf16[6,8,1024]{2,1,0:T(8,128)(2,1)S(1)}, bf16[6,8,1024]{2,1,0:T(8,128)(2,1)S(1)}, u32[]{:S(2)}, u32[]{:S(2)}) %collective-permute-start.7) | collective-permute-done | bytes 98336 | tf_op jit(solution)/shard_map/ppermute | solution.py:685
  34.6 8.2 %front.1 = (bf16[512,1024]{1,0:T(8,128)(2,1)}, f32[512,128]{1,0:T(8,128)S(1)}, f32[512,128]{1,0:T(8,128)S(1)}, f32[512,128]{1,0:T(8,128)S(1)}, bf16[1024,256]{1,...) custom-call(s32[2]{0:T(128)S(1)} %copy-done.7, ...), custom_call_target="tpu_custom_call" | custom-call | bytes 36000000 | tf_op jit(solution)/shard_map/front/pallas_call | solution.py:500
  43.0 8.8 %back.1 = (bf16[512,1024]{1,0:T(8,128)(2,1)}, bf16[512,512]{1,0:T(8,128)(2,1)S(1)}, bf16[512,1024]{1,0:T(8,128)(2,1)S(1)}, f32[320,128]{1,0:T(8,128)S(1)}, bf16[320,128]{1,0:T(8,128)(2,1)S(1)}) custom-call(s32[2]{0:T(128)S(1)} %copy-done.7, bf16[512,1024]{1,0:T(8,128)(2,1)S(1)} %bitcast.15, ...), custom_call_target="tpu_custom_call", output_to_operand_aliasing={{0}: (12, {})} | custom-call | bytes 36000000 | tf_op jit(solution)/shard_map/back/pallas_call | solution.py:527
  52.2 1.7 %collective-permute-start.14 = (bf16[256,512]{1,0:T(8,128)(2,1)S(1)}, bf16[256,512]{1,0:T(8,128)(2,1)S(1)}, u32[]{:S(2)}, u32[]{:S(2)}) collective-permute-start(bf16[256,512]{1,0:T(8,128)(2,1)S(1)} %get-tuple-element.92), channel_id=1, source_target_pairs={{0,2},{2,0},{4,6},{6,4},{8,10},{10,8},{12,14},{14,12},{1,3},{3,1},... | collective-permute-start | bytes 786440 | tf_op jit(solution)/shard_map/ppermute | solution.py:685
  53.9 1.3 %projector.1 = (f32[512,512]{1,0:T(8,128)S(1)}, bf16[512,512]{1,0:T(8,128)(2,1)S(1)}) custom-call(s32[2]{0:T(128)S(1)} %copy-done.7, bf16[800,1024]{1,0:T(8,128)(2,1)S(1)} %get-tuple-element.56.mixed_all, bf16[512,512]{1,0:T(8,128)(2,1)S(1)} %get-tuple-element.66.target_ref, bf16[320,128]{1,0:T(8,128)(2,1)S(1)} %collective-permute-done.10.after_ref), custom_call_target="tpu_custom_call" | custom-call | bytes 7200000 | tf_op jit(solution)/shard_map/projector/pallas_call | solution.py:551
  56.0 4.8 %collective-permute-done.14 = bf16[256,512]{1,0:T(8,128)(2,1)S(1)} collective-permute-done((bf16[256,512]{1,0:T(8,128)(2,1)S(1)}, bf16[256,512]{1,0:T(8,128)(2,1)S(1)}, u32[]{:S(2)}, u32[]{:S(2)}) %collective-permute-start.14) | collective-permute-done | bytes 262176 | tf_op jit(solution)/shard_map/ppermute | solution.py:685
  61.2 1.8 %collective-permute-start.13 = (bf16[320,128]{1,0:T(8,128)(2,1)S(1)}, bf16[320,128]{1,0:T(8,128)(2,1)S(1)}, u32[]{:S(2)}, u32[]{:S(2)}) collective-permute-start(bf16[320,128]{1,0:T(8,128)(2,1)S(1)} %convert_add_fusion.6), channel_id=1, source_target_pairs={{0,2},{2,0},{4,6},{6,4},{8,10},{10,8},{12,14},{14,12},{1,3},{3,1},... | collective-permute-start | bytes 245768 | tf_op jit(solution)/shard_map/ppermute | solution.py:685
  63.2 1.7 %collective-permute-start.18 = (bf16[128,512]{1,0:T(8,128)(2,1)S(1)}, bf16[128,512]{1,0:T(8,128)(2,1)S(1)}, u32[]{:S(2)}, u32[]{:S(2)}) collective-permute-start(bf16[128,512]{1,0:T(8,128)(2,1)S(1)} %get-tuple-element.90), channel_id=1, source_target_pairs={{0,6},{2,4},{4,2},{6,0},{8,14},{10,12},{12,10},{14,8},{1,7},{3,5},... | collective-permute-start | bytes 393224 | tf_op jit(solution)/shard_map/ppermute | solution.py:685
  64.9 1.7 %collective-permute-start.17 = (bf16[128,512]{1,0:T(8,128)(2,1)S(1)}, bf16[128,512]{1,0:T(8,128)(2,1)S(1)}, u32[]{:S(2)}, u32[]{:S(2)}) collective-permute-start(bf16[128,512]{1,0:T(8,128)(2,1)S(1)} %get-tuple-element.91), channel_id=1, source_target_pairs={{0,2},{2,0},{4,6},{6,4},{8,10},{10,8},{12,14},{14,12},{1,3},{3,1},... | collective-permute-start | bytes 393224 | tf_op jit(solution)/shard_map/ppermute | solution.py:685
  66.8 1.2 %collective-permute-start.15 = (bf16[320,128]{1,0:T(8,128)(2,1)S(1)}, bf16[320,128]{1,0:T(8,128)(2,1)S(1)}, u32[]{:S(2)}, u32[]{:S(2)}) collective-permute-start(bf16[320,128]{1,0:T(8,128)(2,1)S(1)} %convert_add_fusion.5), channel_id=1, source_target_pairs={{0,8},{2,10},{4,12},{6,14},{8,0},{10,2},{12,4},{14,6},{1,9},{3,11}... | collective-permute-start | bytes 245768 | tf_op jit(solution)/shard_map/ppermute | solution.py:685
  68.1 1.3 %collective-permute-done.16 = bf16[128,512]{1,0:T(8,128)(2,1)S(1)} collective-permute-done((bf16[128,512]{1,0:T(8,128)(2,1)S(1)}, bf16[128,512]{1,0:T(8,128)(2,1)S(1)}, u32[]{:S(2)}, u32[]{:S(2)}) %collective-permute-start.16) | collective-permute-done | bytes 131104 | tf_op jit(solution)/shard_map/ppermute | solution.py:685
  69.3 1.2 %collective-permute-done.18 = bf16[128,512]{1,0:T(8,128)(2,1)S(1)} collective-permute-done((bf16[128,512]{1,0:T(8,128)(2,1)S(1)}, bf16[128,512]{1,0:T(8,128)(2,1)S(1)}, u32[]{:S(2)}, u32[]{:S(2)}) %collective-permute-start.18) | collective-permute-done | bytes 131104 | tf_op jit(solution)/shard_map/ppermute | solution.py:685
  70.5 1.3 %collective-permute-done.17 = bf16[128,512]{1,0:T(8,128)(2,1)S(1)} collective-permute-done((bf16[128,512]{1,0:T(8,128)(2,1)S(1)}, bf16[128,512]{1,0:T(8,128)(2,1)S(1)}, u32[]{:S(2)}, u32[]{:S(2)}) %collective-permute-start.17) | collective-permute-done | bytes 131104 | tf_op jit(solution)/shard_map/ppermute | solution.py:685
  72.1 1.1 %collective-permute-start.21 = (bf16[128,512]{1,0:T(8,128)(2,1)S(1)}, bf16[128,512]{1,0:T(8,128)(2,1)S(1)}, u32[]{:S(2)}, u32[]{:S(2)}) collective-permute-start(bf16[128,512]{1,0:T(8,128)(2,1)S(1)} %slice.88), channel_id=1, source_target_pairs={{0,4},{2,6},{4,0},{6,2},{8,12},{10,14},{12,8},{14,10},{1,5},{3,7},... | collective-permute-start | bytes 393224 | tf_op jit(solution)/shard_map/ppermute | solution.py:685
  73.2 1.2 %collective-permute-done.15 = bf16[320,128]{1,0:T(8,128)(2,1)S(1)} collective-permute-done((bf16[320,128]{1,0:T(8,128)(2,1)S(1)}, bf16[320,128]{1,0:T(8,128)(2,1)S(1)}, u32[]{:S(2)}, u32[]{:S(2)}) %collective-permute-start.15) | collective-permute-done | bytes 81952 | tf_op jit(solution)/shard_map/ppermute | solution.py:685
  74.5 2.6 %collective-permute-done.21 = bf16[128,512]{1,0:T(8,128)(2,1)S(1)} collective-permute-done((bf16[128,512]{1,0:T(8,128)(2,1)S(1)}, bf16[128,512]{1,0:T(8,128)(2,1)S(1)}, u32[]{:S(2)}, u32[]{:S(2)}) %collective-permute-start.21) | collective-permute-done | bytes 131104 | tf_op jit(solution)/shard_map/ppermute | solution.py:685
  77.2 2.8 %collective-permute-start.22 = (bf16[128,512]{1,0:T(8,128)(2,1)S(1)}, bf16[128,512]{1,0:T(8,128)(2,1)S(1)}, u32[]{:S(2)}, u32[]{:S(2)}) collective-permute-start(bf16[128,512]{1,0:T(8,128)(2,1)S(1)} %pad_maximum_fusion.2), channel_id=1, source_target_pairs={{0,8},{2,10},{4,12},{6,14},{8,0},{10,2},{12,4},{14,6},{1,9},{3,11}... | collective-permute-start | bytes 393224 | tf_op jit(solution)/shard_map/ppermute | solution.py:685
  80.0 3.5 %final.1 = (bf16[512,1024]{1,0:T(8,128)(2,1)}, bf16[512,1024]{1,0:T(8,128)(2,1)}, f32[16]{0:T(128)}, f32[9,1024]{1,0:T(8,128)}) custom-call(s32[2]{0:T(128)S(1)} %copy-done.7, f32[16]{0:T(128)S(1)} %copy-done.8, f32[320,128]{1,0:T(8,128)S(1)} %convert_add_fusion.4.own_ref, f32[320,128]{1,0:T(8,128)S(1)} %collective-permute-done.19.far_ref, ...), custom_call_target="tpu_custom_call" | custom-call | bytes 18000000 | tf_op jit(solution)/shard_map/final/pallas_call | solution.py:661
  83.5 0.8 copy-done.6
  84.4 1.4 %content.1 = bf16[512,1024]{1,0:T(8,128)(2,1)} custom-call(bf16[512,1024]{1,0:T(8,128)(2,1)S(1)} %get-tuple-element.80.grad_ref, bf16[1024,256]{1,0:T(8,128)(2,1)S(1)} %get-tuple-element.81.block_ref, f32[9,1024]{1,0:T(8,128)S(1)} %copy-done.6), custom_call_target="tpu_custom_call" | custom-call | bytes 7200000 | tf_op jit(solution)/shard_map/content/pallas_call | solution.py:571
  85.8 0.7 pad_maximum_fusion.1
  (77 shorter events, 3.7 us)
Async XLA Ops:
  0.6 3.8 %copy-start = (bf16[16,32,1024]{2,1,0:T(8,128)(2,1)S(1)}, bf16[16,32,1024]{2,1,0:T(8,128)(2,1)}, u32[]{:S(2)}) copy-start(bf16[16,32,1024]{2,1,0:T(8,128)(2,1)} %u_tail.1) | copy-start | bytes 3145732
  0.6 3.8 %copy-start.1 = (bf16[16,32,1024]{2,1,0:T(8,128)(2,1)S(1)}, bf16[16,32,1024]{2,1,0:T(8,128)(2,1)}, u32[]{:S(2)}) copy-start(bf16[16,32,1024]{2,1,0:T(8,128)(2,1)} %v_tail.1) | copy-start | bytes 3145732
  4.0 3.8 %copy-start.10 = (f32[272,128]{1,0:T(8,128)S(1)}, f32[272,128]{1,0:T(8,128)}, u32[]{:S(2)}) copy-start(f32[272,128]{1,0:T(8,128)} %get-tuple-element.48) | copy-start | bytes 417796
  4.0 3.7 %collective-permute-start.1 = (f32[272,128]{1,0:T(8,128)}, f32[272,128]{1,0:T(8,128)S(1)}, u32[]{:S(2)}, u32[]{:S(2)}) collective-permute-start(f32[272,128]{1,0:T(8,128)} %get-tuple-element.49), channel_id=1, source_target_pairs={{0,1},{1,0},{2,3},{3,2},{4,5},{5,4},{6,7},{7,6},{8,9},{9,8},{10,11... | collective-permute-start | bytes 417800 | tf_op jit(solution)/shard_map/ppermute | solution.py:685
  5.0 16.7 %collective-permute-start.4 = (bf16[3,32,1024]{2,1,0:T(8,128)(2,1)S(1)}, bf16[3,32,1024]{2,1,0:T(8,128)(2,1)S(1)}, u32[]{:S(2)}, u32[]{:S(2)}) collective-permute-start(bf16[3,32,1024]{2,1,0:T(8,128)(2,1)S(1)} %get-tuple-element.50), channel_id=1, source_target_pairs={{0,2},{2,0},{4,6},{6,4},{8,10},{10,8},{12,14},{14,12},{1,3},{3,1},... | collective-permute-start | bytes 589832 | tf_op jit(solution)/shard_map/ppermute | solution.py:685
  7.7 27.0 %copy-start.2 = (bf16[1024,1024]{1,0:T(8,128)(2,1)S(1)}, bf16[1024,1024]{1,0:T(8,128)(2,1)}, u32[]{:S(2)}) copy-start(bf16[1024,1024]{1,0:T(8,128)(2,1)} %proj_ref.3) | copy-start | bytes 6291460
  7.7 26.9 %copy-start.5 = (f32[9,1024]{1,0:T(8,128)S(1)}, f32[9,1024]{1,0:T(8,128)}, u32[]{:S(2)}) copy-start(f32[9,1024]{1,0:T(8,128)} %taps_ref.3) | copy-start | bytes 110596
  7.7 26.9 %copy-start.8 = (f32[16]{0:T(128)S(1)}, f32[16]{0:T(128)}, u32[]{:S(2)}) copy-start(f32[16]{0:T(128)} %sharp_ref.3) | copy-start | bytes 196
  7.8 8.4 %collective-permute-start.2 = (f32[272,128]{1,0:T(8,128)S(1)}, f32[272,128]{1,0:T(8,128)S(1)}, u32[]{:S(2)}, u32[]{:S(2)}) collective-permute-start(f32[272,128]{1,0:T(8,128)S(1)} %add.54), channel_id=1, source_target_pairs={{0,2},{2,0},{4,6},{6,4},{8,10},{10,8},{12,14},{14,12},{1,3},{3,1},... | collective-permute-start | bytes 417800 | tf_op jit(solution)/shard_map/ppermute | solution.py:685
  8.7 25.0 %collective-permute-start = (bf16[32,8,1024]{2,1,0:T(8,128)(2,1)S(1)}, bf16[32,8,1024]{2,1,0:T(8,128)(2,1)S(1)}, u32[]{:S(2)}, u32[]{:S(2)}) collective-permute-start(bf16[32,8,1024]{2,1,0:T(8,128)(2,1)S(1)} %pad_maximum_fusion), channel_id=1, source_target_pairs={{0,1},{1,0},{2,3},{3,2},{4,5},{5,4},{6,7},{7,6},{8,9},{9,8},{10,11... | collective-permute-start | bytes 1572872 | tf_op jit(solution)/shard_map/ppermute | solution.py:685
  16.2 5.5 %collective-permute-start.3 = (f32[272,128]{1,0:T(8,128)S(1)}, f32[272,128]{1,0:T(8,128)S(1)}, u32[]{:S(2)}, u32[]{:S(2)}) collective-permute-start(f32[272,128]{1,0:T(8,128)S(1)} %add.55), channel_id=1, source_target_pairs={{0,4},{2,6},{4,0},{6,2},{8,12},{10,14},{12,8},{14,10},{1,5},{3,7},... | collective-permute-start | bytes 417800 | tf_op jit(solution)/shard_map/ppermute | solution.py:685
  18.1 14.9 %collective-permute-start.6 = (bf16[3,32,1024]{2,1,0:T(8,128)(2,1)S(1)}, bf16[3,32,1024]{2,1,0:T(8,128)(2,1)S(1)}, u32[]{:S(2)}, u32[]{:S(2)}) collective-permute-start(bf16[3,32,1024]{2,1,0:T(8,128)(2,1)S(1)} %get-tuple-element.53), channel_id=1, source_target_pairs={{2,4},{6,8},{10,12},{4,2},{8,6},{12,10},{3,5},{7,9},{11,13},{5,3},... | collective-permute-start | bytes 589832 | tf_op jit(solution)/shard_map/ppermute | solution.py:762
  21.8 11.2 %collective-permute-start.5 = (f32[272,128]{1,0:T(8,128)S(1)}, f32[272,128]{1,0:T(8,128)S(1)}, u32[]{:S(2)}, u32[]{:S(2)}) collective-permute-start(f32[272,128]{1,0:T(8,128)S(1)} %add.56), channel_id=1, source_target_pairs={{0,8},{2,10},{4,12},{6,14},{8,0},{10,2},{12,4},{14,6},{1,9},{3,11}... | collective-permute-start | bytes 417800 | tf_op jit(solution)/shard_map/ppermute | solution.py:685
  33.0 1.6 %collective-permute-start.8 = (f32[272,128]{1,0:T(8,128)S(1)}, f32[272,128]{1,0:T(8,128)S(1)}, u32[]{:S(2)}, u32[]{:S(2)}) collective-permute-start(f32[272,128]{1,0:T(8,128)S(1)} %add.57.own_ref.energy_own_ref), channel_id=1, source_target_pairs={{0,1},{1,0},{2,3},{3,2},{4,5},{5,4},{6,7},{7,6},{8,9},{9,8},{10,11... | collective-permute-start | bytes 417800 | tf_op jit(solution)/shard_map/ppermute | solution.py:685
  33.1 1.5 %collective-permute-start.7 = (bf16[6,8,1024]{2,1,0:T(8,128)(2,1)S(1)}, bf16[6,8,1024]{2,1,0:T(8,128)(2,1)S(1)}, u32[]{:S(2)}, u32[]{:S(2)}) collective-permute-start(bf16[6,8,1024]{2,1,0:T(8,128)(2,1)S(1)} %fusion.2), channel_id=1, source_target_pairs={{0,1},{1,0},{2,3},{3,2},{4,5},{5,4},{6,7},{7,6},{8,9},{9,8},{10,11... | collective-permute-start | bytes 294920 | tf_op jit(solution)/shard_map/ppermute | solution.py:685
  42.9 8.9 %collective-permute-start.9 = (bf16[256,512]{1,0:T(8,128)(2,1)S(1)}, bf16[256,512]{1,0:T(8,128)(2,1)S(1)}, u32[]{:S(2)}, u32[]{:S(2)}) collective-permute-start(bf16[256,512]{1,0:T(8,128)(2,1)S(1)} %get-tuple-element.93), channel_id=1, source_target_pairs={{0,2},{2,0},{4,6},{6,4},{8,10},{10,8},{12,14},{14,12},{1,3},{3,1},... | collective-permute-start | bytes 786440 | tf_op jit(solution)/shard_map/ppermute | solution.py:685
  51.8 2.1 %collective-permute-start.10 = (bf16[320,128]{1,0:T(8,128)(2,1)S(1)}, bf16[320,128]{1,0:T(8,128)(2,1)S(1)}, u32[]{:S(2)}, u32[]{:S(2)}) collective-permute-start(bf16[320,128]{1,0:T(8,128)(2,1)S(1)} %get-tuple-element.65), channel_id=1, source_target_pairs={{0,1},{1,0},{2,3},{3,2},{4,5},{5,4},{6,7},{7,6},{8,9},{9,8},{10,11... | collective-permute-start | bytes 245768 | tf_op jit(solution)/shard_map/ppermute | solution.py:685
  52.2 8.6 %collective-permute-start.14 = (bf16[256,512]{1,0:T(8,128)(2,1)S(1)}, bf16[256,512]{1,0:T(8,128)(2,1)S(1)}, u32[]{:S(2)}, u32[]{:S(2)}) collective-permute-start(bf16[256,512]{1,0:T(8,128)(2,1)S(1)} %get-tuple-element.92), channel_id=1, source_target_pairs={{0,2},{2,0},{4,6},{6,4},{8,10},{10,8},{12,14},{14,12},{1,3},{3,1},... | collective-permute-start | bytes 786440 | tf_op jit(solution)/shard_map/ppermute | solution.py:685
  55.2 5.8 %collective-permute-start.12 = (bf16[512,512]{1,0:T(8,128)(2,1)S(1)}, bf16[512,512]{1,0:T(8,128)(2,1)S(1)}, u32[]{:S(2)}, u32[]{:S(2)}) collective-permute-start(bf16[512,512]{1,0:T(8,128)(2,1)S(1)} %get-tuple-element.68), channel_id=1, source_target_pairs={{0,1},{1,0},{2,3},{3,2},{4,5},{5,4},{6,7},{7,6},{8,9},{9,8},{10,11... | collective-permute-start | bytes 1572872 | tf_op jit(solution)/shard_map/ppermute | solution.py:685
  55.4 5.5 %collective-permute-start.11 = (bf16[320,128]{1,0:T(8,128)(2,1)S(1)}, bf16[320,128]{1,0:T(8,128)(2,1)S(1)}, u32[]{:S(2)}, u32[]{:S(2)}) collective-permute-start(bf16[320,128]{1,0:T(8,128)(2,1)S(1)} %add_convert_fusion), channel_id=1, source_target_pairs={{0,4},{2,6},{4,0},{6,2},{8,12},{10,14},{12,8},{14,10},{1,5},{3,7},... | collective-permute-start | bytes 245768 | tf_op jit(solution)/shard_map/ppermute | solution.py:685
  61.2 5.5 %collective-permute-start.13 = (bf16[320,128]{1,0:T(8,128)(2,1)S(1)}, bf16[320,128]{1,0:T(8,128)(2,1)S(1)}, u32[]{:S(2)}, u32[]{:S(2)}) collective-permute-start(bf16[320,128]{1,0:T(8,128)(2,1)S(1)} %convert_add_fusion.6), channel_id=1, source_target_pairs={{0,2},{2,0},{4,6},{6,4},{8,10},{10,8},{12,14},{14,12},{1,3},{3,1},... | collective-permute-start | bytes 245768 | tf_op jit(solution)/shard_map/ppermute | solution.py:685
  63.1 6.2 %collective-permute-start.16 = (bf16[128,512]{1,0:T(8,128)(2,1)S(1)}, bf16[128,512]{1,0:T(8,128)(2,1)S(1)}, u32[]{:S(2)}, u32[]{:S(2)}) collective-permute-start(bf16[128,512]{1,0:T(8,128)(2,1)S(1)} %get-tuple-element.89), channel_id=1, source_target_pairs={{0,4},{2,6},{4,0},{6,2},{8,12},{10,14},{12,8},{14,10},{1,5},{3,7},... | collective-permute-start | bytes 393224 | tf_op jit(solution)/shard_map/ppermute | solution.py:685
  63.2 7.4 %collective-permute-start.18 = (bf16[128,512]{1,0:T(8,128)(2,1)S(1)}, bf16[128,512]{1,0:T(8,128)(2,1)S(1)}, u32[]{:S(2)}, u32[]{:S(2)}) collective-permute-start(bf16[128,512]{1,0:T(8,128)(2,1)S(1)} %get-tuple-element.90), channel_id=1, source_target_pairs={{0,6},{2,4},{4,2},{6,0},{8,14},{10,12},{12,10},{14,8},{1,7},{3,5},... | collective-permute-start | bytes 393224 | tf_op jit(solution)/shard_map/ppermute | solution.py:685
  64.9 7.0 %collective-permute-start.17 = (bf16[128,512]{1,0:T(8,128)(2,1)S(1)}, bf16[128,512]{1,0:T(8,128)(2,1)S(1)}, u32[]{:S(2)}, u32[]{:S(2)}) collective-permute-start(bf16[128,512]{1,0:T(8,128)(2,1)S(1)} %get-tuple-element.91), channel_id=1, source_target_pairs={{0,2},{2,0},{4,6},{6,4},{8,10},{10,8},{12,14},{14,12},{1,3},{3,1},... | collective-permute-start | bytes 393224 | tf_op jit(solution)/shard_map/ppermute | solution.py:685
  66.7 13.3 %copy-start.3 = (bf16[16,32,1024]{2,1,0:T(8,128)(2,1)S(1)}, bf16[16,32,1024]{2,1,0:T(8,128)(2,1)}, u32[]{:S(2)}) copy-start(bf16[16,32,1024]{2,1,0:T(8,128)(2,1)} %param.7) | copy-start | bytes 3145732
  66.7 13.3 %copy-start.4 = (bf16[16,32,1024]{2,1,0:T(8,128)(2,1)S(1)}, bf16[16,32,1024]{2,1,0:T(8,128)(2,1)}, u32[]{:S(2)}) copy-start(bf16[16,32,1024]{2,1,0:T(8,128)(2,1)} %param.8) | copy-start | bytes 3145732
  66.7 5.2 %collective-permute-start.20 = (bf16[256,512]{1,0:T(8,128)(2,1)S(1)}, bf16[256,512]{1,0:T(8,128)(2,1)S(1)}, u32[]{:S(2)}, u32[]{:S(2)}) collective-permute-start(bf16[256,512]{1,0:T(8,128)(2,1)S(1)} %slice.87), channel_id=1, source_target_pairs={{0,1},{1,0},{2,3},{3,2},{4,5},{5,4},{6,7},{7,6},{8,9},{9,8},{10,11... | collective-permute-start | bytes 786440 | tf_op jit(solution)/shard_map/ppermute | solution.py:685
  66.8 7.6 %collective-permute-start.15 = (bf16[320,128]{1,0:T(8,128)(2,1)S(1)}, bf16[320,128]{1,0:T(8,128)(2,1)S(1)}, u32[]{:S(2)}, u32[]{:S(2)}) collective-permute-start(bf16[320,128]{1,0:T(8,128)(2,1)S(1)} %convert_add_fusion.5), channel_id=1, source_target_pairs={{0,8},{2,10},{4,12},{6,14},{8,0},{10,2},{12,4},{14,6},{1,9},{3,11}... | collective-permute-start | bytes 245768 | tf_op jit(solution)/shard_map/ppermute | solution.py:685
  71.9 11.6 %copy-start.9 = (f32[128,512]{1,0:T(8,128)}, f32[128,512]{1,0:T(8,128)S(1)}, u32[]{:S(2)}) copy-start(f32[128,512]{1,0:T(8,128)S(1)} %convert_add_fusion.3) | copy-start | bytes 786436
  72.1 5.1 %collective-permute-start.21 = (bf16[128,512]{1,0:T(8,128)(2,1)S(1)}, bf16[128,512]{1,0:T(8,128)(2,1)S(1)}, u32[]{:S(2)}, u32[]{:S(2)}) collective-permute-start(bf16[128,512]{1,0:T(8,128)(2,1)S(1)} %slice.88), channel_id=1, source_target_pairs={{0,4},{2,6},{4,0},{6,2},{8,12},{10,14},{12,8},{14,10},{1,5},{3,7},... | collective-permute-start | bytes 393224 | tf_op jit(solution)/shard_map/ppermute | solution.py:685
  74.4 5.5 %collective-permute-start.19 = (f32[320,128]{1,0:T(8,128)S(1)}, f32[320,128]{1,0:T(8,128)S(1)}, u32[]{:S(2)}, u32[]{:S(2)}) collective-permute-start(f32[320,128]{1,0:T(8,128)S(1)} %convert_add_fusion.4.own_ref), channel_id=1, source_target_pairs={{0,1},{1,0},{2,3},{3,2},{4,5},{5,4},{6,7},{7,6},{8,9},{9,8},{10,11... | collective-permute-start | bytes 491528 | tf_op jit(solution)/shard_map/ppermute | solution.py:685
  77.2 8.6 %collective-permute-start.22 = (bf16[128,512]{1,0:T(8,128)(2,1)S(1)}, bf16[128,512]{1,0:T(8,128)(2,1)S(1)}, u32[]{:S(2)}, u32[]{:S(2)}) collective-permute-start(bf16[128,512]{1,0:T(8,128)(2,1)S(1)} %pad_maximum_fusion.2), channel_id=1, source_target_pairs={{0,8},{2,10},{4,12},{6,14},{8,0},{10,2},{12,4},{14,6},{1,9},{3,11}... | collective-permute-start | bytes 393224 | tf_op jit(solution)/shard_map/ppermute | solution.py:685
  (3 other events, 5.5 us)

commit v3 on v2

--- a/solution.py
+++ b/solution.py
@@ -240,17 +240,15 @@
 
 
 def stencil_chunk(
-    step, tile, col_ref, u_ref, side_ref, twin_ref, next_ref, corner_ref, mixed_all, proj, taps_ref,
+    step, tile, col_ref, u_ref, side_ref, twin_ref, next_ref, corner_ref, taps_ref,
     merged_ref, target_ref, tapsum_ref, field_ref, slope_ref, projected_ref, upside_ref,
-    first_channel,
+    first_channel, beside,
 ):
     tile_rows, tile_cols = tile
     tokens = tile_rows * tile_cols
     ring = tile_cols + RIM
     side = tile_rows * RIM
-    chunk = pl.ds(pl.multiple_of(first_channel + step * GROUP, GROUP), GROUP)
-    here = pl.ds(pl.multiple_of(step * GROUP, GROUP), GROUP)
-    projected_ref[...] = dot_nn(mixed_all[...], proj[:, chunk])
+    chunk = pl.ds(first_channel + step * GROUP, GROUP)
     for at, size, ref, start in (
         (0, side, side_ref, side),
         (side, tile_cols, twin_ref, 2 * tile_cols),
@@ -269,6 +267,7 @@
         taps = [taps_ref[pl.ds(t, 1), glob] for t in range(9)]
         rim = tokens + side
         from_next = 1 - lax.rem(col_ref[1], 2)
+        beside(part)
 
         def ring_row(r):
             if 0 <= r < tile_rows:
@@ -320,7 +319,7 @@
             slope_ref[r + 1] = (up_row(r) * slope).astype(bf16).astype(f32)
             if 0 <= r < tile_rows:
                 at = pl.ds(r * tile_cols, tile_cols)
-                merged_ref[at, lanes] = (projected_ref[at, lanes] + active[:tile_cols]).astype(bf16)
+                merged_ref[at, away] = (projected_ref[at, lanes] + active[:tile_cols]).astype(bf16)
         weights = [jnp.zeros((8, LANES), f32) for _ in range(9)]
         blank = jnp.zeros((RIM, LANES), f32)
         for r in range(tile_rows):
@@ -373,99 +372,112 @@
     col_ref, sharp_ref, own_ref, far_ref, v_ref, u_ref, side_ref, twin_ref, next_ref,
     corner_ref, proj_ref, taps_ref,
     merged_ref, attn_ref, gram_ref, scale_ref, block_ref, mixed_all, target_ref, tapsum_ref,
-    mine_ref, other_ref,
-    field_ref, slope_ref, projected_ref, upside_ref,
+    mine_ref, other_ref, carry_ref,
+    field_ref, slope_ref, upside_ref, *projected,
 ):
-    step = pl.program_id(0)
     tile_rows, tile_cols = tile
     tokens, width = v_ref.shape
     side = tile_rows * RIM
     two = 2 * tile_cols
 
-    @pl.when(step == 0)
-    def _():
-        tapsum_ref[...] = jnp.zeros(tapsum_ref.shape, f32)
-        attention_phase(
-            head_size, col_ref, sharp_ref, own_ref, far_ref, attn_ref, gram_ref, scale_ref, block_ref
+    tapsum_ref[...] = jnp.zeros(tapsum_ref.shape, f32)
+    attention_phase(
+        head_size, col_ref, sharp_ref, own_ref, far_ref, attn_ref, gram_ref, scale_ref, block_ref
+    )
+    for g in range(width // GROUP):
+        at = pl.ds(g * GROUP, GROUP)
+        weights = block_ref[at, :]
+        mixed_all[pl.ds(0, tokens), at] = dot_nt(v_ref[:, at], weights).astype(bf16)
+        around = [(side_ref, side), (twin_ref, two), (next_ref, two), (corner_ref, 4 * RIM)]
+        value = dot_nt(
+            jnp.concatenate([ref[pl.ds(0, size), at] for ref, size in around], axis=0), weights
         )
-        for g in range(width // GROUP):
-            at = pl.ds(g * GROUP, GROUP)
-            weights = block_ref[at, :]
-            mixed_all[pl.ds(0, tokens), at] = dot_nt(v_ref[:, at], weights).astype(bf16)
-            around = [(side_ref, side), (twin_ref, two), (next_ref, two), (corner_ref, 4 * RIM)]
-            value = dot_nt(
-                jnp.concatenate([ref[pl.ds(0, size), at] for ref, size in around], axis=0), weights
-            )
-            start = 0
-            for ref, size in around:
-                piece = value[start : start + size]
-                if ref is side_ref or ref is corner_ref:
-                    piece = piece * keep_side(col_ref, piece.shape)
-                mixed_all[pl.ds(tokens + start, size), at] = piece.astype(bf16)
-                start += size
-
-    stencil_chunk(
-        step, tile, col_ref, u_ref, side_ref, twin_ref, next_ref, corner_ref, mixed_all, proj_ref,
-        taps_ref, merged_ref, target_ref, tapsum_ref, field_ref, slope_ref, projected_ref, upside_ref, 0,
-    )
-
-    @pl.when(step == pl.num_programs(0) - 1)
-    def _():
-        spread_product(piece_rows, cols, order, col_ref, mixed_all, target_ref, mine_ref, other_ref)
+        start = 0
+        for ref, size in around:
+            piece = value[start : start + size]
+            if ref is side_ref or ref is corner_ref:
+                piece = piece * keep_side(col_ref, piece.shape)
+            mixed_all[pl.ds(tokens + start, size), at] = piece.astype(bf16)
+            start += size
+
+    steps = target_ref.shape[1] // GROUP
+    projected[0][...] = dot_nn(mixed_all[...], proj_ref[:, pl.ds(0, GROUP)])
+    for step in range(steps):
+        into = carry_ref if step == steps - 1 else projected[(step + 1) % 2]
+        stencil_chunk(
+            step, tile, col_ref, u_ref, side_ref, twin_ref, next_ref, corner_ref, taps_ref,
+            merged_ref, target_ref, tapsum_ref, field_ref, slope_ref, projected[step % 2], upside_ref, 0,
+            functools.partial(project_part, mixed_all, proj_ref, into, (step + 1) * GROUP),
+        )
+    spread_product(piece_rows, cols, order, col_ref, mixed_all, target_ref, mine_ref, other_ref)
+
+
+def project_part(mixed_all, proj_ref, into_ref, channel, part):
+    rows = mixed_all.shape[0] // (GROUP // LANES)
+    at = pl.ds(pl.multiple_of(part * rows, 16), rows)
+    into_ref[at, :] = dot_nn(mixed_all[at, :], proj_ref[:, pl.ds(channel, GROUP)])
 
 
 def back_kernel(
     head_size, tile, first_channel,
     col_ref, u_ref, v_ref, side_ref, twin_ref, next_ref, corner_ref, mixed_all, proj_ref, taps_ref,
-    front_target, front_taps, merged_before,
+    front_target, front_taps, carry_ref,
     merged_ref, target_ref, grad_ref, mine_ref, other_ref,
-    field_ref, slope_ref, projected_ref, upside_ref, tapsum_ref, whole_ref,
+    field_ref, slope_ref, upside_ref, projected_a, projected_b, tapsum_ref, partial_ref,
 ):
-    step = pl.program_id(0)
-    last = pl.num_programs(0) - 1
     tokens, width = v_ref.shape
     blocks = width // LANES
     half_blocks = blocks // 2
-
-    @pl.when(step == 0)
-    def _():
-        tapsum_ref[...] = jnp.zeros(tapsum_ref.shape, f32)
-
-    stencil_chunk(
-        step, tile, col_ref, u_ref, side_ref, twin_ref, next_ref, corner_ref, mixed_all, proj_ref,
-        taps_ref, merged_ref, target_ref, tapsum_ref, field_ref, slope_ref, projected_ref, upside_ref,
-        first_channel,
-    )
-
-    @pl.when(step == last)
-    def _():
-        whole_ref[:, pl.ds(0, first_channel)] = front_target[...]
-        whole_ref[:, pl.ds(first_channel, width - first_channel)] = target_ref[...]
-        grad_ref[...] = dot_nt(whole_ref[...], proj_ref[...]).astype(bf16)
-        for g in range(width // GROUP):
-            at = pl.ds(g * GROUP, GROUP)
-            square = dot_tn(grad_ref[:, at], v_ref[:, at])
-            for p in range(GROUP // LANES):
-                cut = slice(p * LANES, (p + 1) * LANES)
-                block = g * (GROUP // LANES) + p
-                h, inner = divmod(block, half_blocks)
-                packed_rows = pack_diagonal(square[cut, cut], head_size)
-                if block * LANES < first_channel:
-                    tap_rows = front_taps[:, pl.ds(block * LANES, LANES)]
-                else:
-                    tap_rows = tapsum_ref[:, pl.ds(block * LANES - first_channel, LANES)]
-
-                def put(ref, inner=inner, packed_rows=packed_rows, tap_rows=tap_rows):
-                    ref[pl.ds(inner * head_size, head_size), :] = packed_rows.astype(ref.dtype)
-                    ref[pl.ds(half_blocks * head_size + inner * 16, 16), :] = tap_rows.astype(ref.dtype)
-
-                @pl.when(col_ref[0] == h)
-                def _():
-                    put(mine_ref)
-
-                @pl.when(col_ref[0] != h)
-                def _():
-                    put(other_ref)
+    span = width - first_channel
+    tapsum_ref[...] = jnp.zeros(tapsum_ref.shape, f32)
+
+    def grad_part(part):
+        rows = width // (GROUP // LANES)
+        at = pl.ds(pl.multiple_of(part * rows, LANES), rows)
+        partial_ref[:, at] = dot_nt(front_target[...], proj_ref[at, pl.ds(0, first_channel)])
+
+    steps = span // GROUP
+    source = carry_ref
+    for step in range(steps):
+        into = (projected_a, projected_b)[step % 2]
+        if step == steps - 1:
+            beside = grad_part
+        else:
+            beside = functools.partial(
+                project_part, mixed_all, proj_ref, into, first_channel + (step + 1) * GROUP
+            )
+        stencil_chunk(
+            step, tile, col_ref, u_ref, side_ref, twin_ref, next_ref, corner_ref, taps_ref,
+            merged_ref, target_ref, tapsum_ref, field_ref, slope_ref, source, upside_ref, first_channel, beside,
+        )
+        source = into
+    grad_ref[...] = (
+        partial_ref[...] + dot_nt(target_ref[...], proj_ref[:, pl.ds(first_channel, span)])
+    ).astype(bf16)
+    for g in range(width // GROUP):
+        at = pl.ds(g * GROUP, GROUP)
+        square = dot_tn(grad_ref[:, at], v_ref[:, at])
+        for p in range(GROUP // LANES):
+            cut = slice(p * LANES, (p + 1) * LANES)
+            block = g * (GROUP // LANES) + p
+            h, inner = divmod(block, half_blocks)
+            packed_rows = pack_diagonal(square[cut, cut], head_size)
+            if block * LANES < first_channel:
+                tap_rows = front_taps[:, pl.ds(block * LANES, LANES)]
+            else:
+                tap_rows = tapsum_ref[:, pl.ds(block * LANES - first_channel, LANES)]
+
+            def put(ref, inner=inner, packed_rows=packed_rows, tap_rows=tap_rows):
+                ref[pl.ds(inner * head_size, head_size), :] = packed_rows.astype(ref.dtype)
+                ref[pl.ds(half_blocks * head_size + inner * 16, 16), :] = tap_rows.astype(ref.dtype)
+
+            @pl.when(col_ref[0] == h)
+            def _():
+                put(mine_ref)
+
+            @pl.when(col_ref[0] != h)
+            def _():
+                put(other_ref)
 
 
 def stencil_scratch(tile):
@@ -473,8 +485,9 @@
     return [
         pltpu.VMEM((tile[0] + 4, ring, LANES), f32),
         pltpu.VMEM((tile[0] + 2, ring, LANES), f32),
+        pltpu.VMEM(((tile[0] + 2) * ring, GROUP), f32),
         pltpu.VMEM(((tile[0] + 4) * ring, GROUP), f32),
-        pltpu.VMEM(((tile[0] + 2) * ring, GROUP), f32),
+        pltpu.VMEM(((tile[0] + 4) * ring, GROUP), f32),
     ]
 
 
@@ -485,7 +498,7 @@
     grams = width // LANES * head_size
     sds = jax.ShapeDtypeStruct
     outs = [
-        sds((tokens, width), bf16),
+        sds((tokens, span), bf16),
         sds((grams, LANES), f32),
         sds((grams, LANES), f32),
         sds((grams, LANES), f32),
@@ -495,13 +508,13 @@
         sds((16, span), f32),
         sds((width // 2, span), f32),
         sds((width // 2, span), bf16),
+        sds(((tile[0] + 4) * ring, GROUP), f32),
     ]
     args = (col, sharp, own, far, v, u, *halo, proj, taps)
     return pl.pallas_call(
         functools.partial(front_kernel, head_size, tile, piece_rows, cols, order),
-        grid=(span // GROUP,),
         in_specs=[SCALAR] * 2 + [LOCAL] * (len(args) - 2),
-        out_specs=[pl.BlockSpec((tokens, GROUP), lambda i: (0, i))] + [LOCAL] * (len(outs) - 1),
+        out_specs=[LOCAL] * len(outs),
         out_shape=outs,
         scratch_shapes=stencil_scratch(tile),
         compiler_params=params(),
@@ -510,29 +523,26 @@
     )(*args)
 
 
-def back_call(col, u, v, halo, mixed_all, proj, taps, target, tapsum, merged, tile, head_size):
+def back_call(col, u, v, halo, mixed_all, proj, taps, target, tapsum, carry, tile, head_size):
     tokens, width = v.shape
     span = width // 2
     lines = width // LANES // 2 * (head_size + 16)
     sds = jax.ShapeDtypeStruct
     outs = [
-        sds((tokens, width), bf16),
+        sds((tokens, span), bf16),
         sds((tokens, span), bf16),
         sds((tokens, width), bf16),
         sds((lines, LANES), f32),
         sds((lines, LANES), bf16),
     ]
-    args = (col, u, v, *halo, mixed_all, proj, taps, target, tapsum, merged)
-    first = span // GROUP
+    args = (col, u, v, *halo, mixed_all, proj, taps, target, tapsum, carry)
     return pl.pallas_call(
         functools.partial(back_kernel, head_size, tile, span),
-        grid=(span // GROUP,),
-        in_specs=[SCALAR] + [LOCAL] * (len(args) - 2) + [pl.BlockSpec(memory_space=pl.ANY)],
-        out_specs=[pl.BlockSpec((tokens, GROUP), lambda i: (0, i + first))] + [LOCAL] * (len(outs) - 1),
+        in_specs=[SCALAR] + [LOCAL] * (len(args) - 1),
+        out_specs=[LOCAL] * len(outs),
         out_shape=outs,
-        input_output_aliases={len(args) - 1: 0},
         scratch_shapes=stencil_scratch(tile)
-        + [pltpu.VMEM((16, span), f32), pltpu.VMEM((tokens, width), bf16)],
+        + [pltpu.VMEM((16, span), f32), pltpu.VMEM((tokens, width), f32)],
         compiler_params=params(),
         cost_estimate=cost(10),
         name="back",
@@ -559,25 +569,35 @@
     )(here, mixed_all, target, after)
 
 
-def content_kernel(grad_ref, block_ref, after_ref, out_ref):
+def content_kernel(grad_ref, block_ref, merged_front, merged_back, after_ref, out_ref, merged_ref):
     span = out_ref.shape[1]
     for g in range(span // GROUP):
         at = pl.ds(pl.multiple_of(pl.program_id(0) * span + g * GROUP, GROUP), GROUP)
         out_ref[:, pl.ds(g * GROUP, GROUP)] = dot_nn(grad_ref[:, at], block_ref[at, :]).astype(bf16)
 
-
-def content_call(grad, block, after):
+    @pl.when(pl.program_id(0) == 0)
+    def _():
+        merged_ref[...] = merged_front[...]
+
+    @pl.when(pl.program_id(0) != 0)
+    def _():
+        merged_ref[...] = merged_back[...]
+
+
+def content_call(grad, block, merged_front, merged_back, after):
     tokens, width = grad.shape
+    half = pl.BlockSpec((tokens, width // 2), lambda i: (0, i))
+    out = jax.ShapeDtypeStruct((tokens, width), bf16)
     return pl.pallas_call(
         content_kernel,
         grid=(2,),
-        in_specs=[LOCAL] * 2 + [pl.BlockSpec(memory_space=pl.ANY)],
-        out_specs=pl.BlockSpec((tokens, width // 2), lambda i: (0, i)),
-        out_shape=jax.ShapeDtypeStruct((tokens, width), bf16),
+        in_specs=[LOCAL] * 4 + [pl.BlockSpec(memory_space=pl.ANY)],
+        out_specs=[half, half],
+        out_shape=[out, out],
         compiler_params=params(),
         cost_estimate=cost(2),
         name="content",
-    )(grad, block, after)
+    )(grad, block, merged_front, merged_back, after)
 
 
 def final_kernel(
@@ -599,27 +619,27 @@
     taps_ref,
     mixer_ref,
 ):
-    step = pl.program_id(0)
-    steps = pl.num_programs(0)
+    half = pl.program_id(0)
+    groups = dq_ref.shape[1] // GROUP
     packed = LANES // head_size
     per = GROUP // LANES
-    half_blocks = steps * per // 2
-    mine = (step // (steps // 2)) == col_ref[0]
+    half_blocks = groups * per
+    mine = half == col_ref[0]
     owner = lane_head(head_size)
     row = lax.broadcasted_iota(jnp.int32, (head_size, LANES), 0)
     lane = lax.broadcasted_iota(jnp.int32, (head_size, LANES), 1)
     mixer_ref[...] = jnp.zeros(mixer_ref.shape, bf16)
     q_terms, k_terms = [], []
-    for p in range(per):
-        block = step * per + p
-        inner = lax.rem(block, half_blocks)
-
-        def take(own, far, at, size):
-            return jnp.where(mine, own[pl.ds(at, size), :], far[pl.ds(at, size), :])
-
-        grad = take(own_ref, far_ref, pl.multiple_of(inner * head_size, head_size), head_size)
-        taps_ref[:, pl.ds(p * LANES, LANES)] = take(
-            own_ref, far_ref, pl.multiple_of(half_blocks * head_size + inner * 16, 16), 16
+
+    def take(own, far, at, size):
+        return jnp.where(mine, own[pl.ds(at, size), :], far[pl.ds(at, size), :])
+
+    for inner in range(half_blocks):
+        block = half * half_blocks + inner
+        p = inner % per
+        grad = take(own_ref, far_ref, inner * head_size, head_size)
+        taps_ref[:, pl.ds(inner * LANES, LANES)] = take(
+            own_ref, far_ref, half_blocks * head_size + inner * 16, 16
         )[:9]
         q_line = take(energy_own_ref, energy_far_ref, half_blocks * head_size + inner, 1)
         k_line = take(energy_own_ref, energy_far_ref, half_blocks * head_size + 8 + inner, 1)
@@ -643,30 +663,34 @@
         k_terms.append(k_scale * k_scale * k_corr)
         low = (scale * gram_grad).astype(bf16)
         for k in range(packed):
-            mixer_ref[pl.ds(p * LANES + k * head_size, head_size), pl.ds(p * LANES, LANES)] = jnp.where(
+            mixer_ref[pl.ds(inner * LANES + k * head_size, head_size), pl.ds(p * LANES, LANES)] = jnp.where(
                 owner == k, low, jnp.zeros_like(low)
             )
-    here = pl.ds(pl.multiple_of(step * GROUP, GROUP), GROUP)
-    q, k = q_ref[:, here], k_ref[:, here]
-    mixer = mixer_ref[...]
-    dq_ref[...] = (dot_nt(k, mixer) - q.astype(f32) * jnp.concatenate(q_terms, axis=1)).astype(bf16)
-    dk_ref[...] = (dot_nn(q, mixer) - k.astype(f32) * jnp.concatenate(k_terms, axis=1)).astype(bf16)
+    for g in range(groups):
+        here = pl.ds(pl.multiple_of((half * groups + g) * GROUP, GROUP), GROUP)
+        at = pl.ds(g * GROUP, GROUP)
+        q, k = q_ref[:, here], k_ref[:, here]
+        mixer = mixer_ref[at, :]
+        q_term = jnp.concatenate(q_terms[g * per : (g + 1) * per], axis=1)
+        k_term = jnp.concatenate(k_terms[g * per : (g + 1) * per], axis=1)
+        dq_ref[:, at] = (dot_nt(k, mixer) - q.astype(f32) * q_term).astype(bf16)
+        dk_ref[:, at] = (dot_nn(q, mixer) - k.astype(f32) * k_term).astype(bf16)
 
 
 def final_call(col, sharp, own, far, energy_own, energy_far, attn, gram, scale, q, k, head_size):
     tokens, width = q.shape
     sds = jax.ShapeDtypeStruct
-    token_block = pl.BlockSpec((tokens, GROUP), lambda i: (0, i))
+    token_block = pl.BlockSpec((tokens, width // 2), lambda i: (0, i))
     args = (col, sharp, own, far, energy_own, energy_far, attn, gram, scale, q, k)
     return pl.pallas_call(
         functools.partial(final_kernel, head_size),
-        grid=(width // GROUP,),
+        grid=(2,),
         in_specs=[SCALAR, SCALAR] + [LOCAL] * 9,
         out_specs=[
             token_block,
             token_block,
             SCALAR,
-            pl.BlockSpec((9, GROUP), lambda i: (0, i)),
+            pl.BlockSpec((9, width // 2), lambda i: (0, i)),
         ],
         out_shape=[
             sds((tokens, width), bf16),
@@ -674,7 +698,7 @@
             sds(sharp.shape, f32),
             sds((9, width), f32),
         ],
-        scratch_shapes=[pltpu.VMEM((GROUP, GROUP), bf16)],
+        scratch_shapes=[pltpu.VMEM((width // 2, GROUP), bf16)],
         compiler_params=params(),
         cost_estimate=cost(5),
         name="final",
@@ -755,7 +779,7 @@
     side = swap(jnp.concatenate([edge(v), edge(u)]), "col", 1)
     for i, bit in enumerate(bits):
         total = total + swap(total, "row", bit)
-        if i == 1:
+        if i == 2:
             from_twin = swap(to_twin, "row", 1)
             total, from_twin = tie(total, from_twin)
         if i == 2:
@@ -767,14 +791,14 @@
     around = tuple(x.reshape(-1, width) for x in (side, from_twin, from_next, corner))
     energy_own, energy_far = total, swap(total, "col", 1)
 
-    (merged, attn, gram, scale, block, mixed_all, front_target, front_taps, mine, other) = front_call(
+    (merged_front, attn, gram, scale, block, mixed_all, front_target, front_taps, mine, other, carry) = front_call(
         here, sharp, energy_own, energy_far, v2, u2, around, proj, taps, tile, head_size, piece_rows, cols, early
     )
     halves = [swap(x, "row", bits[0]) for x in jnp.split(other, 2)]
     first = halves[:1]
     front_mine = mine
-    merged, target, grad, mine, other = back_call(
-        here, u2, v2, around, mixed_all, proj, taps, front_target, front_taps, merged, tile, head_size
+    merged_back, target, grad, mine, other = back_call(
+        here, u2, v2, around, mixed_all, proj, taps, front_target, front_taps, carry, tile, head_size
     )
 
     mine, other, *first = tie(mine, other, *first)
@@ -803,7 +827,7 @@
     dq, dk, heat, tap_sums = final_call(
         here, sharp, total, far, energy_own, energy_far, attn, gram, scale, q2, k2, head_size
     )
-    content = content_call(grad, block, tap_sums)
+    content, merged = content_call(grad, block, merged_front, merged_back, tap_sums)
     content, *kept = tie(content, *kept)
     front_sum, back_sum = (add_low(x, y) for x, y in zip(kept, jnp.split(got, 2)))
     projector = jnp.concatenate([front_sum, back_sum], axis=1)

time: 86.7 us -> 84.5 us (0.975)
  waiting for transfers between devices: 32.4 us -> 29.4 us
  Pallas kernels: 26.6 us -> 25.2 us
  starting transfers between devices: 23.3 us -> 24.5 us
  other arithmetic: 2.13 us -> 3.04 us
    ppermute x22, waiting for transfers between devices: 32.4 us -> 29.4 us  [swap(): lax.ppermute(x, axis, [(i, i ^ bit) for i in range(lax.axis_size(axis))])]
    pallas_call x3, Pallas kernels: 13.8 us -> 12.5 us  [the longest x1 8.13 us: back_call(): pl.pallas_call(functools.partial(back_kernel, head_size, tile, span), in_...]
    ppermute x22, starting transfers between devices: 22.6 us -> 23.8 us  [swap(): lax.ppermute(x, axis, [(i, i ^ bit) for i in range(lax.axis_size(axis))])]
    add x7, other arithmetic: 0.54 us -> 1.45 us  [add_low(): return total + got.astype(f32)]
  transfers between devices with their start and end apart: 23 -> 23, of which waited for: 10 -> 12; matrix products, arithmetic and copies ran while one was open for 1% -> 1% of each run, Pallas kernels for 18% -> 17%
where the time goes in v3:
time: 84.5 us; the launch traced here: 84.3 us
  waiting for transfers between devices  29.4 us (35%)
  Pallas kernels  25.2 us (30%)
  starting transfers between devices  24.5 us (29%)
  other arithmetic  3.04 us (4%)
  local copies, waits for them, and re-layouts  1.11 us (1%)
  between operations  1.05 us (1%)
    ppermute x22, waiting for transfers between devices, swap(): lax.ppermute(x, axis, [(i, i ^ bit) for i in range(lax.axis_size(axis))])  29.4 us
    ppermute x22, starting transfers between devices, swap(): lax.ppermute(x, axis, [(i, i ^ bit) for i in range(lax.axis_size(axis))])  23.8 us
    pallas_call x1, Pallas kernels, back_call(): pl.pallas_call(functools.partial(back_kernel, head_size, tile, span), in_...  8.13 us
    pallas_call x1, Pallas kernels, front_call(): pl.pallas_call(functools.partial(front_kernel, head_size, tile, piece_row...  8.06 us
    pallas_call x1, Pallas kernels, final_call(): pl.pallas_call(functools.partial(final_kernel, head_size), grid=(2,), in_...  2.76 us
    pallas_call x1, Pallas kernels, gram_call(): pl.pallas_call(functools.partial(gram_kernel, head_size), grid=(2,), in_s...  2.74 us
  transfers between devices with their start and end apart: 23, of which 12 were waited for; matrix products, arithmetic and copies ran while one was open for 1% of the time, Pallas kernels for 17%

profile of v3, /device:TPU:0, one launch (start us, length us, event | category | flops | bytes accessed | tf_op | source)
XLA Modules:
  0.0 84.3 jit_solution(5869557511904240346)
XLA Ops:
  0.7 0.6 pad_add_fusion.col_ref.here_ref
  1.2 2.7 %gram.1 = (f32[272,128]{1,0:T(8,128)}, f32[272,128]{1,0:T(8,128)}) custom-call(s32[2]{0:T(128)} %pad_add_fusion.col_ref.here_ref, bf16[512,1024]{1,0:T(8,128)(2,1)} %bitcast.18, bf16[512,1024]{1,0:T(8,128)(2,1)} %bitcast.20), custom_call_target="tpu_custom_call" | custom-call | bytes 9000000 | tf_op jit(solution)/shard_map/gram/pallas_call | solution.py:154
  4.5 1.2 %collective-permute-done.1 = f32[272,128]{1,0:T(8,128)S(1)} collective-permute-done((f32[272,128]{1,0:T(8,128)}, f32[272,128]{1,0:T(8,128)S(1)}, u32[]{:S(2)}, u32[]{:S(2)}) %collective-permute-start.1) | collective-permute-done | bytes 139296 | tf_op jit(solution)/shard_map/ppermute | solution.py:709
  5.6 0.9 %add.54 = f32[272,128]{1,0:T(8,128)S(1)} add(f32[272,128]{1,0:T(8,128)} %get-tuple-element.51, f32[272,128]{1,0:T(8,128)S(1)} %collective-permute-done.1) | non-fusion elementwise | flops 34816 | bytes 417792 | tf_op jit(solution)/shard_map/add | solution.py:726
  6.6 2.9 %collective-permute-start.2 = (f32[272,128]{1,0:T(8,128)S(1)}, f32[272,128]{1,0:T(8,128)S(1)}, u32[]{:S(2)}, u32[]{:S(2)}) collective-permute-start(f32[272,128]{1,0:T(8,128)S(1)} %add.54), channel_id=1, source_target_pairs={{0,2},{2,0},{4,6},{6,4},{8,10},{10,8},{12,14},{14,12},{1,3},{3,1},... | collective-permute-start | bytes 417800 | tf_op jit(solution)/shard_map/ppermute | solution.py:709
  9.6 3.9 %collective-permute-done.2 = f32[272,128]{1,0:T(8,128)S(1)} collective-permute-done((f32[272,128]{1,0:T(8,128)S(1)}, f32[272,128]{1,0:T(8,128)S(1)}, u32[]{:S(2)}, u32[]{:S(2)}) %collective-permute-start.2) | collective-permute-done | bytes 139296 | tf_op jit(solution)/shard_map/ppermute | solution.py:709
  13.5 1.9 %collective-permute-start.3 = (f32[272,128]{1,0:T(8,128)S(1)}, f32[272,128]{1,0:T(8,128)S(1)}, u32[]{:S(2)}, u32[]{:S(2)}) collective-permute-start(f32[272,128]{1,0:T(8,128)S(1)} %add.55), channel_id=1, source_target_pairs={{0,4},{2,6},{4,0},{6,2},{8,12},{10,14},{12,8},{14,10},{1,5},{3,7},... | collective-permute-start | bytes 417800 | tf_op jit(solution)/shard_map/ppermute | solution.py:709
  16.0 1.6 %collective-permute-start.5 = (bf16[3,32,1024]{2,1,0:T(8,128)(2,1)S(1)}, bf16[3,32,1024]{2,1,0:T(8,128)(2,1)S(1)}, u32[]{:S(2)}, u32[]{:S(2)}) collective-permute-start(bf16[3,32,1024]{2,1,0:T(8,128)(2,1)S(1)} %get-tuple-element.53), channel_id=1, source_target_pairs={{0,2},{2,0},{4,6},{6,4},{8,10},{10,8},{12,14},{14,12},{1,3},{3,1},... | collective-permute-start | bytes 589832 | tf_op jit(solution)/shard_map/ppermute | solution.py:709
  17.6 0.7 collective-permute-start.6
  18.8 3.4 %collective-permute-start.4 = (f32[272,128]{1,0:T(8,128)S(1)}, f32[272,128]{1,0:T(8,128)S(1)}, u32[]{:S(2)}, u32[]{:S(2)}) collective-permute-start(f32[272,128]{1,0:T(8,128)S(1)} %add.56), channel_id=1, source_target_pairs={{0,8},{2,10},{4,12},{6,14},{8,0},{10,2},{12,4},{14,6},{1,9},{3,11}... | collective-permute-start | bytes 417800 | tf_op jit(solution)/shard_map/ppermute | solution.py:709
  22.2 9.7 %collective-permute-done.4 = f32[272,128]{1,0:T(8,128)S(1)} collective-permute-done((f32[272,128]{1,0:T(8,128)S(1)}, f32[272,128]{1,0:T(8,128)S(1)}, u32[]{:S(2)}, u32[]{:S(2)}) %collective-permute-start.4) | collective-permute-done | bytes 139296 | tf_op jit(solution)/shard_map/ppermute | solution.py:709
  32.6 0.9 %collective-permute-done.7 = bf16[6,8,1024]{2,1,0:T(8,128)(2,1)S(1)} collective-permute-done((bf16[6,8,1024]{2,1,0:T(8,128)(2,1)S(1)}, bf16[6,8,1024]{2,1,0:T(8,128)(2,1)S(1)}, u32[]{:S(2)}, u32[]{:S(2)}) %collective-permute-start.7) | collective-permute-done | bytes 98336 | tf_op jit(solution)/shard_map/ppermute | solution.py:709
  33.6 8.1 %front.1 = (bf16[512,512]{1,0:T(8,128)(2,1)S(1)}, f32[512,128]{1,0:T(8,128)S(1)}, f32[512,128]{1,0:T(8,128)S(1)}, f32[512,128]{1,0:T(8,128)S(1)}, bf16[1024,256]...) custom-call(s32[2]{0:T(128)S(1)} %copy-done.7, ...), custom_call_target="tpu_custom_call" | custom-call | bytes 36000000 | tf_op jit(solution)/shard_map/front/pallas_call | solution.py:514
  41.8 8.1 %back.1 = (bf16[512,512]{1,0:T(8,128)(2,1)S(1)}, bf16[512,512]{1,0:T(8,128)(2,1)S(1)}, bf16[512,1024]{1,0:T(8,128)(2,1)S(1)}, f32[320,128]{1,0:T(8,128)S(1)}, bf16[320,128]{1,0:T(8,128)(2,1)S(1)}) custom-call(s32[2]{0:T(128)S(1)} %copy-done.7, bf16[512,1024]{1,0:T(8,128)(2,1)S(1)} %bitcast.15, bf16[512,1024]{1,0:T(8,128)(2,1)S(1)} %bitcast.17, ...), custom_call_target="tpu_custom_call" | custom-call | bytes 36000000 | tf_op jit(solution)/shard_map/back/pallas_call | solution.py:539
  50.4 1.7 %collective-permute-start.14 = (bf16[256,512]{1,0:T(8,128)(2,1)S(1)}, bf16[256,512]{1,0:T(8,128)(2,1)S(1)}, u32[]{:S(2)}, u32[]{:S(2)}) collective-permute-start(bf16[256,512]{1,0:T(8,128)(2,1)S(1)} %get-tuple-element.98), channel_id=1, source_target_pairs={{0,2},{2,0},{4,6},{6,4},{8,10},{10,8},{12,14},{14,12},{1,3},{3,1},... | collective-permute-start | bytes 786440 | tf_op jit(solution)/shard_map/ppermute | solution.py:709
  52.1 1.3 %projector.1 = (f32[512,512]{1,0:T(8,128)S(1)}, bf16[512,512]{1,0:T(8,128)(2,1)S(1)}) custom-call(s32[2]{0:T(128)S(1)} %copy-done.7, bf16[800,1024]{1,0:T(8,128)(2,1)S(1)} %get-tuple-element.59.mixed_all, bf16[512,512]{1,0:T(8,128)(2,1)S(1)} %get-tuple-element.72.target_ref, bf16[320,128]{1,0:T(8,128)(2,1)S(1)} %collective-permute-done.10.after_ref), custom_call_target="tpu_custom_call" | custom-call | bytes 7200000 | tf_op jit(solution)/shard_map/projector/pallas_call | solution.py:561
  54.2 4.9 %collective-permute-done.14 = bf16[256,512]{1,0:T(8,128)(2,1)S(1)} collective-permute-done((bf16[256,512]{1,0:T(8,128)(2,1)S(1)}, bf16[256,512]{1,0:T(8,128)(2,1)S(1)}, u32[]{:S(2)}, u32[]{:S(2)}) %collective-permute-start.14) | collective-permute-done | bytes 262176 | tf_op jit(solution)/shard_map/ppermute | solution.py:709
  59.5 1.7 %collective-permute-start.13 = (bf16[320,128]{1,0:T(8,128)(2,1)S(1)}, bf16[320,128]{1,0:T(8,128)(2,1)S(1)}, u32[]{:S(2)}, u32[]{:S(2)}) collective-permute-start(bf16[320,128]{1,0:T(8,128)(2,1)S(1)} %convert_add_fusion.6), channel_id=1, source_target_pairs={{0,2},{2,0},{4,6},{6,4},{8,10},{10,8},{12,14},{14,12},{1,3},{3,1},... | collective-permute-start | bytes 245768 | tf_op jit(solution)/shard_map/ppermute | solution.py:709
  61.4 1.8 %collective-permute-start.18 = (bf16[128,512]{1,0:T(8,128)(2,1)S(1)}, bf16[128,512]{1,0:T(8,128)(2,1)S(1)}, u32[]{:S(2)}, u32[]{:S(2)}) collective-permute-start(bf16[128,512]{1,0:T(8,128)(2,1)S(1)} %get-tuple-element.96), channel_id=1, source_target_pairs={{0,6},{2,4},{4,2},{6,0},{8,14},{10,12},{12,10},{14,8},{1,7},{3,5},... | collective-permute-start | bytes 393224 | tf_op jit(solution)/shard_map/ppermute | solution.py:709
  63.2 1.7 %collective-permute-start.17 = (bf16[128,512]{1,0:T(8,128)(2,1)S(1)}, bf16[128,512]{1,0:T(8,128)(2,1)S(1)}, u32[]{:S(2)}, u32[]{:S(2)}) collective-permute-start(bf16[128,512]{1,0:T(8,128)(2,1)S(1)} %get-tuple-element.97), channel_id=1, source_target_pairs={{0,2},{2,0},{4,6},{6,4},{8,10},{10,8},{12,14},{14,12},{1,3},{3,1},... | collective-permute-start | bytes 393224 | tf_op jit(solution)/shard_map/ppermute | solution.py:709
  65.0 1.2 %collective-permute-start.15 = (bf16[320,128]{1,0:T(8,128)(2,1)S(1)}, bf16[320,128]{1,0:T(8,128)(2,1)S(1)}, u32[]{:S(2)}, u32[]{:S(2)}) collective-permute-start(bf16[320,128]{1,0:T(8,128)(2,1)S(1)} %convert_add_fusion.5), channel_id=1, source_target_pairs={{0,8},{2,10},{4,12},{6,14},{8,0},{10,2},{12,4},{14,6},{1,9},{3,11}... | collective-permute-start | bytes 245768 | tf_op jit(solution)/shard_map/ppermute | solution.py:709
  66.3 1.3 %collective-permute-done.16 = bf16[128,512]{1,0:T(8,128)(2,1)S(1)} collective-permute-done((bf16[128,512]{1,0:T(8,128)(2,1)S(1)}, bf16[128,512]{1,0:T(8,128)(2,1)S(1)}, u32[]{:S(2)}, u32[]{:S(2)}) %collective-permute-start.16) | collective-permute-done | bytes 131104 | tf_op jit(solution)/shard_map/ppermute | solution.py:709
  67.5 1.3 %collective-permute-done.18 = bf16[128,512]{1,0:T(8,128)(2,1)S(1)} collective-permute-done((bf16[128,512]{1,0:T(8,128)(2,1)S(1)}, bf16[128,512]{1,0:T(8,128)(2,1)S(1)}, u32[]{:S(2)}, u32[]{:S(2)}) %collective-permute-start.18) | collective-permute-done | bytes 131104 | tf_op jit(solution)/shard_map/ppermute | solution.py:709
  68.9 1.3 %collective-permute-done.17 = bf16[128,512]{1,0:T(8,128)(2,1)S(1)} collective-permute-done((bf16[128,512]{1,0:T(8,128)(2,1)S(1)}, bf16[128,512]{1,0:T(8,128)(2,1)S(1)}, u32[]{:S(2)}, u32[]{:S(2)}) %collective-permute-start.17) | collective-permute-done | bytes 131104 | tf_op jit(solution)/shard_map/ppermute | solution.py:709
  70.4 1.0 %collective-permute-start.21 = (bf16[128,512]{1,0:T(8,128)(2,1)S(1)}, bf16[128,512]{1,0:T(8,128)(2,1)S(1)}, u32[]{:S(2)}, u32[]{:S(2)}) collective-permute-start(bf16[128,512]{1,0:T(8,128)(2,1)S(1)} %slice.88), channel_id=1, source_target_pairs={{0,4},{2,6},{4,0},{6,2},{8,12},{10,14},{12,8},{14,10},{1,5},{3,7},... | collective-permute-start | bytes 393224 | tf_op jit(solution)/shard_map/ppermute | solution.py:709
  71.4 1.2 %collective-permute-done.15 = bf16[320,128]{1,0:T(8,128)(2,1)S(1)} collective-permute-done((bf16[320,128]{1,0:T(8,128)(2,1)S(1)}, bf16[320,128]{1,0:T(8,128)(2,1)S(1)}, u32[]{:S(2)}, u32[]{:S(2)}) %collective-permute-start.15) | collective-permute-done | bytes 81952 | tf_op jit(solution)/shard_map/ppermute | solution.py:709
  72.7 2.7 %collective-permute-done.21 = bf16[128,512]{1,0:T(8,128)(2,1)S(1)} collective-permute-done((bf16[128,512]{1,0:T(8,128)(2,1)S(1)}, bf16[128,512]{1,0:T(8,128)(2,1)S(1)}, u32[]{:S(2)}, u32[]{:S(2)}) %collective-permute-start.21) | collective-permute-done | bytes 131104 | tf_op jit(solution)/shard_map/ppermute | solution.py:709
  75.5 2.7 %collective-permute-start.22 = (bf16[128,512]{1,0:T(8,128)(2,1)S(1)}, bf16[128,512]{1,0:T(8,128)(2,1)S(1)}, u32[]{:S(2)}, u32[]{:S(2)}) collective-permute-start(bf16[128,512]{1,0:T(8,128)(2,1)S(1)} %pad_maximum_fusion.2), channel_id=1, source_target_pairs={{0,8},{2,10},{4,12},{6,14},{8,0},{10,2},{12,4},{14,6},{1,9},{3,11}... | collective-permute-start | bytes 393224 | tf_op jit(solution)/shard_map/ppermute | solution.py:709
  78.2 2.8 %final.1 = (bf16[512,1024]{1,0:T(8,128)(2,1)}, bf16[512,1024]{1,0:T(8,128)(2,1)}, f32[16]{0:T(128)}, f32[9,1024]{1,0:T(8,128)}) custom-call(s32[2]{0:T(128)S(1)} %copy-done.7, f32[16]{0:T(128)S(1)} %copy-done.8, f32[320,128]{1,0:T(8,128)S(1)} %convert_add_fusion.4.own_ref, f32[320,128]{1,0:T(8,128)S(1)} %collective-permute-done.19.far_ref, ...), custom_call_target="tpu_custom_call" | custom-call | bytes 18000000 | tf_op jit(solution)/shard_map/final/pallas_call | solution.py:685
  81.0 0.8 copy-done.6
  81.8 1.6 %content.1 = (bf16[512,1024]{1,0:T(8,128)(2,1)}, bf16[512,1024]{1,0:T(8,128)(2,1)}) custom-call(bf16[512,1024]{1,0:T(8,128)(2,1)S(1)} %get-tuple-element.63.grad_ref, bf16[1024,256]{1,0:T(8,128)(2,1)S(1)} %get-tuple-element.64.block_ref, bf16[512,512]{1,0:T(8,128)(2,1)S(1)} %get-tuple-element.65.merged_front, ...), custom_call_target="tpu_custom_call" | custom-call | bytes 7200000 | tf_op jit(solution)/shard_map/content/pallas_call | solution.py:591
  83.5 0.7 pad_maximum_fusion.1
  (75 shorter events, 4.8 us)
Async XLA Ops:
  0.6 3.8 %copy-start = (bf16[16,32,1024]{2,1,0:T(8,128)(2,1)S(1)}, bf16[16,32,1024]{2,1,0:T(8,128)(2,1)}, u32[]{:S(2)}) copy-start(bf16[16,32,1024]{2,1,0:T(8,128)(2,1)} %u_tail.1) | copy-start | bytes 3145732
  0.6 3.8 %copy-start.1 = (bf16[16,32,1024]{2,1,0:T(8,128)(2,1)S(1)}, bf16[16,32,1024]{2,1,0:T(8,128)(2,1)}, u32[]{:S(2)}) copy-start(bf16[16,32,1024]{2,1,0:T(8,128)(2,1)} %v_tail.1) | copy-start | bytes 3145732
  1.2 14.1 %copy-start.7 = (s32[2]{0:T(128)S(1)}, s32[2]{0:T(128)}, u32[]{:S(2)}) copy-start(s32[2]{0:T(128)} %pad_add_fusion.col_ref.here_ref) | copy-start | bytes 28
  4.0 1.7 %collective-permute-start.1 = (f32[272,128]{1,0:T(8,128)}, f32[272,128]{1,0:T(8,128)S(1)}, u32[]{:S(2)}, u32[]{:S(2)}) collective-permute-start(f32[272,128]{1,0:T(8,128)} %get-tuple-element.52), channel_id=1, source_target_pairs={{0,1},{1,0},{2,3},{3,2},{4,5},{5,4},{6,7},{7,6},{8,9},{9,8},{10,11... | collective-permute-start | bytes 417800 | tf_op jit(solution)/shard_map/ppermute | solution.py:709
  6.6 6.9 %collective-permute-start.2 = (f32[272,128]{1,0:T(8,128)S(1)}, f32[272,128]{1,0:T(8,128)S(1)}, u32[]{:S(2)}, u32[]{:S(2)}) collective-permute-start(f32[272,128]{1,0:T(8,128)S(1)} %add.54), channel_id=1, source_target_pairs={{0,2},{2,0},{4,6},{6,4},{8,10},{10,8},{12,14},{14,12},{1,3},{3,1},... | collective-permute-start | bytes 417800 | tf_op jit(solution)/shard_map/ppermute | solution.py:709
  9.6 23.1 %collective-permute-start = (bf16[32,8,1024]{2,1,0:T(8,128)(2,1)S(1)}, bf16[32,8,1024]{2,1,0:T(8,128)(2,1)S(1)}, u32[]{:S(2)}, u32[]{:S(2)}) collective-permute-start(bf16[32,8,1024]{2,1,0:T(8,128)(2,1)S(1)} %pad_maximum_fusion), channel_id=1, source_target_pairs={{0,1},{1,0},{2,3},{3,2},{4,5},{5,4},{6,7},{7,6},{8,9},{9,8},{10,11... | collective-permute-start | bytes 1572872 | tf_op jit(solution)/shard_map/ppermute | solution.py:709
  13.5 5.3 %collective-permute-start.3 = (f32[272,128]{1,0:T(8,128)S(1)}, f32[272,128]{1,0:T(8,128)S(1)}, u32[]{:S(2)}, u32[]{:S(2)}) collective-permute-start(f32[272,128]{1,0:T(8,128)S(1)} %add.55), channel_id=1, source_target_pairs={{0,4},{2,6},{4,0},{6,2},{8,12},{10,14},{12,8},{14,10},{1,5},{3,7},... | collective-permute-start | bytes 417800 | tf_op jit(solution)/shard_map/ppermute | solution.py:709
  15.4 18.2 %copy-start.5 = (f32[9,1024]{1,0:T(8,128)S(1)}, f32[9,1024]{1,0:T(8,128)}, u32[]{:S(2)}) copy-start(f32[9,1024]{1,0:T(8,128)} %taps_ref.3) | copy-start | bytes 110596
  16.0 17.6 %copy-start.2 = (bf16[1024,1024]{1,0:T(8,128)(2,1)S(1)}, bf16[1024,1024]{1,0:T(8,128)(2,1)}, u32[]{:S(2)}) copy-start(bf16[1024,1024]{1,0:T(8,128)(2,1)} %proj_ref.3) | copy-start | bytes 6291460
  16.0 17.6 %copy-start.8 = (f32[16]{0:T(128)S(1)}, f32[16]{0:T(128)}, u32[]{:S(2)}) copy-start(f32[16]{0:T(128)} %sharp_ref.3) | copy-start | bytes 196
  16.0 15.9 %collective-permute-start.5 = (bf16[3,32,1024]{2,1,0:T(8,128)(2,1)S(1)}, bf16[3,32,1024]{2,1,0:T(8,128)(2,1)S(1)}, u32[]{:S(2)}, u32[]{:S(2)}) collective-permute-start(bf16[3,32,1024]{2,1,0:T(8,128)(2,1)S(1)} %get-tuple-element.53), channel_id=1, source_target_pairs={{0,2},{2,0},{4,6},{6,4},{8,10},{10,8},{12,14},{14,12},{1,3},{3,1},... | collective-permute-start | bytes 589832 | tf_op jit(solution)/shard_map/ppermute | solution.py:709
  17.6 14.4 %collective-permute-start.6 = (bf16[3,32,1024]{2,1,0:T(8,128)(2,1)S(1)}, bf16[3,32,1024]{2,1,0:T(8,128)(2,1)S(1)}, u32[]{:S(2)}, u32[]{:S(2)}) collective-permute-start(bf16[3,32,1024]{2,1,0:T(8,128)(2,1)S(1)} %get-tuple-element.56), channel_id=1, source_target_pairs={{2,4},{6,8},{10,12},{4,2},{8,6},{12,10},{3,5},{7,9},{11,13},{5,3},... | collective-permute-start | bytes 589832 | tf_op jit(solution)/shard_map/ppermute | solution.py:786
  18.8 13.1 %collective-permute-start.4 = (f32[272,128]{1,0:T(8,128)S(1)}, f32[272,128]{1,0:T(8,128)S(1)}, u32[]{:S(2)}, u32[]{:S(2)}) collective-permute-start(f32[272,128]{1,0:T(8,128)S(1)} %add.56), channel_id=1, source_target_pairs={{0,8},{2,10},{4,12},{6,14},{8,0},{10,2},{12,4},{14,6},{1,9},{3,11}... | collective-permute-start | bytes 417800 | tf_op jit(solution)/shard_map/ppermute | solution.py:709
  32.0 1.6 %collective-permute-start.8 = (f32[272,128]{1,0:T(8,128)S(1)}, f32[272,128]{1,0:T(8,128)S(1)}, u32[]{:S(2)}, u32[]{:S(2)}) collective-permute-start(f32[272,128]{1,0:T(8,128)S(1)} %add.57.own_ref.energy_own_ref), channel_id=1, source_target_pairs={{0,1},{1,0},{2,3},{3,2},{4,5},{5,4},{6,7},{7,6},{8,9},{9,8},{10,11... | collective-permute-start | bytes 417800 | tf_op jit(solution)/shard_map/ppermute | solution.py:709
  32.1 1.5 %collective-permute-start.7 = (bf16[6,8,1024]{2,1,0:T(8,128)(2,1)S(1)}, bf16[6,8,1024]{2,1,0:T(8,128)(2,1)S(1)}, u32[]{:S(2)}, u32[]{:S(2)}) collective-permute-start(bf16[6,8,1024]{2,1,0:T(8,128)(2,1)S(1)} %fusion.2), channel_id=1, source_target_pairs={{0,1},{1,0},{2,3},{3,2},{4,5},{5,4},{6,7},{7,6},{8,9},{9,8},{10,11... | collective-permute-start | bytes 294920 | tf_op jit(solution)/shard_map/ppermute | solution.py:709
  41.7 8.6 %collective-permute-start.9 = (bf16[256,512]{1,0:T(8,128)(2,1)S(1)}, bf16[256,512]{1,0:T(8,128)(2,1)S(1)}, u32[]{:S(2)}, u32[]{:S(2)}) collective-permute-start(bf16[256,512]{1,0:T(8,128)(2,1)S(1)} %get-tuple-element.99), channel_id=1, source_target_pairs={{0,2},{2,0},{4,6},{6,4},{8,10},{10,8},{12,14},{14,12},{1,3},{3,1},... | collective-permute-start | bytes 786440 | tf_op jit(solution)/shard_map/ppermute | solution.py:709
  50.4 1.7 %collective-permute-start.10 = (bf16[320,128]{1,0:T(8,128)(2,1)S(1)}, bf16[320,128]{1,0:T(8,128)(2,1)S(1)}, u32[]{:S(2)}, u32[]{:S(2)}) collective-permute-start(bf16[320,128]{1,0:T(8,128)(2,1)S(1)} %get-tuple-element.71), channel_id=1, source_target_pairs={{0,1},{1,0},{2,3},{3,2},{4,5},{5,4},{6,7},{7,6},{8,9},{9,8},{10,11... | collective-permute-start | bytes 245768 | tf_op jit(solution)/shard_map/ppermute | solution.py:709
  50.4 8.7 %collective-permute-start.14 = (bf16[256,512]{1,0:T(8,128)(2,1)S(1)}, bf16[256,512]{1,0:T(8,128)(2,1)S(1)}, u32[]{:S(2)}, u32[]{:S(2)}) collective-permute-start(bf16[256,512]{1,0:T(8,128)(2,1)S(1)} %get-tuple-element.98), channel_id=1, source_target_pairs={{0,2},{2,0},{4,6},{6,4},{8,10},{10,8},{12,14},{14,12},{1,3},{3,1},... | collective-permute-start | bytes 786440 | tf_op jit(solution)/shard_map/ppermute | solution.py:709
  53.4 5.9 %collective-permute-start.12 = (bf16[512,512]{1,0:T(8,128)(2,1)S(1)}, bf16[512,512]{1,0:T(8,128)(2,1)S(1)}, u32[]{:S(2)}, u32[]{:S(2)}) collective-permute-start(bf16[512,512]{1,0:T(8,128)(2,1)S(1)} %get-tuple-element.74), channel_id=1, source_target_pairs={{0,1},{1,0},{2,3},{3,2},{4,5},{5,4},{6,7},{7,6},{8,9},{9,8},{10,11... | collective-permute-start | bytes 1572872 | tf_op jit(solution)/shard_map/ppermute | solution.py:709
  53.7 5.6 %collective-permute-start.11 = (bf16[320,128]{1,0:T(8,128)(2,1)S(1)}, bf16[320,128]{1,0:T(8,128)(2,1)S(1)}, u32[]{:S(2)}, u32[]{:S(2)}) collective-permute-start(bf16[320,128]{1,0:T(8,128)(2,1)S(1)} %add_convert_fusion), channel_id=1, source_target_pairs={{0,4},{2,6},{4,0},{6,2},{8,12},{10,14},{12,8},{14,10},{1,5},{3,7},... | collective-permute-start | bytes 245768 | tf_op jit(solution)/shard_map/ppermute | solution.py:709
  59.5 5.4 %collective-permute-start.13 = (bf16[320,128]{1,0:T(8,128)(2,1)S(1)}, bf16[320,128]{1,0:T(8,128)(2,1)S(1)}, u32[]{:S(2)}, u32[]{:S(2)}) collective-permute-start(bf16[320,128]{1,0:T(8,128)(2,1)S(1)} %convert_add_fusion.6), channel_id=1, source_target_pairs={{0,2},{2,0},{4,6},{6,4},{8,10},{10,8},{12,14},{14,12},{1,3},{3,1},... | collective-permute-start | bytes 245768 | tf_op jit(solution)/shard_map/ppermute | solution.py:709
  61.3 6.2 %collective-permute-start.16 = (bf16[128,512]{1,0:T(8,128)(2,1)S(1)}, bf16[128,512]{1,0:T(8,128)(2,1)S(1)}, u32[]{:S(2)}, u32[]{:S(2)}) collective-permute-start(bf16[128,512]{1,0:T(8,128)(2,1)S(1)} %get-tuple-element.95), channel_id=1, source_target_pairs={{0,4},{2,6},{4,0},{6,2},{8,12},{10,14},{12,8},{14,10},{1,5},{3,7},... | collective-permute-start | bytes 393224 | tf_op jit(solution)/shard_map/ppermute | solution.py:709
  61.4 7.5 %collective-permute-start.18 = (bf16[128,512]{1,0:T(8,128)(2,1)S(1)}, bf16[128,512]{1,0:T(8,128)(2,1)S(1)}, u32[]{:S(2)}, u32[]{:S(2)}) collective-permute-start(bf16[128,512]{1,0:T(8,128)(2,1)S(1)} %get-tuple-element.96), channel_id=1, source_target_pairs={{0,6},{2,4},{4,2},{6,0},{8,14},{10,12},{12,10},{14,8},{1,7},{3,5},... | collective-permute-start | bytes 393224 | tf_op jit(solution)/shard_map/ppermute | solution.py:709
  63.2 7.0 %collective-permute-start.17 = (bf16[128,512]{1,0:T(8,128)(2,1)S(1)}, bf16[128,512]{1,0:T(8,128)(2,1)S(1)}, u32[]{:S(2)}, u32[]{:S(2)}) collective-permute-start(bf16[128,512]{1,0:T(8,128)(2,1)S(1)} %get-tuple-element.97), channel_id=1, source_target_pairs={{0,2},{2,0},{4,6},{6,4},{8,10},{10,8},{12,14},{14,12},{1,3},{3,1},... | collective-permute-start | bytes 393224 | tf_op jit(solution)/shard_map/ppermute | solution.py:709
  64.9 13.3 %copy-start.3 = (bf16[16,32,1024]{2,1,0:T(8,128)(2,1)S(1)}, bf16[16,32,1024]{2,1,0:T(8,128)(2,1)}, u32[]{:S(2)}) copy-start(bf16[16,32,1024]{2,1,0:T(8,128)(2,1)} %param.7) | copy-start | bytes 3145732
  64.9 13.3 %copy-start.4 = (bf16[16,32,1024]{2,1,0:T(8,128)(2,1)S(1)}, bf16[16,32,1024]{2,1,0:T(8,128)(2,1)}, u32[]{:S(2)}) copy-start(bf16[16,32,1024]{2,1,0:T(8,128)(2,1)} %param.8) | copy-start | bytes 3145732
  65.0 5.3 %collective-permute-start.20 = (bf16[256,512]{1,0:T(8,128)(2,1)S(1)}, bf16[256,512]{1,0:T(8,128)(2,1)S(1)}, u32[]{:S(2)}, u32[]{:S(2)}) collective-permute-start(bf16[256,512]{1,0:T(8,128)(2,1)S(1)} %slice.87), channel_id=1, source_target_pairs={{0,1},{1,0},{2,3},{3,2},{4,5},{5,4},{6,7},{7,6},{8,9},{9,8},{10,11... | collective-permute-start | bytes 786440 | tf_op jit(solution)/shard_map/ppermute | solution.py:709
  65.0 7.6 %collective-permute-start.15 = (bf16[320,128]{1,0:T(8,128)(2,1)S(1)}, bf16[320,128]{1,0:T(8,128)(2,1)S(1)}, u32[]{:S(2)}, u32[]{:S(2)}) collective-permute-start(bf16[320,128]{1,0:T(8,128)(2,1)S(1)} %convert_add_fusion.5), channel_id=1, source_target_pairs={{0,8},{2,10},{4,12},{6,14},{8,0},{10,2},{12,4},{14,6},{1,9},{3,11}... | collective-permute-start | bytes 245768 | tf_op jit(solution)/shard_map/ppermute | solution.py:709
  70.3 10.7 %copy-start.9 = (f32[128,512]{1,0:T(8,128)}, f32[128,512]{1,0:T(8,128)S(1)}, u32[]{:S(2)}) copy-start(f32[128,512]{1,0:T(8,128)S(1)} %convert_add_fusion.3) | copy-start | bytes 786436
  70.4 5.0 %collective-permute-start.21 = (bf16[128,512]{1,0:T(8,128)(2,1)S(1)}, bf16[128,512]{1,0:T(8,128)(2,1)S(1)}, u32[]{:S(2)}, u32[]{:S(2)}) collective-permute-start(bf16[128,512]{1,0:T(8,128)(2,1)S(1)} %slice.88), channel_id=1, source_target_pairs={{0,4},{2,6},{4,0},{6,2},{8,12},{10,14},{12,8},{14,10},{1,5},{3,7},... | collective-permute-start | bytes 393224 | tf_op jit(solution)/shard_map/ppermute | solution.py:709
  72.6 5.6 %collective-permute-start.19 = (f32[320,128]{1,0:T(8,128)S(1)}, f32[320,128]{1,0:T(8,128)S(1)}, u32[]{:S(2)}, u32[]{:S(2)}) collective-permute-start(f32[320,128]{1,0:T(8,128)S(1)} %convert_add_fusion.4.own_ref), channel_id=1, source_target_pairs={{0,1},{1,0},{2,3},{3,2},{4,5},{5,4},{6,7},{7,6},{8,9},{9,8},{10,11... | collective-permute-start | bytes 491528 | tf_op jit(solution)/shard_map/ppermute | solution.py:709
  75.5 8.0 %collective-permute-start.22 = (bf16[128,512]{1,0:T(8,128)(2,1)S(1)}, bf16[128,512]{1,0:T(8,128)(2,1)S(1)}, u32[]{:S(2)}, u32[]{:S(2)}) collective-permute-start(bf16[128,512]{1,0:T(8,128)(2,1)S(1)} %pad_maximum_fusion.2), channel_id=1, source_target_pairs={{0,8},{2,10},{4,12},{6,14},{8,0},{10,2},{12,4},{14,6},{1,9},{3,11}... | collective-permute-start | bytes 393224 | tf_op jit(solution)/shard_map/ppermute | solution.py:709
  (2 other events, 2.5 us)

commit v4 on v3

--- a/solution.py
+++ b/solution.py
@@ -113,7 +113,7 @@
     )(here, v, v, u, u)
 
 
-def gram_kernel(head_size, col_ref, q_ref, k_ref, mine_ref, other_ref):
+def gram_kernel(head_size, q_ref, k_ref, mine_ref, other_ref):
     half = pl.program_id(0)
     per = GROUP // LANES
     energy = mine_ref.shape[0] - 16
@@ -138,16 +138,18 @@
         mine_ref[pl.ds(energy, 16), :] = jnp.zeros((16, LANES), f32)
         other_ref[pl.ds(energy, 16), :] = jnp.zeros((16, LANES), f32)
 
-    @pl.when(half == col_ref[0])
+    col = lax.axis_index("col")
+
+    @pl.when(half == col)
     def _():
         put(mine_ref)
 
-    @pl.when(half != col_ref[0])
+    @pl.when(half != col)
     def _():
         put(other_ref)
 
 
-def gram_call(col, q, k, head_size):
+def gram_call(q, k, head_size):
     tokens, width = q.shape
     lines = width // 2 // LANES * head_size + 16
     out = jax.ShapeDtypeStruct((lines, LANES), f32)
@@ -155,16 +157,15 @@
         functools.partial(gram_kernel, head_size),
         grid=(2,),
         in_specs=[
-            SCALAR,
             pl.BlockSpec((tokens, width // 2), lambda i: (0, i)),
             pl.BlockSpec((tokens, width // 2), lambda i: (0, i)),
         ],
         out_specs=[LOCAL, LOCAL],
         out_shape=[out, out],
-        compiler_params=params(60 * 1024 * 1024),
+        compiler_params=params(48 * 1024 * 1024),
         cost_estimate=cost(2.5),
         name="gram",
-    )(col, q, k)
+    )(q, k)
 
 
 def gelu_terms(u):
@@ -769,7 +770,7 @@
     late = [("col", 1)] + [("row", bit) for bit in bits]
     piece_rows = width // (rows * cols)
 
-    mine, other = gram_call(here, q2, k2, head_size)
+    mine, other = gram_call(q2, k2, head_size)
     to_twin, to_next = edges_call(here, v, u)
     total = add_low(mine, swap(other, "col", 1))
     start = jnp.where(lax.axis_index("col") == 0, v.shape[1] - RIM, 0)

time: 84.5 us -> 83.7 us (level)
  local copies, waits for them, and re-layouts: 1.11 us -> 3.7 us
  Pallas kernels: 25.2 us -> 23.4 us
  other arithmetic: 3.04 us -> 1.63 us
    unnamed x20 -> x22, local copies, waits for them, and re-layouts: 0.88 us -> 3.47 us
    pallas_call x1, Pallas kernels: 2.74 us -> 0.94 us  [gram_call(): pl.pallas_call(functools.partial(gram_kernel, head_size), grid=(2,), in_s...]
    add x7, other arithmetic: 1.45 us -> 0.53 us  [add_low(): return total + got.astype(f32)]
where the time goes in v4:
time: 83.7 us; the launch traced here: 83.5 us
  waiting for transfers between devices  29 us (35%)
  starting transfers between devices  24.7 us (30%)
  Pallas kernels  23.4 us (28%)
  local copies, waits for them, and re-layouts  3.7 us (4%)
  other arithmetic  1.63 us (2%)
  between operations  1.07 us (1%)
    ppermute x22, waiting for transfers between devices, swap(): lax.ppermute(x, axis, [(i, i ^ bit) for i in range(lax.axis_size(axis))])  29 us
    ppermute x22, starting transfers between devices, swap(): lax.ppermute(x, axis, [(i, i ^ bit) for i in range(lax.axis_size(axis))])  24 us
    pallas_call x1, Pallas kernels, back_call(): pl.pallas_call(functools.partial(back_kernel, head_size, tile, span), in_...  8.13 us
    pallas_call x1, Pallas kernels, front_call(): pl.pallas_call(functools.partial(front_kernel, head_size, tile, piece_row...  8.07 us
    unnamed x22, local copies, waits for them, and re-layouts  3.47 us
    pallas_call x1, Pallas kernels, final_call(): pl.pallas_call(functools.partial(final_kernel, head_size), grid=(2,), in_...  2.76 us
  transfers between devices with their start and end apart: 23, of which 12 were waited for; matrix products, arithmetic and copies ran while one was open for 1% of the time, Pallas kernels for 17%

profile of v4, /device:TPU:0, one launch (start us, length us, event | category | flops | bytes accessed | tf_op | source)
XLA Modules:
  0.0 83.5 jit_solution(16501901372135413482)
XLA Ops:
  0.7 1.4 %copy-done.3 = bf16[16,32,1024]{2,1,0:T(8,128)(2,1)S(1)} copy-done((bf16[16,32,1024]{2,1,0:T(8,128)(2,1)S(1)}, bf16[16,32,1024]{2,1,0:T(8,128)(2,1)}, u32[]{:S(2)}) %copy-start.3) | copy-done | bytes 1048600
  2.0 1.2 %copy-done.5 = bf16[16,32,1024]{2,1,0:T(8,128)(2,1)S(1)} copy-done((bf16[16,32,1024]{2,1,0:T(8,128)(2,1)S(1)}, bf16[16,32,1024]{2,1,0:T(8,128)(2,1)}, u32[]{:S(2)}) %copy-start.5) | copy-done | bytes 1048600
  3.3 0.9 %gram.1 = (f32[272,128]{1,0:T(8,128)S(1)}, f32[272,128]{1,0:T(8,128)S(1)}) custom-call(bf16[512,1024]{1,0:T(8,128)(2,1)S(1)} %bitcast.18, bf16[512,1024]{1,0:T(8,128)(2,1)S(1)} %bitcast.20), custom_call_target="tpu_custom_call" | custom-call | bytes 9000000 | tf_op jit(solution)/shard_map/gram/pallas_call | solution.py:156
  4.7 1.0 %collective-permute-done.1 = f32[272,128]{1,0:T(8,128)S(1)} collective-permute-done((f32[272,128]{1,0:T(8,128)S(1)}, f32[272,128]{1,0:T(8,128)S(1)}, u32[]{:S(2)}, u32[]{:S(2)}) %collective-permute-start.1) | collective-permute-done | bytes 139296 | tf_op jit(solution)/shard_map/ppermute | solution.py:710
  5.7 2.9 %collective-permute-start.2 = (f32[272,128]{1,0:T(8,128)S(1)}, f32[272,128]{1,0:T(8,128)S(1)}, u32[]{:S(2)}, u32[]{:S(2)}) collective-permute-start(f32[272,128]{1,0:T(8,128)S(1)} %add.54), channel_id=1, source_target_pairs={{0,2},{2,0},{4,6},{6,4},{8,10},{10,8},{12,14},{14,12},{1,3},{3,1},... | collective-permute-start | bytes 417800 | tf_op jit(solution)/shard_map/ppermute | solution.py:710
  8.9 3.8 %collective-permute-done.2 = f32[272,128]{1,0:T(8,128)S(1)} collective-permute-done((f32[272,128]{1,0:T(8,128)S(1)}, f32[272,128]{1,0:T(8,128)S(1)}, u32[]{:S(2)}, u32[]{:S(2)}) %collective-permute-start.2) | collective-permute-done | bytes 139296 | tf_op jit(solution)/shard_map/ppermute | solution.py:710
  12.7 1.9 %collective-permute-start.3 = (f32[272,128]{1,0:T(8,128)S(1)}, f32[272,128]{1,0:T(8,128)S(1)}, u32[]{:S(2)}, u32[]{:S(2)}) collective-permute-start(f32[272,128]{1,0:T(8,128)S(1)} %add.55), channel_id=1, source_target_pairs={{0,4},{2,6},{4,0},{6,2},{8,12},{10,14},{12,8},{14,10},{1,5},{3,7},... | collective-permute-start | bytes 417800 | tf_op jit(solution)/shard_map/ppermute | solution.py:710
  15.2 1.6 %collective-permute-start.5 = (bf16[3,32,1024]{2,1,0:T(8,128)(2,1)S(1)}, bf16[3,32,1024]{2,1,0:T(8,128)(2,1)S(1)}, u32[]{:S(2)}, u32[]{:S(2)}) collective-permute-start(bf16[3,32,1024]{2,1,0:T(8,128)(2,1)S(1)} %get-tuple-element.53), channel_id=1, source_target_pairs={{0,2},{2,0},{4,6},{6,4},{8,10},{10,8},{12,14},{14,12},{1,3},{3,1},... | collective-permute-start | bytes 589832 | tf_op jit(solution)/shard_map/ppermute | solution.py:710
  16.8 0.7 collective-permute-start.6
  18.0 3.4 %collective-permute-start.4 = (f32[272,128]{1,0:T(8,128)S(1)}, f32[272,128]{1,0:T(8,128)S(1)}, u32[]{:S(2)}, u32[]{:S(2)}) collective-permute-start(f32[272,128]{1,0:T(8,128)S(1)} %add.56), channel_id=1, source_target_pairs={{0,8},{2,10},{4,12},{6,14},{8,0},{10,2},{12,4},{14,6},{1,9},{3,11}... | collective-permute-start | bytes 417800 | tf_op jit(solution)/shard_map/ppermute | solution.py:710
  21.4 9.7 %collective-permute-done.4 = f32[272,128]{1,0:T(8,128)S(1)} collective-permute-done((f32[272,128]{1,0:T(8,128)S(1)}, f32[272,128]{1,0:T(8,128)S(1)}, u32[]{:S(2)}, u32[]{:S(2)}) %collective-permute-start.4) | collective-permute-done | bytes 139296 | tf_op jit(solution)/shard_map/ppermute | solution.py:710
  31.9 0.9 %collective-permute-done.7 = bf16[6,8,1024]{2,1,0:T(8,128)(2,1)S(1)} collective-permute-done((bf16[6,8,1024]{2,1,0:T(8,128)(2,1)S(1)}, bf16[6,8,1024]{2,1,0:T(8,128)(2,1)S(1)}, u32[]{:S(2)}, u32[]{:S(2)}) %collective-permute-start.7) | collective-permute-done | bytes 98336 | tf_op jit(solution)/shard_map/ppermute | solution.py:710
  32.8 8.1 %front.1 = (bf16[512,512]{1,0:T(8,128)(2,1)S(1)}, f32[512,128]{1,0:T(8,128)S(1)}, f32[512,128]{1,0:T(8,128)S(1)}, f32[512,128]{1,0:T(8,128)S(1)}, bf16[1024,256]...) custom-call(s32[2]{0:T(128)S(1)} %pad_add_fusion.here_ref.col_ref, ...), custom_call_target="tpu_custom_call" | custom-call | bytes 36000000 | tf_op jit(solution)/shard_map/front/pallas_call | solution.py:515
  41.0 8.1 %back.1 = (bf16[512,512]{1,0:T(8,128)(2,1)S(1)}, bf16[512,512]{1,0:T(8,128)(2,1)S(1)}, bf16[512,1024]{1,0:T(8,128)(2,1)S(1)}, f32[320,128]{1,0:T(8,128)S(1)}, bf16[320,128]{1,0:T(8,128)(2,1)S(1)}) custom-call(s32[2]{0:T(128)S(1)} %pad_add_fusion.here_ref.col_ref, bf16[512,1024]{1,0:T(8,128)(2,1)S(1)} %bitcast.15, bf16[512,1024]{1,0:T(8,128)(2,1)S(1)} %bitcast.17, ...), custom_call_target="tpu_custom_call" | custom-call | bytes 36000000 | tf_op jit(solution)/shard_map/back/pallas_call | solution.py:540
  49.6 1.7 %collective-permute-start.14 = (bf16[256,512]{1,0:T(8,128)(2,1)S(1)}, bf16[256,512]{1,0:T(8,128)(2,1)S(1)}, u32[]{:S(2)}, u32[]{:S(2)}) collective-permute-start(bf16[256,512]{1,0:T(8,128)(2,1)S(1)} %get-tuple-element.98), channel_id=1, source_target_pairs={{0,2},{2,0},{4,6},{6,4},{8,10},{10,8},{12,14},{14,12},{1,3},{3,1},... | collective-permute-start | bytes 786440 | tf_op jit(solution)/shard_map/ppermute | solution.py:710
  51.3 1.3 %projector.1 = (f32[512,512]{1,0:T(8,128)S(1)}, bf16[512,512]{1,0:T(8,128)(2,1)S(1)}) custom-call(s32[2]{0:T(128)S(1)} %pad_add_fusion.here_ref.col_ref, bf16[800,1024]{1,0:T(8,128)(2,1)S(1)} %get-tuple-element.59.mixed_all, bf16[512,512]{1,0:T(8,128)(2,1)S(1)} %get-tuple-element.72.target_ref, bf16[320,128]{1,0:T(8,128)(2,1)S(1)} %collective-permute-done.10.after_ref), custom_call_target="tpu_custom_call" | custom-call | bytes 7200000 | tf_op jit(solution)/shard_map/projector/pallas_call | solution.py:562
  53.4 4.9 %collective-permute-done.14 = bf16[256,512]{1,0:T(8,128)(2,1)S(1)} collective-permute-done((bf16[256,512]{1,0:T(8,128)(2,1)S(1)}, bf16[256,512]{1,0:T(8,128)(2,1)S(1)}, u32[]{:S(2)}, u32[]{:S(2)}) %collective-permute-start.14) | collective-permute-done | bytes 262176 | tf_op jit(solution)/shard_map/ppermute | solution.py:710
  58.7 1.8 %collective-permute-start.13 = (bf16[320,128]{1,0:T(8,128)(2,1)S(1)}, bf16[320,128]{1,0:T(8,128)(2,1)S(1)}, u32[]{:S(2)}, u32[]{:S(2)}) collective-permute-start(bf16[320,128]{1,0:T(8,128)(2,1)S(1)} %convert_add_fusion.6), channel_id=1, source_target_pairs={{0,2},{2,0},{4,6},{6,4},{8,10},{10,8},{12,14},{14,12},{1,3},{3,1},... | collective-permute-start | bytes 245768 | tf_op jit(solution)/shard_map/ppermute | solution.py:710
  60.6 1.8 %collective-permute-start.18 = (bf16[128,512]{1,0:T(8,128)(2,1)S(1)}, bf16[128,512]{1,0:T(8,128)(2,1)S(1)}, u32[]{:S(2)}, u32[]{:S(2)}) collective-permute-start(bf16[128,512]{1,0:T(8,128)(2,1)S(1)} %get-tuple-element.96), channel_id=1, source_target_pairs={{0,6},{2,4},{4,2},{6,0},{8,14},{10,12},{12,10},{14,8},{1,7},{3,5},... | collective-permute-start | bytes 393224 | tf_op jit(solution)/shard_map/ppermute | solution.py:710
  62.4 1.7 %collective-permute-start.17 = (bf16[128,512]{1,0:T(8,128)(2,1)S(1)}, bf16[128,512]{1,0:T(8,128)(2,1)S(1)}, u32[]{:S(2)}, u32[]{:S(2)}) collective-permute-start(bf16[128,512]{1,0:T(8,128)(2,1)S(1)} %get-tuple-element.97), channel_id=1, source_target_pairs={{0,2},{2,0},{4,6},{6,4},{8,10},{10,8},{12,14},{14,12},{1,3},{3,1},... | collective-permute-start | bytes 393224 | tf_op jit(solution)/shard_map/ppermute | solution.py:710
  64.3 1.2 %collective-permute-start.15 = (bf16[320,128]{1,0:T(8,128)(2,1)S(1)}, bf16[320,128]{1,0:T(8,128)(2,1)S(1)}, u32[]{:S(2)}, u32[]{:S(2)}) collective-permute-start(bf16[320,128]{1,0:T(8,128)(2,1)S(1)} %convert_add_fusion.5), channel_id=1, source_target_pairs={{0,8},{2,10},{4,12},{6,14},{8,0},{10,2},{12,4},{14,6},{1,9},{3,11}... | collective-permute-start | bytes 245768 | tf_op jit(solution)/shard_map/ppermute | solution.py:710
  65.5 1.3 %collective-permute-done.16 = bf16[128,512]{1,0:T(8,128)(2,1)S(1)} collective-permute-done((bf16[128,512]{1,0:T(8,128)(2,1)S(1)}, bf16[128,512]{1,0:T(8,128)(2,1)S(1)}, u32[]{:S(2)}, u32[]{:S(2)}) %collective-permute-start.16) | collective-permute-done | bytes 131104 | tf_op jit(solution)/shard_map/ppermute | solution.py:710
  66.8 1.3 %collective-permute-done.18 = bf16[128,512]{1,0:T(8,128)(2,1)S(1)} collective-permute-done((bf16[128,512]{1,0:T(8,128)(2,1)S(1)}, bf16[128,512]{1,0:T(8,128)(2,1)S(1)}, u32[]{:S(2)}, u32[]{:S(2)}) %collective-permute-start.18) | collective-permute-done | bytes 131104 | tf_op jit(solution)/shard_map/ppermute | solution.py:710
  68.1 1.3 %collective-permute-done.17 = bf16[128,512]{1,0:T(8,128)(2,1)S(1)} collective-permute-done((bf16[128,512]{1,0:T(8,128)(2,1)S(1)}, bf16[128,512]{1,0:T(8,128)(2,1)S(1)}, u32[]{:S(2)}, u32[]{:S(2)}) %collective-permute-start.17) | collective-permute-done | bytes 131104 | tf_op jit(solution)/shard_map/ppermute | solution.py:710
  69.6 1.0 %collective-permute-start.21 = (bf16[128,512]{1,0:T(8,128)(2,1)S(1)}, bf16[128,512]{1,0:T(8,128)(2,1)S(1)}, u32[]{:S(2)}, u32[]{:S(2)}) collective-permute-start(bf16[128,512]{1,0:T(8,128)(2,1)S(1)} %slice.88), channel_id=1, source_target_pairs={{0,4},{2,6},{4,0},{6,2},{8,12},{10,14},{12,8},{14,10},{1,5},{3,7},... | collective-permute-start | bytes 393224 | tf_op jit(solution)/shard_map/ppermute | solution.py:710
  70.7 1.2 %collective-permute-done.15 = bf16[320,128]{1,0:T(8,128)(2,1)S(1)} collective-permute-done((bf16[320,128]{1,0:T(8,128)(2,1)S(1)}, bf16[320,128]{1,0:T(8,128)(2,1)S(1)}, u32[]{:S(2)}, u32[]{:S(2)}) %collective-permute-start.15) | collective-permute-done | bytes 81952 | tf_op jit(solution)/shard_map/ppermute | solution.py:710
  72.0 2.7 %collective-permute-done.21 = bf16[128,512]{1,0:T(8,128)(2,1)S(1)} collective-permute-done((bf16[128,512]{1,0:T(8,128)(2,1)S(1)}, bf16[128,512]{1,0:T(8,128)(2,1)S(1)}, u32[]{:S(2)}, u32[]{:S(2)}) %collective-permute-start.21) | collective-permute-done | bytes 131104 | tf_op jit(solution)/shard_map/ppermute | solution.py:710
  74.7 2.7 %collective-permute-start.22 = (bf16[128,512]{1,0:T(8,128)(2,1)S(1)}, bf16[128,512]{1,0:T(8,128)(2,1)S(1)}, u32[]{:S(2)}, u32[]{:S(2)}) collective-permute-start(bf16[128,512]{1,0:T(8,128)(2,1)S(1)} %pad_maximum_fusion.2), channel_id=1, source_target_pairs={{0,8},{2,10},{4,12},{6,14},{8,0},{10,2},{12,4},{14,6},{1,9},{3,11}... | collective-permute-start | bytes 393224 | tf_op jit(solution)/shard_map/ppermute | solution.py:710
  77.5 2.8 %final.1 = (bf16[512,1024]{1,0:T(8,128)(2,1)}, bf16[512,1024]{1,0:T(8,128)(2,1)}, f32[16]{0:T(128)}, f32[9,1024]{1,0:T(8,128)}) custom-call(s32[2]{0:T(128)S(1)} %pad_add_fusion.here_ref.col_ref, f32[16]{0:T(128)S(1)} %copy-done.9, f32[320,128]{1,0:T(8,128)S(1)} %convert_add_fusion.4.own_ref, f32[320,128]{1,0:T(8,128)S(1)} %collective-permute-done.19.far_ref, ...), custom_call_target="tpu_custom_call" | custom-call | bytes 18000000 | tf_op jit(solution)/shard_map/final/pallas_call | solution.py:686
  80.2 0.8 %copy-done.8 = f32[9,1024]{1,0:T(8,128)S(1)} copy-done((f32[9,1024]{1,0:T(8,128)S(1)}, f32[9,1024]{1,0:T(8,128)}, u32[]{:S(2)}) %copy-start.8) | copy-done | bytes 36888
  81.1 1.6 %content.1 = (bf16[512,1024]{1,0:T(8,128)(2,1)}, bf16[512,1024]{1,0:T(8,128)(2,1)}) custom-call(bf16[512,1024]{1,0:T(8,128)(2,1)S(1)} %get-tuple-element.63.grad_ref, bf16[1024,256]{1,0:T(8,128)(2,1)S(1)} %get-tuple-element.64.block_ref, bf16[512,512]{1,0:T(8,128)(2,1)S(1)} %get-tuple-element.65.merged_front, ...), custom_call_target="tpu_custom_call" | custom-call | bytes 7200000 | tf_op jit(solution)/shard_map/content/pallas_call | solution.py:592
  82.8 0.7 pad_maximum_fusion.1
  (77 shorter events, 4.9 us)
Async XLA Ops:
  0.6 8.0 %copy-start = (bf16[16,32,1024]{2,1,0:T(8,128)(2,1)S(1)}, bf16[16,32,1024]{2,1,0:T(8,128)(2,1)}, u32[]{:S(2)}) copy-start(bf16[16,32,1024]{2,1,0:T(8,128)(2,1)} %u_tail.1) | copy-start | bytes 3145732
  0.6 8.0 %copy-start.1 = (bf16[16,32,1024]{2,1,0:T(8,128)(2,1)S(1)}, bf16[16,32,1024]{2,1,0:T(8,128)(2,1)}, u32[]{:S(2)}) copy-start(bf16[16,32,1024]{2,1,0:T(8,128)(2,1)} %v_tail.1) | copy-start | bytes 3145732
  4.2 1.5 %collective-permute-start.1 = (f32[272,128]{1,0:T(8,128)S(1)}, f32[272,128]{1,0:T(8,128)S(1)}, u32[]{:S(2)}, u32[]{:S(2)}) collective-permute-start(f32[272,128]{1,0:T(8,128)S(1)} %get-tuple-element.52), channel_id=1, source_target_pairs={{0,1},{1,0},{2,3},{3,2},{4,5},{5,4},{6,7},{7,6},{8,9},{9,8},{10,11... | collective-permute-start | bytes 417800 | tf_op jit(solution)/shard_map/ppermute | solution.py:710
  5.7 6.9 %collective-permute-start.2 = (f32[272,128]{1,0:T(8,128)S(1)}, f32[272,128]{1,0:T(8,128)S(1)}, u32[]{:S(2)}, u32[]{:S(2)}) collective-permute-start(f32[272,128]{1,0:T(8,128)S(1)} %add.54), channel_id=1, source_target_pairs={{0,2},{2,0},{4,6},{6,4},{8,10},{10,8},{12,14},{14,12},{1,3},{3,1},... | collective-permute-start | bytes 417800 | tf_op jit(solution)/shard_map/ppermute | solution.py:710
  8.8 23.1 %collective-permute-start = (bf16[32,8,1024]{2,1,0:T(8,128)(2,1)S(1)}, bf16[32,8,1024]{2,1,0:T(8,128)(2,1)S(1)}, u32[]{:S(2)}, u32[]{:S(2)}) collective-permute-start(bf16[32,8,1024]{2,1,0:T(8,128)(2,1)S(1)} %pad_maximum_fusion), channel_id=1, source_target_pairs={{0,1},{1,0},{2,3},{3,2},{4,5},{5,4},{6,7},{7,6},{8,9},{9,8},{10,11... | collective-permute-start | bytes 1572872 | tf_op jit(solution)/shard_map/ppermute | solution.py:710
  12.7 5.3 %collective-permute-start.3 = (f32[272,128]{1,0:T(8,128)S(1)}, f32[272,128]{1,0:T(8,128)S(1)}, u32[]{:S(2)}, u32[]{:S(2)}) collective-permute-start(f32[272,128]{1,0:T(8,128)S(1)} %add.55), channel_id=1, source_target_pairs={{0,4},{2,6},{4,0},{6,2},{8,12},{10,14},{12,8},{14,10},{1,5},{3,7},... | collective-permute-start | bytes 417800 | tf_op jit(solution)/shard_map/ppermute | solution.py:710
  14.6 18.2 %copy-start.7 = (f32[9,1024]{1,0:T(8,128)S(1)}, f32[9,1024]{1,0:T(8,128)}, u32[]{:S(2)}) copy-start(f32[9,1024]{1,0:T(8,128)} %taps_ref.3) | copy-start | bytes 110596
  15.2 17.6 %copy-start.2 = (bf16[1024,1024]{1,0:T(8,128)(2,1)S(1)}, bf16[1024,1024]{1,0:T(8,128)(2,1)}, u32[]{:S(2)}) copy-start(bf16[1024,1024]{1,0:T(8,128)(2,1)} %proj_ref.3) | copy-start | bytes 6291460
  15.2 17.6 %copy-start.9 = (f32[16]{0:T(128)S(1)}, f32[16]{0:T(128)}, u32[]{:S(2)}) copy-start(f32[16]{0:T(128)} %sharp_ref.3) | copy-start | bytes 196
  15.2 15.9 %collective-permute-start.5 = (bf16[3,32,1024]{2,1,0:T(8,128)(2,1)S(1)}, bf16[3,32,1024]{2,1,0:T(8,128)(2,1)S(1)}, u32[]{:S(2)}, u32[]{:S(2)}) collective-permute-start(bf16[3,32,1024]{2,1,0:T(8,128)(2,1)S(1)} %get-tuple-element.53), channel_id=1, source_target_pairs={{0,2},{2,0},{4,6},{6,4},{8,10},{10,8},{12,14},{14,12},{1,3},{3,1},... | collective-permute-start | bytes 589832 | tf_op jit(solution)/shard_map/ppermute | solution.py:710
  16.8 14.4 %collective-permute-start.6 = (bf16[3,32,1024]{2,1,0:T(8,128)(2,1)S(1)}, bf16[3,32,1024]{2,1,0:T(8,128)(2,1)S(1)}, u32[]{:S(2)}, u32[]{:S(2)}) collective-permute-start(bf16[3,32,1024]{2,1,0:T(8,128)(2,1)S(1)} %get-tuple-element.56), channel_id=1, source_target_pairs={{2,4},{6,8},{10,12},{4,2},{8,6},{12,10},{3,5},{7,9},{11,13},{5,3},... | collective-permute-start | bytes 589832 | tf_op jit(solution)/shard_map/ppermute | solution.py:787
  18.0 13.1 %collective-permute-start.4 = (f32[272,128]{1,0:T(8,128)S(1)}, f32[272,128]{1,0:T(8,128)S(1)}, u32[]{:S(2)}, u32[]{:S(2)}) collective-permute-start(f32[272,128]{1,0:T(8,128)S(1)} %add.56), channel_id=1, source_target_pairs={{0,8},{2,10},{4,12},{6,14},{8,0},{10,2},{12,4},{14,6},{1,9},{3,11}... | collective-permute-start | bytes 417800 | tf_op jit(solution)/shard_map/ppermute | solution.py:710
  31.2 1.6 %collective-permute-start.8 = (f32[272,128]{1,0:T(8,128)S(1)}, f32[272,128]{1,0:T(8,128)S(1)}, u32[]{:S(2)}, u32[]{:S(2)}) collective-permute-start(f32[272,128]{1,0:T(8,128)S(1)} %add.57.own_ref.energy_own_ref), channel_id=1, source_target_pairs={{0,1},{1,0},{2,3},{3,2},{4,5},{5,4},{6,7},{7,6},{8,9},{9,8},{10,11... | collective-permute-start | bytes 417800 | tf_op jit(solution)/shard_map/ppermute | solution.py:710
  31.3 1.5 %collective-permute-start.7 = (bf16[6,8,1024]{2,1,0:T(8,128)(2,1)S(1)}, bf16[6,8,1024]{2,1,0:T(8,128)(2,1)S(1)}, u32[]{:S(2)}, u32[]{:S(2)}) collective-permute-start(bf16[6,8,1024]{2,1,0:T(8,128)(2,1)S(1)} %fusion.2), channel_id=1, source_target_pairs={{0,1},{1,0},{2,3},{3,2},{4,5},{5,4},{6,7},{7,6},{8,9},{9,8},{10,11... | collective-permute-start | bytes 294920 | tf_op jit(solution)/shard_map/ppermute | solution.py:710
  41.0 8.6 %collective-permute-start.9 = (bf16[256,512]{1,0:T(8,128)(2,1)S(1)}, bf16[256,512]{1,0:T(8,128)(2,1)S(1)}, u32[]{:S(2)}, u32[]{:S(2)}) collective-permute-start(bf16[256,512]{1,0:T(8,128)(2,1)S(1)} %get-tuple-element.99), channel_id=1, source_target_pairs={{0,2},{2,0},{4,6},{6,4},{8,10},{10,8},{12,14},{14,12},{1,3},{3,1},... | collective-permute-start | bytes 786440 | tf_op jit(solution)/shard_map/ppermute | solution.py:710
  49.6 1.8 %collective-permute-start.10 = (bf16[320,128]{1,0:T(8,128)(2,1)S(1)}, bf16[320,128]{1,0:T(8,128)(2,1)S(1)}, u32[]{:S(2)}, u32[]{:S(2)}) collective-permute-start(bf16[320,128]{1,0:T(8,128)(2,1)S(1)} %get-tuple-element.71), channel_id=1, source_target_pairs={{0,1},{1,0},{2,3},{3,2},{4,5},{5,4},{6,7},{7,6},{8,9},{9,8},{10,11... | collective-permute-start | bytes 245768 | tf_op jit(solution)/shard_map/ppermute | solution.py:710
  49.6 8.7 %collective-permute-start.14 = (bf16[256,512]{1,0:T(8,128)(2,1)S(1)}, bf16[256,512]{1,0:T(8,128)(2,1)S(1)}, u32[]{:S(2)}, u32[]{:S(2)}) collective-permute-start(bf16[256,512]{1,0:T(8,128)(2,1)S(1)} %get-tuple-element.98), channel_id=1, source_target_pairs={{0,2},{2,0},{4,6},{6,4},{8,10},{10,8},{12,14},{14,12},{1,3},{3,1},... | collective-permute-start | bytes 786440 | tf_op jit(solution)/shard_map/ppermute | solution.py:710
  52.7 5.9 %collective-permute-start.12 = (bf16[512,512]{1,0:T(8,128)(2,1)S(1)}, bf16[512,512]{1,0:T(8,128)(2,1)S(1)}, u32[]{:S(2)}, u32[]{:S(2)}) collective-permute-start(bf16[512,512]{1,0:T(8,128)(2,1)S(1)} %get-tuple-element.74), channel_id=1, source_target_pairs={{0,1},{1,0},{2,3},{3,2},{4,5},{5,4},{6,7},{7,6},{8,9},{9,8},{10,11... | collective-permute-start | bytes 1572872 | tf_op jit(solution)/shard_map/ppermute | solution.py:710
  52.9 5.5 %collective-permute-start.11 = (bf16[320,128]{1,0:T(8,128)(2,1)S(1)}, bf16[320,128]{1,0:T(8,128)(2,1)S(1)}, u32[]{:S(2)}, u32[]{:S(2)}) collective-permute-start(bf16[320,128]{1,0:T(8,128)(2,1)S(1)} %add_convert_fusion), channel_id=1, source_target_pairs={{0,4},{2,6},{4,0},{6,2},{8,12},{10,14},{12,8},{14,10},{1,5},{3,7},... | collective-permute-start | bytes 245768 | tf_op jit(solution)/shard_map/ppermute | solution.py:710
  58.7 5.4 %collective-permute-start.13 = (bf16[320,128]{1,0:T(8,128)(2,1)S(1)}, bf16[320,128]{1,0:T(8,128)(2,1)S(1)}, u32[]{:S(2)}, u32[]{:S(2)}) collective-permute-start(bf16[320,128]{1,0:T(8,128)(2,1)S(1)} %convert_add_fusion.6), channel_id=1, source_target_pairs={{0,2},{2,0},{4,6},{6,4},{8,10},{10,8},{12,14},{14,12},{1,3},{3,1},... | collective-permute-start | bytes 245768 | tf_op jit(solution)/shard_map/ppermute | solution.py:710
  60.6 6.3 %collective-permute-start.16 = (bf16[128,512]{1,0:T(8,128)(2,1)S(1)}, bf16[128,512]{1,0:T(8,128)(2,1)S(1)}, u32[]{:S(2)}, u32[]{:S(2)}) collective-permute-start(bf16[128,512]{1,0:T(8,128)(2,1)S(1)} %get-tuple-element.95), channel_id=1, source_target_pairs={{0,4},{2,6},{4,0},{6,2},{8,12},{10,14},{12,8},{14,10},{1,5},{3,7},... | collective-permute-start | bytes 393224 | tf_op jit(solution)/shard_map/ppermute | solution.py:710
  60.6 7.5 %collective-permute-start.18 = (bf16[128,512]{1,0:T(8,128)(2,1)S(1)}, bf16[128,512]{1,0:T(8,128)(2,1)S(1)}, u32[]{:S(2)}, u32[]{:S(2)}) collective-permute-start(bf16[128,512]{1,0:T(8,128)(2,1)S(1)} %get-tuple-element.96), channel_id=1, source_target_pairs={{0,6},{2,4},{4,2},{6,0},{8,14},{10,12},{12,10},{14,8},{1,7},{3,5},... | collective-permute-start | bytes 393224 | tf_op jit(solution)/shard_map/ppermute | solution.py:710
  62.4 7.0 %collective-permute-start.17 = (bf16[128,512]{1,0:T(8,128)(2,1)S(1)}, bf16[128,512]{1,0:T(8,128)(2,1)S(1)}, u32[]{:S(2)}, u32[]{:S(2)}) collective-permute-start(bf16[128,512]{1,0:T(8,128)(2,1)S(1)} %get-tuple-element.97), channel_id=1, source_target_pairs={{0,2},{2,0},{4,6},{6,4},{8,10},{10,8},{12,14},{14,12},{1,3},{3,1},... | collective-permute-start | bytes 393224 | tf_op jit(solution)/shard_map/ppermute | solution.py:710
  64.2 13.3 %copy-start.4 = (bf16[16,32,1024]{2,1,0:T(8,128)(2,1)S(1)}, bf16[16,32,1024]{2,1,0:T(8,128)(2,1)}, u32[]{:S(2)}) copy-start(bf16[16,32,1024]{2,1,0:T(8,128)(2,1)} %param.7) | copy-start | bytes 3145732
  64.2 13.3 %copy-start.6 = (bf16[16,32,1024]{2,1,0:T(8,128)(2,1)S(1)}, bf16[16,32,1024]{2,1,0:T(8,128)(2,1)}, u32[]{:S(2)}) copy-start(bf16[16,32,1024]{2,1,0:T(8,128)(2,1)} %param.8) | copy-start | bytes 3145732
  64.2 5.3 %collective-permute-start.20 = (bf16[256,512]{1,0:T(8,128)(2,1)S(1)}, bf16[256,512]{1,0:T(8,128)(2,1)S(1)}, u32[]{:S(2)}, u32[]{:S(2)}) collective-permute-start(bf16[256,512]{1,0:T(8,128)(2,1)S(1)} %slice.87), channel_id=1, source_target_pairs={{0,1},{1,0},{2,3},{3,2},{4,5},{5,4},{6,7},{7,6},{8,9},{9,8},{10,11... | collective-permute-start | bytes 786440 | tf_op jit(solution)/shard_map/ppermute | solution.py:710
  64.3 7.6 %collective-permute-start.15 = (bf16[320,128]{1,0:T(8,128)(2,1)S(1)}, bf16[320,128]{1,0:T(8,128)(2,1)S(1)}, u32[]{:S(2)}, u32[]{:S(2)}) collective-permute-start(bf16[320,128]{1,0:T(8,128)(2,1)S(1)} %convert_add_fusion.5), channel_id=1, source_target_pairs={{0,8},{2,10},{4,12},{6,14},{8,0},{10,2},{12,4},{14,6},{1,9},{3,11}... | collective-permute-start | bytes 245768 | tf_op jit(solution)/shard_map/ppermute | solution.py:710
  69.5 10.7 %copy-start.10 = (f32[128,512]{1,0:T(8,128)}, f32[128,512]{1,0:T(8,128)S(1)}, u32[]{:S(2)}) copy-start(f32[128,512]{1,0:T(8,128)S(1)} %convert_add_fusion.3) | copy-start | bytes 786436
  69.6 5.0 %collective-permute-start.21 = (bf16[128,512]{1,0:T(8,128)(2,1)S(1)}, bf16[128,512]{1,0:T(8,128)(2,1)S(1)}, u32[]{:S(2)}, u32[]{:S(2)}) collective-permute-start(bf16[128,512]{1,0:T(8,128)(2,1)S(1)} %slice.88), channel_id=1, source_target_pairs={{0,4},{2,6},{4,0},{6,2},{8,12},{10,14},{12,8},{14,10},{1,5},{3,7},... | collective-permute-start | bytes 393224 | tf_op jit(solution)/shard_map/ppermute | solution.py:710
  71.9 5.6 %collective-permute-start.19 = (f32[320,128]{1,0:T(8,128)S(1)}, f32[320,128]{1,0:T(8,128)S(1)}, u32[]{:S(2)}, u32[]{:S(2)}) collective-permute-start(f32[320,128]{1,0:T(8,128)S(1)} %convert_add_fusion.4.own_ref), channel_id=1, source_target_pairs={{0,1},{1,0},{2,3},{3,2},{4,5},{5,4},{6,7},{7,6},{8,9},{9,8},{10,11... | collective-permute-start | bytes 491528 | tf_op jit(solution)/shard_map/ppermute | solution.py:710
  74.7 8.0 %collective-permute-start.22 = (bf16[128,512]{1,0:T(8,128)(2,1)S(1)}, bf16[128,512]{1,0:T(8,128)(2,1)S(1)}, u32[]{:S(2)}, u32[]{:S(2)}) collective-permute-start(bf16[128,512]{1,0:T(8,128)(2,1)S(1)} %pad_maximum_fusion.2), channel_id=1, source_target_pairs={{0,8},{2,10},{4,12},{6,14},{8,0},{10,2},{12,4},{14,6},{1,9},{3,11}... | collective-permute-start | bytes 393224 | tf_op jit(solution)/shard_map/ppermute | solution.py:710
  81.1 1.7 %slice-start = ((f32[128,512]{1,0:T(8,128)}), f32[64,512]{1,0:T(8,128)S(1)}, s32[]{:S(2)}) async-start(f32[128,512]{1,0:T(8,128)} %copy-done.10), calls=%async_computation | async-start | bytes 262144 | tf_op jit(solution)/shard_map/slice | solution.py:723
  (3 other events, 3.4 us)

commit v5 on v4

--- a/solution.py
+++ b/solution.py
@@ -778,7 +778,7 @@
     pairs_next = [(j, j + 1) for j in range(1, rows - 1, 2)]
     pairs_next = pairs_next + [(b, a) for a, b in pairs_next]
     side = swap(jnp.concatenate([edge(v), edge(u)]), "col", 1)
-    for i, bit in enumerate(bits):
+    for i, bit in enumerate(bits[:1] + bits[2:] + bits[1:2]):
         total = total + swap(total, "row", bit)
         if i == 2:
             from_twin = swap(to_twin, "row", 1)

time: 83.7 us -> 82.4 us (0.984)
  waiting for transfers between devices: 29 us -> 26.6 us
  starting transfers between devices: 24.7 us -> 25.7 us
    ppermute x22, waiting for transfers between devices: 29 us -> 26.6 us  [swap(): lax.ppermute(x, axis, [(i, i ^ bit) for i in range(lax.axis_size(axis))])]
    ppermute x22, starting transfers between devices: 24 us -> 25 us  [swap(): lax.ppermute(x, axis, [(i, i ^ bit) for i in range(lax.axis_size(axis))])]
  transfers between devices with their start and end apart: 23 -> 23, of which waited for: 12 -> 12; matrix products, arithmetic and copies ran while one was open for 1% -> 1% of each run, Pallas kernels for 17% -> 18%
where the time goes in v5:
time: 82.4 us; the launch traced here: 82.2 us
  waiting for transfers between devices  26.6 us (32%)
  starting transfers between devices  25.7 us (31%)
  Pallas kernels  23.4 us (28%)
  local copies, waits for them, and re-layouts  3.7 us (4%)
  other arithmetic  1.63 us (2%)
  between operations  1.06 us (1%)
    ppermute x22, waiting for transfers between devices, swap(): lax.ppermute(x, axis, [(i, i ^ bit) for i in range(lax.axis_size(axis))])  26.6 us
    ppermute x22, starting transfers between devices, swap(): lax.ppermute(x, axis, [(i, i ^ bit) for i in range(lax.axis_size(axis))])  25 us
    pallas_call x1, Pallas kernels, back_call(): pl.pallas_call(functools.partial(back_kernel, head_size, tile, span), in_...  8.13 us
    pallas_call x1, Pallas kernels, front_call(): pl.pallas_call(functools.partial(front_kernel, head_size, tile, piece_row...  8.07 us
    unnamed x22, local copies, waits for them, and re-layouts  3.47 us
    pallas_call x1, Pallas kernels, final_call(): pl.pallas_call(functools.partial(final_kernel, head_size), grid=(2,), in_...  2.76 us
  transfers between devices with their start and end apart: 23, of which 12 were waited for; matrix products, arithmetic and copies ran while one was open for 1% of the time, Pallas kernels for 18%

profile of v5, /device:TPU:0, one launch (start us, length us, event | category | flops | bytes accessed | tf_op | source)
XLA Modules:
  0.0 82.2 jit_solution(10688308696759387881)
XLA Ops:
  0.7 1.4 %copy-done.3 = bf16[16,32,1024]{2,1,0:T(8,128)(2,1)S(1)} copy-done((bf16[16,32,1024]{2,1,0:T(8,128)(2,1)S(1)}, bf16[16,32,1024]{2,1,0:T(8,128)(2,1)}, u32[]{:S(2)}) %copy-start.3) | copy-done | bytes 1048600
  2.0 1.2 %copy-done.5 = bf16[16,32,1024]{2,1,0:T(8,128)(2,1)S(1)} copy-done((bf16[16,32,1024]{2,1,0:T(8,128)(2,1)S(1)}, bf16[16,32,1024]{2,1,0:T(8,128)(2,1)}, u32[]{:S(2)}) %copy-start.5) | copy-done | bytes 1048600
  3.3 0.9 %gram.1 = (f32[272,128]{1,0:T(8,128)S(1)}, f32[272,128]{1,0:T(8,128)S(1)}) custom-call(bf16[512,1024]{1,0:T(8,128)(2,1)S(1)} %bitcast.18, bf16[512,1024]{1,0:T(8,128)(2,1)S(1)} %bitcast.20), custom_call_target="tpu_custom_call" | custom-call | bytes 9000000 | tf_op jit(solution)/shard_map/gram/pallas_call | solution.py:156
  4.7 1.0 %collective-permute-done.1 = f32[272,128]{1,0:T(8,128)S(1)} collective-permute-done((f32[272,128]{1,0:T(8,128)S(1)}, f32[272,128]{1,0:T(8,128)S(1)}, u32[]{:S(2)}, u32[]{:S(2)}) %collective-permute-start.1) | collective-permute-done | bytes 139296 | tf_op jit(solution)/shard_map/ppermute | solution.py:710
  5.7 2.9 %collective-permute-start.2 = (f32[272,128]{1,0:T(8,128)S(1)}, f32[272,128]{1,0:T(8,128)S(1)}, u32[]{:S(2)}, u32[]{:S(2)}) collective-permute-start(f32[272,128]{1,0:T(8,128)S(1)} %add.54), channel_id=1, source_target_pairs={{0,2},{2,0},{4,6},{6,4},{8,10},{10,8},{12,14},{14,12},{1,3},{3,1},... | collective-permute-start | bytes 417800 | tf_op jit(solution)/shard_map/ppermute | solution.py:710
  8.9 3.8 %collective-permute-done.2 = f32[272,128]{1,0:T(8,128)S(1)} collective-permute-done((f32[272,128]{1,0:T(8,128)S(1)}, f32[272,128]{1,0:T(8,128)S(1)}, u32[]{:S(2)}, u32[]{:S(2)}) %collective-permute-start.2) | collective-permute-done | bytes 139296 | tf_op jit(solution)/shard_map/ppermute | solution.py:710
  12.7 2.9 %collective-permute-start.3 = (f32[272,128]{1,0:T(8,128)S(1)}, f32[272,128]{1,0:T(8,128)S(1)}, u32[]{:S(2)}, u32[]{:S(2)}) collective-permute-start(f32[272,128]{1,0:T(8,128)S(1)} %add.55), channel_id=1, source_target_pairs={{0,8},{2,10},{4,12},{6,14},{8,0},{10,2},{12,4},{14,6},{1,9},{3,11}... | collective-permute-start | bytes 417800 | tf_op jit(solution)/shard_map/ppermute | solution.py:710
  16.2 1.6 %collective-permute-start.5 = (bf16[3,32,1024]{2,1,0:T(8,128)(2,1)S(1)}, bf16[3,32,1024]{2,1,0:T(8,128)(2,1)S(1)}, u32[]{:S(2)}, u32[]{:S(2)}) collective-permute-start(bf16[3,32,1024]{2,1,0:T(8,128)(2,1)S(1)} %get-tuple-element.53), channel_id=1, source_target_pairs={{0,2},{2,0},{4,6},{6,4},{8,10},{10,8},{12,14},{14,12},{1,3},{3,1},... | collective-permute-start | bytes 589832 | tf_op jit(solution)/shard_map/ppermute | solution.py:710
  17.8 0.7 collective-permute-start.6
  18.5 3.4 %collective-permute-done.3 = f32[272,128]{1,0:T(8,128)S(1)} collective-permute-done((f32[272,128]{1,0:T(8,128)S(1)}, f32[272,128]{1,0:T(8,128)S(1)}, u32[]{:S(2)}, u32[]{:S(2)}) %collective-permute-start.3) | collective-permute-done | bytes 139296 | tf_op jit(solution)/shard_map/ppermute | solution.py:710
  22.5 6.6 %collective-permute-done.4 = f32[272,128]{1,0:T(8,128)S(1)} collective-permute-done((f32[272,128]{1,0:T(8,128)S(1)}, f32[272,128]{1,0:T(8,128)S(1)}, u32[]{:S(2)}, u32[]{:S(2)}) %collective-permute-start.4) | collective-permute-done | bytes 139296 | tf_op jit(solution)/shard_map/ppermute | solution.py:710
  29.8 0.9 %collective-permute-done.7 = bf16[6,8,1024]{2,1,0:T(8,128)(2,1)S(1)} collective-permute-done((bf16[6,8,1024]{2,1,0:T(8,128)(2,1)S(1)}, bf16[6,8,1024]{2,1,0:T(8,128)(2,1)S(1)}, u32[]{:S(2)}, u32[]{:S(2)}) %collective-permute-start.7) | collective-permute-done | bytes 98336 | tf_op jit(solution)/shard_map/ppermute | solution.py:710
  30.8 8.1 %front.1 = (bf16[512,512]{1,0:T(8,128)(2,1)S(1)}, f32[512,128]{1,0:T(8,128)S(1)}, f32[512,128]{1,0:T(8,128)S(1)}, f32[512,128]{1,0:T(8,128)S(1)}, bf16[1024,256]...) custom-call(s32[2]{0:T(128)S(1)} %pad_add_fusion.here_ref.col_ref, ...), custom_call_target="tpu_custom_call" | custom-call | bytes 36000000 | tf_op jit(solution)/shard_map/front/pallas_call | solution.py:515
  39.0 8.1 %back.1 = (bf16[512,512]{1,0:T(8,128)(2,1)S(1)}, bf16[512,512]{1,0:T(8,128)(2,1)S(1)}, bf16[512,1024]{1,0:T(8,128)(2,1)S(1)}, f32[320,128]{1,0:T(8,128)S(1)}, bf16[320,128]{1,0:T(8,128)(2,1)S(1)}) custom-call(s32[2]{0:T(128)S(1)} %pad_add_fusion.here_ref.col_ref, bf16[512,1024]{1,0:T(8,128)(2,1)S(1)} %bitcast.15, bf16[512,1024]{1,0:T(8,128)(2,1)S(1)} %bitcast.17, ...), custom_call_target="tpu_custom_call" | custom-call | bytes 36000000 | tf_op jit(solution)/shard_map/back/pallas_call | solution.py:540
  47.6 1.7 %collective-permute-start.14 = (bf16[256,512]{1,0:T(8,128)(2,1)S(1)}, bf16[256,512]{1,0:T(8,128)(2,1)S(1)}, u32[]{:S(2)}, u32[]{:S(2)}) collective-permute-start(bf16[256,512]{1,0:T(8,128)(2,1)S(1)} %get-tuple-element.98), channel_id=1, source_target_pairs={{0,2},{2,0},{4,6},{6,4},{8,10},{10,8},{12,14},{14,12},{1,3},{3,1},... | collective-permute-start | bytes 786440 | tf_op jit(solution)/shard_map/ppermute | solution.py:710
  49.3 1.3 %projector.1 = (f32[512,512]{1,0:T(8,128)S(1)}, bf16[512,512]{1,0:T(8,128)(2,1)S(1)}) custom-call(s32[2]{0:T(128)S(1)} %pad_add_fusion.here_ref.col_ref, bf16[800,1024]{1,0:T(8,128)(2,1)S(1)} %get-tuple-element.59.mixed_all, bf16[512,512]{1,0:T(8,128)(2,1)S(1)} %get-tuple-element.72.target_ref, bf16[320,128]{1,0:T(8,128)(2,1)S(1)} %collective-permute-done.10.after_ref), custom_call_target="tpu_custom_call" | custom-call | bytes 7200000 | tf_op jit(solution)/shard_map/projector/pallas_call | solution.py:562
  50.9 1.5 %collective-permute-start.11 = (bf16[320,128]{1,0:T(8,128)(2,1)S(1)}, bf16[320,128]{1,0:T(8,128)(2,1)S(1)}, u32[]{:S(2)}, u32[]{:S(2)}) collective-permute-start(bf16[320,128]{1,0:T(8,128)(2,1)S(1)} %add_convert_fusion), channel_id=1, source_target_pairs={{0,4},{2,6},{4,0},{6,2},{8,12},{10,14},{12,8},{14,10},{1,5},{3,7},... | collective-permute-start | bytes 245768 | tf_op jit(solution)/shard_map/ppermute | solution.py:710
  52.4 3.8 %collective-permute-done.14 = bf16[256,512]{1,0:T(8,128)(2,1)S(1)} collective-permute-done((bf16[256,512]{1,0:T(8,128)(2,1)S(1)}, bf16[256,512]{1,0:T(8,128)(2,1)S(1)}, u32[]{:S(2)}, u32[]{:S(2)}) %collective-permute-start.14) | collective-permute-done | bytes 262176 | tf_op jit(solution)/shard_map/ppermute | solution.py:710
  56.6 1.8 %collective-permute-start.13 = (bf16[320,128]{1,0:T(8,128)(2,1)S(1)}, bf16[320,128]{1,0:T(8,128)(2,1)S(1)}, u32[]{:S(2)}, u32[]{:S(2)}) collective-permute-start(bf16[320,128]{1,0:T(8,128)(2,1)S(1)} %convert_add_fusion.6), channel_id=1, source_target_pairs={{0,2},{2,0},{4,6},{6,4},{8,10},{10,8},{12,14},{14,12},{1,3},{3,1},... | collective-permute-start | bytes 245768 | tf_op jit(solution)/shard_map/ppermute | solution.py:710
  58.5 0.7 collective-permute-start.16
  59.2 1.2 %collective-permute-start.18 = (bf16[128,512]{1,0:T(8,128)(2,1)S(1)}, bf16[128,512]{1,0:T(8,128)(2,1)S(1)}, u32[]{:S(2)}, u32[]{:S(2)}) collective-permute-start(bf16[128,512]{1,0:T(8,128)(2,1)S(1)} %get-tuple-element.96), channel_id=1, source_target_pairs={{0,6},{2,4},{4,2},{6,0},{8,14},{10,12},{12,10},{14,8},{1,7},{3,5},... | collective-permute-start | bytes 393224 | tf_op jit(solution)/shard_map/ppermute | solution.py:710
  60.4 1.7 %collective-permute-start.17 = (bf16[128,512]{1,0:T(8,128)(2,1)S(1)}, bf16[128,512]{1,0:T(8,128)(2,1)S(1)}, u32[]{:S(2)}, u32[]{:S(2)}) collective-permute-start(bf16[128,512]{1,0:T(8,128)(2,1)S(1)} %get-tuple-element.97), channel_id=1, source_target_pairs={{0,2},{2,0},{4,6},{6,4},{8,10},{10,8},{12,14},{14,12},{1,3},{3,1},... | collective-permute-start | bytes 393224 | tf_op jit(solution)/shard_map/ppermute | solution.py:710
  62.2 1.9 %collective-permute-start.15 = (bf16[320,128]{1,0:T(8,128)(2,1)S(1)}, bf16[320,128]{1,0:T(8,128)(2,1)S(1)}, u32[]{:S(2)}, u32[]{:S(2)}) collective-permute-start(bf16[320,128]{1,0:T(8,128)(2,1)S(1)} %convert_add_fusion.5), channel_id=1, source_target_pairs={{0,8},{2,10},{4,12},{6,14},{8,0},{10,2},{12,4},{14,6},{1,9},{3,11}... | collective-permute-start | bytes 245768 | tf_op jit(solution)/shard_map/ppermute | solution.py:710
  64.8 1.5 %collective-permute-done.18 = bf16[128,512]{1,0:T(8,128)(2,1)S(1)} collective-permute-done((bf16[128,512]{1,0:T(8,128)(2,1)S(1)}, bf16[128,512]{1,0:T(8,128)(2,1)S(1)}, u32[]{:S(2)}, u32[]{:S(2)}) %collective-permute-start.18) | collective-permute-done | bytes 131104 | tf_op jit(solution)/shard_map/ppermute | solution.py:710
  66.3 1.4 %collective-permute-done.17 = bf16[128,512]{1,0:T(8,128)(2,1)S(1)} collective-permute-done((bf16[128,512]{1,0:T(8,128)(2,1)S(1)}, bf16[128,512]{1,0:T(8,128)(2,1)S(1)}, u32[]{:S(2)}, u32[]{:S(2)}) %collective-permute-start.17) | collective-permute-done | bytes 131104 | tf_op jit(solution)/shard_map/ppermute | solution.py:710
  67.8 1.7 %collective-permute-start.21 = (bf16[128,512]{1,0:T(8,128)(2,1)S(1)}, bf16[128,512]{1,0:T(8,128)(2,1)S(1)}, u32[]{:S(2)}, u32[]{:S(2)}) collective-permute-start(bf16[128,512]{1,0:T(8,128)(2,1)S(1)} %slice.88), channel_id=1, source_target_pairs={{0,4},{2,6},{4,0},{6,2},{8,12},{10,14},{12,8},{14,10},{1,5},{3,7},... | collective-permute-start | bytes 393224 | tf_op jit(solution)/shard_map/ppermute | solution.py:710
  69.9 3.0 %collective-permute-done.21 = bf16[128,512]{1,0:T(8,128)(2,1)S(1)} collective-permute-done((bf16[128,512]{1,0:T(8,128)(2,1)S(1)}, bf16[128,512]{1,0:T(8,128)(2,1)S(1)}, u32[]{:S(2)}, u32[]{:S(2)}) %collective-permute-start.21) | collective-permute-done | bytes 131104 | tf_op jit(solution)/shard_map/ppermute | solution.py:710
  73.0 3.1 %collective-permute-start.22 = (bf16[128,512]{1,0:T(8,128)(2,1)S(1)}, bf16[128,512]{1,0:T(8,128)(2,1)S(1)}, u32[]{:S(2)}, u32[]{:S(2)}) collective-permute-start(bf16[128,512]{1,0:T(8,128)(2,1)S(1)} %pad_maximum_fusion.2), channel_id=1, source_target_pairs={{0,8},{2,10},{4,12},{6,14},{8,0},{10,2},{12,4},{14,6},{1,9},{3,11}... | collective-permute-start | bytes 393224 | tf_op jit(solution)/shard_map/ppermute | solution.py:710
  76.1 2.8 %final.1 = (bf16[512,1024]{1,0:T(8,128)(2,1)}, bf16[512,1024]{1,0:T(8,128)(2,1)}, f32[16]{0:T(128)}, f32[9,1024]{1,0:T(8,128)}) custom-call(s32[2]{0:T(128)S(1)} %pad_add_fusion.here_ref.col_ref, f32[16]{0:T(128)S(1)} %copy-done.9, f32[320,128]{1,0:T(8,128)S(1)} %convert_add_fusion.4.own_ref, f32[320,128]{1,0:T(8,128)S(1)} %collective-permute-done.19.far_ref, ...), custom_call_target="tpu_custom_call" | custom-call | bytes 18000000 | tf_op jit(solution)/shard_map/final/pallas_call | solution.py:686
  78.9 0.8 %copy-done.8 = f32[9,1024]{1,0:T(8,128)S(1)} copy-done((f32[9,1024]{1,0:T(8,128)S(1)}, f32[9,1024]{1,0:T(8,128)}, u32[]{:S(2)}) %copy-start.8) | copy-done | bytes 36888
  79.7 1.6 %content.1 = (bf16[512,1024]{1,0:T(8,128)(2,1)}, bf16[512,1024]{1,0:T(8,128)(2,1)}) custom-call(bf16[512,1024]{1,0:T(8,128)(2,1)S(1)} %get-tuple-element.63.grad_ref, bf16[1024,256]{1,0:T(8,128)(2,1)S(1)} %get-tuple-element.64.block_ref, bf16[512,512]{1,0:T(8,128)(2,1)S(1)} %get-tuple-element.65.merged_front, ...), custom_call_target="tpu_custom_call" | custom-call | bytes 7200000 | tf_op jit(solution)/shard_map/content/pallas_call | solution.py:592
  81.4 0.7 pad_maximum_fusion.1
  (77 shorter events, 5.2 us)
Async XLA Ops:
  0.6 8.0 %copy-start = (bf16[16,32,1024]{2,1,0:T(8,128)(2,1)S(1)}, bf16[16,32,1024]{2,1,0:T(8,128)(2,1)}, u32[]{:S(2)}) copy-start(bf16[16,32,1024]{2,1,0:T(8,128)(2,1)} %u_tail.1) | copy-start | bytes 3145732
  0.6 8.0 %copy-start.1 = (bf16[16,32,1024]{2,1,0:T(8,128)(2,1)S(1)}, bf16[16,32,1024]{2,1,0:T(8,128)(2,1)}, u32[]{:S(2)}) copy-start(bf16[16,32,1024]{2,1,0:T(8,128)(2,1)} %v_tail.1) | copy-start | bytes 3145732
  4.2 1.5 %collective-permute-start.1 = (f32[272,128]{1,0:T(8,128)S(1)}, f32[272,128]{1,0:T(8,128)S(1)}, u32[]{:S(2)}, u32[]{:S(2)}) collective-permute-start(f32[272,128]{1,0:T(8,128)S(1)} %get-tuple-element.52), channel_id=1, source_target_pairs={{0,1},{1,0},{2,3},{3,2},{4,5},{5,4},{6,7},{7,6},{8,9},{9,8},{10,11... | collective-permute-start | bytes 417800 | tf_op jit(solution)/shard_map/ppermute | solution.py:710
  5.7 6.9 %collective-permute-start.2 = (f32[272,128]{1,0:T(8,128)S(1)}, f32[272,128]{1,0:T(8,128)S(1)}, u32[]{:S(2)}, u32[]{:S(2)}) collective-permute-start(f32[272,128]{1,0:T(8,128)S(1)} %add.54), channel_id=1, source_target_pairs={{0,2},{2,0},{4,6},{6,4},{8,10},{10,8},{12,14},{14,12},{1,3},{3,1},... | collective-permute-start | bytes 417800 | tf_op jit(solution)/shard_map/ppermute | solution.py:710
  8.8 21.1 %collective-permute-start = (bf16[32,8,1024]{2,1,0:T(8,128)(2,1)S(1)}, bf16[32,8,1024]{2,1,0:T(8,128)(2,1)S(1)}, u32[]{:S(2)}, u32[]{:S(2)}) collective-permute-start(bf16[32,8,1024]{2,1,0:T(8,128)(2,1)S(1)} %pad_maximum_fusion), channel_id=1, source_target_pairs={{0,1},{1,0},{2,3},{3,2},{4,5},{5,4},{6,7},{7,6},{8,9},{9,8},{10,11... | collective-permute-start | bytes 1572872 | tf_op jit(solution)/shard_map/ppermute | solution.py:710
  12.7 9.2 %collective-permute-start.3 = (f32[272,128]{1,0:T(8,128)S(1)}, f32[272,128]{1,0:T(8,128)S(1)}, u32[]{:S(2)}, u32[]{:S(2)}) collective-permute-start(f32[272,128]{1,0:T(8,128)S(1)} %add.55), channel_id=1, source_target_pairs={{0,8},{2,10},{4,12},{6,14},{8,0},{10,2},{12,4},{14,6},{1,9},{3,11}... | collective-permute-start | bytes 417800 | tf_op jit(solution)/shard_map/ppermute | solution.py:710
  15.6 15.2 %copy-start.7 = (f32[9,1024]{1,0:T(8,128)S(1)}, f32[9,1024]{1,0:T(8,128)}, u32[]{:S(2)}) copy-start(f32[9,1024]{1,0:T(8,128)} %taps_ref.3) | copy-start | bytes 110596
  16.2 14.6 %copy-start.2 = (bf16[1024,1024]{1,0:T(8,128)(2,1)S(1)}, bf16[1024,1024]{1,0:T(8,128)(2,1)}, u32[]{:S(2)}) copy-start(bf16[1024,1024]{1,0:T(8,128)(2,1)} %proj_ref.3) | copy-start | bytes 6291460
  16.2 14.6 %copy-start.9 = (f32[16]{0:T(128)S(1)}, f32[16]{0:T(128)}, u32[]{:S(2)}) copy-start(f32[16]{0:T(128)} %sharp_ref.3) | copy-start | bytes 196
  16.2 12.9 %collective-permute-start.5 = (bf16[3,32,1024]{2,1,0:T(8,128)(2,1)S(1)}, bf16[3,32,1024]{2,1,0:T(8,128)(2,1)S(1)}, u32[]{:S(2)}, u32[]{:S(2)}) collective-permute-start(bf16[3,32,1024]{2,1,0:T(8,128)(2,1)S(1)} %get-tuple-element.53), channel_id=1, source_target_pairs={{0,2},{2,0},{4,6},{6,4},{8,10},{10,8},{12,14},{14,12},{1,3},{3,1},... | collective-permute-start | bytes 589832 | tf_op jit(solution)/shard_map/ppermute | solution.py:710
  17.8 11.3 %collective-permute-start.6 = (bf16[3,32,1024]{2,1,0:T(8,128)(2,1)S(1)}, bf16[3,32,1024]{2,1,0:T(8,128)(2,1)S(1)}, u32[]{:S(2)}, u32[]{:S(2)}) collective-permute-start(bf16[3,32,1024]{2,1,0:T(8,128)(2,1)S(1)} %get-tuple-element.56), channel_id=1, source_target_pairs={{2,4},{6,8},{10,12},{4,2},{8,6},{12,10},{3,5},{7,9},{11,13},{5,3},... | collective-permute-start | bytes 589832 | tf_op jit(solution)/shard_map/ppermute | solution.py:787
  21.9 7.1 %collective-permute-start.4 = (f32[272,128]{1,0:T(8,128)S(1)}, f32[272,128]{1,0:T(8,128)S(1)}, u32[]{:S(2)}, u32[]{:S(2)}) collective-permute-start(f32[272,128]{1,0:T(8,128)S(1)} %add.56), channel_id=1, source_target_pairs={{0,4},{2,6},{4,0},{6,2},{8,12},{10,14},{12,8},{14,10},{1,5},{3,7},... | collective-permute-start | bytes 417800 | tf_op jit(solution)/shard_map/ppermute | solution.py:710
  29.2 1.6 %collective-permute-start.8 = (f32[272,128]{1,0:T(8,128)S(1)}, f32[272,128]{1,0:T(8,128)S(1)}, u32[]{:S(2)}, u32[]{:S(2)}) collective-permute-start(f32[272,128]{1,0:T(8,128)S(1)} %add.57.own_ref.energy_own_ref), channel_id=1, source_target_pairs={{0,1},{1,0},{2,3},{3,2},{4,5},{5,4},{6,7},{7,6},{8,9},{9,8},{10,11... | collective-permute-start | bytes 417800 | tf_op jit(solution)/shard_map/ppermute | solution.py:710
  29.3 1.5 %collective-permute-start.7 = (bf16[6,8,1024]{2,1,0:T(8,128)(2,1)S(1)}, bf16[6,8,1024]{2,1,0:T(8,128)(2,1)S(1)}, u32[]{:S(2)}, u32[]{:S(2)}) collective-permute-start(bf16[6,8,1024]{2,1,0:T(8,128)(2,1)S(1)} %fusion.2), channel_id=1, source_target_pairs={{0,1},{1,0},{2,3},{3,2},{4,5},{5,4},{6,7},{7,6},{8,9},{9,8},{10,11... | collective-permute-start | bytes 294920 | tf_op jit(solution)/shard_map/ppermute | solution.py:710
  38.9 8.6 %collective-permute-start.9 = (bf16[256,512]{1,0:T(8,128)(2,1)S(1)}, bf16[256,512]{1,0:T(8,128)(2,1)S(1)}, u32[]{:S(2)}, u32[]{:S(2)}) collective-permute-start(bf16[256,512]{1,0:T(8,128)(2,1)S(1)} %get-tuple-element.99), channel_id=1, source_target_pairs={{0,2},{2,0},{4,6},{6,4},{8,10},{10,8},{12,14},{14,12},{1,3},{3,1},... | collective-permute-start | bytes 786440 | tf_op jit(solution)/shard_map/ppermute | solution.py:710
  47.5 1.8 %collective-permute-start.10 = (bf16[320,128]{1,0:T(8,128)(2,1)S(1)}, bf16[320,128]{1,0:T(8,128)(2,1)S(1)}, u32[]{:S(2)}, u32[]{:S(2)}) collective-permute-start(bf16[320,128]{1,0:T(8,128)(2,1)S(1)} %get-tuple-element.71), channel_id=1, source_target_pairs={{0,1},{1,0},{2,3},{3,2},{4,5},{5,4},{6,7},{7,6},{8,9},{9,8},{10,11... | collective-permute-start | bytes 245768 | tf_op jit(solution)/shard_map/ppermute | solution.py:710
  47.6 8.7 %collective-permute-start.14 = (bf16[256,512]{1,0:T(8,128)(2,1)S(1)}, bf16[256,512]{1,0:T(8,128)(2,1)S(1)}, u32[]{:S(2)}, u32[]{:S(2)}) collective-permute-start(bf16[256,512]{1,0:T(8,128)(2,1)S(1)} %get-tuple-element.98), channel_id=1, source_target_pairs={{0,2},{2,0},{4,6},{6,4},{8,10},{10,8},{12,14},{14,12},{1,3},{3,1},... | collective-permute-start | bytes 786440 | tf_op jit(solution)/shard_map/ppermute | solution.py:710
  50.6 5.9 %collective-permute-start.12 = (bf16[512,512]{1,0:T(8,128)(2,1)S(1)}, bf16[512,512]{1,0:T(8,128)(2,1)S(1)}, u32[]{:S(2)}, u32[]{:S(2)}) collective-permute-start(bf16[512,512]{1,0:T(8,128)(2,1)S(1)} %get-tuple-element.74), channel_id=1, source_target_pairs={{0,1},{1,0},{2,3},{3,2},{4,5},{5,4},{6,7},{7,6},{8,9},{9,8},{10,11... | collective-permute-start | bytes 1572872 | tf_op jit(solution)/shard_map/ppermute | solution.py:710
  50.9 5.5 %collective-permute-start.11 = (bf16[320,128]{1,0:T(8,128)(2,1)S(1)}, bf16[320,128]{1,0:T(8,128)(2,1)S(1)}, u32[]{:S(2)}, u32[]{:S(2)}) collective-permute-start(bf16[320,128]{1,0:T(8,128)(2,1)S(1)} %add_convert_fusion), channel_id=1, source_target_pairs={{0,4},{2,6},{4,0},{6,2},{8,12},{10,14},{12,8},{14,10},{1,5},{3,7},... | collective-permute-start | bytes 245768 | tf_op jit(solution)/shard_map/ppermute | solution.py:710
  56.6 5.4 %collective-permute-start.13 = (bf16[320,128]{1,0:T(8,128)(2,1)S(1)}, bf16[320,128]{1,0:T(8,128)(2,1)S(1)}, u32[]{:S(2)}, u32[]{:S(2)}) collective-permute-start(bf16[320,128]{1,0:T(8,128)(2,1)S(1)} %convert_add_fusion.6), channel_id=1, source_target_pairs={{0,2},{2,0},{4,6},{6,4},{8,10},{10,8},{12,14},{14,12},{1,3},{3,1},... | collective-permute-start | bytes 245768 | tf_op jit(solution)/shard_map/ppermute | solution.py:710
  58.5 6.3 %collective-permute-start.16 = (bf16[128,512]{1,0:T(8,128)(2,1)S(1)}, bf16[128,512]{1,0:T(8,128)(2,1)S(1)}, u32[]{:S(2)}, u32[]{:S(2)}) collective-permute-start(bf16[128,512]{1,0:T(8,128)(2,1)S(1)} %get-tuple-element.95), channel_id=1, source_target_pairs={{0,4},{2,6},{4,0},{6,2},{8,12},{10,14},{12,8},{14,10},{1,5},{3,7},... | collective-permute-start | bytes 393224 | tf_op jit(solution)/shard_map/ppermute | solution.py:710
  59.2 7.1 %collective-permute-start.18 = (bf16[128,512]{1,0:T(8,128)(2,1)S(1)}, bf16[128,512]{1,0:T(8,128)(2,1)S(1)}, u32[]{:S(2)}, u32[]{:S(2)}) collective-permute-start(bf16[128,512]{1,0:T(8,128)(2,1)S(1)} %get-tuple-element.96), channel_id=1, source_target_pairs={{0,6},{2,4},{4,2},{6,0},{8,14},{10,12},{12,10},{14,8},{1,7},{3,5},... | collective-permute-start | bytes 393224 | tf_op jit(solution)/shard_map/ppermute | solution.py:710
  60.4 7.2 %collective-permute-start.17 = (bf16[128,512]{1,0:T(8,128)(2,1)S(1)}, bf16[128,512]{1,0:T(8,128)(2,1)S(1)}, u32[]{:S(2)}, u32[]{:S(2)}) collective-permute-start(bf16[128,512]{1,0:T(8,128)(2,1)S(1)} %get-tuple-element.97), channel_id=1, source_target_pairs={{0,2},{2,0},{4,6},{6,4},{8,10},{10,8},{12,14},{14,12},{1,3},{3,1},... | collective-permute-start | bytes 393224 | tf_op jit(solution)/shard_map/ppermute | solution.py:710
  62.1 14.0 %copy-start.4 = (bf16[16,32,1024]{2,1,0:T(8,128)(2,1)S(1)}, bf16[16,32,1024]{2,1,0:T(8,128)(2,1)}, u32[]{:S(2)}) copy-start(bf16[16,32,1024]{2,1,0:T(8,128)(2,1)} %param.7) | copy-start | bytes 3145732
  62.1 14.0 %copy-start.6 = (bf16[16,32,1024]{2,1,0:T(8,128)(2,1)S(1)}, bf16[16,32,1024]{2,1,0:T(8,128)(2,1)}, u32[]{:S(2)}) copy-start(bf16[16,32,1024]{2,1,0:T(8,128)(2,1)} %param.8) | copy-start | bytes 3145732
  62.2 5.6 %collective-permute-start.20 = (bf16[256,512]{1,0:T(8,128)(2,1)S(1)}, bf16[256,512]{1,0:T(8,128)(2,1)S(1)}, u32[]{:S(2)}, u32[]{:S(2)}) collective-permute-start(bf16[256,512]{1,0:T(8,128)(2,1)S(1)} %slice.87), channel_id=1, source_target_pairs={{0,1},{1,0},{2,3},{3,2},{4,5},{5,4},{6,7},{7,6},{8,9},{9,8},{10,11... | collective-permute-start | bytes 786440 | tf_op jit(solution)/shard_map/ppermute | solution.py:710
  62.2 7.5 %collective-permute-start.15 = (bf16[320,128]{1,0:T(8,128)(2,1)S(1)}, bf16[320,128]{1,0:T(8,128)(2,1)S(1)}, u32[]{:S(2)}, u32[]{:S(2)}) collective-permute-start(bf16[320,128]{1,0:T(8,128)(2,1)S(1)} %convert_add_fusion.5), channel_id=1, source_target_pairs={{0,8},{2,10},{4,12},{6,14},{8,0},{10,2},{12,4},{14,6},{1,9},{3,11}... | collective-permute-start | bytes 245768 | tf_op jit(solution)/shard_map/ppermute | solution.py:710
  67.7 11.2 %copy-start.10 = (f32[128,512]{1,0:T(8,128)}, f32[128,512]{1,0:T(8,128)S(1)}, u32[]{:S(2)}) copy-start(f32[128,512]{1,0:T(8,128)S(1)} %convert_add_fusion.3) | copy-start | bytes 786436
  67.8 5.0 %collective-permute-start.21 = (bf16[128,512]{1,0:T(8,128)(2,1)S(1)}, bf16[128,512]{1,0:T(8,128)(2,1)S(1)}, u32[]{:S(2)}, u32[]{:S(2)}) collective-permute-start(bf16[128,512]{1,0:T(8,128)(2,1)S(1)} %slice.88), channel_id=1, source_target_pairs={{0,4},{2,6},{4,0},{6,2},{8,12},{10,14},{12,8},{14,10},{1,5},{3,7},... | collective-permute-start | bytes 393224 | tf_op jit(solution)/shard_map/ppermute | solution.py:710
  69.8 6.3 %collective-permute-start.19 = (f32[320,128]{1,0:T(8,128)S(1)}, f32[320,128]{1,0:T(8,128)S(1)}, u32[]{:S(2)}, u32[]{:S(2)}) collective-permute-start(f32[320,128]{1,0:T(8,128)S(1)} %convert_add_fusion.4.own_ref), channel_id=1, source_target_pairs={{0,1},{1,0},{2,3},{3,2},{4,5},{5,4},{6,7},{7,6},{8,9},{9,8},{10,11... | collective-permute-start | bytes 491528 | tf_op jit(solution)/shard_map/ppermute | solution.py:710
  73.0 8.4 %collective-permute-start.22 = (bf16[128,512]{1,0:T(8,128)(2,1)S(1)}, bf16[128,512]{1,0:T(8,128)(2,1)S(1)}, u32[]{:S(2)}, u32[]{:S(2)}) collective-permute-start(bf16[128,512]{1,0:T(8,128)(2,1)S(1)} %pad_maximum_fusion.2), channel_id=1, source_target_pairs={{0,8},{2,10},{4,12},{6,14},{8,0},{10,2},{12,4},{14,6},{1,9},{3,11}... | collective-permute-start | bytes 393224 | tf_op jit(solution)/shard_map/ppermute | solution.py:710
  79.7 1.7 %slice-start = ((f32[128,512]{1,0:T(8,128)}), f32[64,512]{1,0:T(8,128)S(1)}, s32[]{:S(2)}) async-start(f32[128,512]{1,0:T(8,128)} %copy-done.10), calls=%async_computation | async-start | bytes 262144 | tf_op jit(solution)/shard_map/slice | solution.py:723
  (3 other events, 3.4 us)

commit v6 on v5

--- a/solution.py
+++ b/solution.py
@@ -795,7 +795,7 @@
     (merged_front, attn, gram, scale, block, mixed_all, front_target, front_taps, mine, other, carry) = front_call(
         here, sharp, energy_own, energy_far, v2, u2, around, proj, taps, tile, head_size, piece_rows, cols, early
     )
-    halves = [swap(x, "row", bits[0]) for x in jnp.split(other, 2)]
+    halves = [swap(x, "row", bits[0]) for x in jnp.split(other, [other.shape[0] * 3 // 8])]
     first = halves[:1]
     front_mine = mine
     merged_back, target, grad, mine, other = back_call(

time: 82.4 us -> 81.5 us (0.989)
  starting transfers between devices: 25.7 us -> 22.8 us
  waiting for transfers between devices: 26.6 us -> 28.7 us
    ppermute x22, starting transfers between devices: 25 us -> 22.1 us  [swap(): lax.ppermute(x, axis, [(i, i ^ bit) for i in range(lax.axis_size(axis))])]
    ppermute x22, waiting for transfers between devices: 26.6 us -> 28.7 us  [swap(): lax.ppermute(x, axis, [(i, i ^ bit) for i in range(lax.axis_size(axis))])]
where the time goes in v6:
time: 81.5 us; the launch traced here: 81.4 us
  waiting for transfers between devices  28.7 us (35%)
  Pallas kernels  23.4 us (29%)
  starting transfers between devices  22.8 us (28%)
  local copies, waits for them, and re-layouts  3.7 us (5%)
  other arithmetic  1.64 us (2%)
  between operations  1.07 us (1%)
    ppermute x22, waiting for transfers between devices, swap(): lax.ppermute(x, axis, [(i, i ^ bit) for i in range(lax.axis_size(axis))])  28.7 us
    ppermute x22, starting transfers between devices, swap(): lax.ppermute(x, axis, [(i, i ^ bit) for i in range(lax.axis_size(axis))])  22.1 us
    pallas_call x1, Pallas kernels, back_call(): pl.pallas_call(functools.partial(back_kernel, head_size, tile, span), in_...  8.12 us
    pallas_call x1, Pallas kernels, front_call(): pl.pallas_call(functools.partial(front_kernel, head_size, tile, piece_row...  8.07 us
    unnamed x22, local copies, waits for them, and re-layouts  3.47 us
    pallas_call x1, Pallas kernels, final_call(): pl.pallas_call(functools.partial(final_kernel, head_size), grid=(2,), in_...  2.76 us
    pallas_call x1, Pallas kernels, content_call(): pl.pallas_call(content_kernel, grid=(2,), in_specs=[LOCAL] * 4 + [pl.Bloc...  1.65 us
  transfers between devices with their start and end apart: 23, of which 12 were waited for; matrix products, arithmetic and copies ran while one was open for 1% of the time, Pallas kernels for 18%

profile of v6, /device:TPU:0, one launch (start us, length us, event | category | flops | bytes accessed | tf_op | source)
XLA Modules:
  0.0 81.4 jit_solution(1413901236014301546)
XLA Ops:
  0.7 1.4 %copy-done.3 = bf16[16,32,1024]{2,1,0:T(8,128)(2,1)S(1)} copy-done((bf16[16,32,1024]{2,1,0:T(8,128)(2,1)S(1)}, bf16[16,32,1024]{2,1,0:T(8,128)(2,1)}, u32[]{:S(2)}) %copy-start.3) | copy-done | bytes 1048600
  2.0 1.2 %copy-done.5 = bf16[16,32,1024]{2,1,0:T(8,128)(2,1)S(1)} copy-done((bf16[16,32,1024]{2,1,0:T(8,128)(2,1)S(1)}, bf16[16,32,1024]{2,1,0:T(8,128)(2,1)}, u32[]{:S(2)}) %copy-start.5) | copy-done | bytes 1048600
  3.3 0.9 %gram.1 = (f32[272,128]{1,0:T(8,128)S(1)}, f32[272,128]{1,0:T(8,128)S(1)}) custom-call(bf16[512,1024]{1,0:T(8,128)(2,1)S(1)} %bitcast.18, bf16[512,1024]{1,0:T(8,128)(2,1)S(1)} %bitcast.20), custom_call_target="tpu_custom_call" | custom-call | bytes 9000000 | tf_op jit(solution)/shard_map/gram/pallas_call | solution.py:156
  4.7 1.0 %collective-permute-done.1 = f32[272,128]{1,0:T(8,128)S(1)} collective-permute-done((f32[272,128]{1,0:T(8,128)S(1)}, f32[272,128]{1,0:T(8,128)S(1)}, u32[]{:S(2)}, u32[]{:S(2)}) %collective-permute-start.1) | collective-permute-done | bytes 139296 | tf_op jit(solution)/shard_map/ppermute | solution.py:710
  5.7 2.9 %collective-permute-start.2 = (f32[272,128]{1,0:T(8,128)S(1)}, f32[272,128]{1,0:T(8,128)S(1)}, u32[]{:S(2)}, u32[]{:S(2)}) collective-permute-start(f32[272,128]{1,0:T(8,128)S(1)} %add.54), channel_id=1, source_target_pairs={{0,2},{2,0},{4,6},{6,4},{8,10},{10,8},{12,14},{14,12},{1,3},{3,1},... | collective-permute-start | bytes 417800 | tf_op jit(solution)/shard_map/ppermute | solution.py:710
  8.9 3.8 %collective-permute-done.2 = f32[272,128]{1,0:T(8,128)S(1)} collective-permute-done((f32[272,128]{1,0:T(8,128)S(1)}, f32[272,128]{1,0:T(8,128)S(1)}, u32[]{:S(2)}, u32[]{:S(2)}) %collective-permute-start.2) | collective-permute-done | bytes 139296 | tf_op jit(solution)/shard_map/ppermute | solution.py:710
  12.7 2.9 %collective-permute-start.3 = (f32[272,128]{1,0:T(8,128)S(1)}, f32[272,128]{1,0:T(8,128)S(1)}, u32[]{:S(2)}, u32[]{:S(2)}) collective-permute-start(f32[272,128]{1,0:T(8,128)S(1)} %add.55), channel_id=1, source_target_pairs={{0,8},{2,10},{4,12},{6,14},{8,0},{10,2},{12,4},{14,6},{1,9},{3,11}... | collective-permute-start | bytes 417800 | tf_op jit(solution)/shard_map/ppermute | solution.py:710
  16.2 1.6 %collective-permute-start.5 = (bf16[3,32,1024]{2,1,0:T(8,128)(2,1)S(1)}, bf16[3,32,1024]{2,1,0:T(8,128)(2,1)S(1)}, u32[]{:S(2)}, u32[]{:S(2)}) collective-permute-start(bf16[3,32,1024]{2,1,0:T(8,128)(2,1)S(1)} %get-tuple-element.53), channel_id=1, source_target_pairs={{0,2},{2,0},{4,6},{6,4},{8,10},{10,8},{12,14},{14,12},{1,3},{3,1},... | collective-permute-start | bytes 589832 | tf_op jit(solution)/shard_map/ppermute | solution.py:710
  17.8 0.7 collective-permute-start.6
  18.5 3.4 %collective-permute-done.3 = f32[272,128]{1,0:T(8,128)S(1)} collective-permute-done((f32[272,128]{1,0:T(8,128)S(1)}, f32[272,128]{1,0:T(8,128)S(1)}, u32[]{:S(2)}, u32[]{:S(2)}) %collective-permute-start.3) | collective-permute-done | bytes 139296 | tf_op jit(solution)/shard_map/ppermute | solution.py:710
  22.5 6.6 %collective-permute-done.4 = f32[272,128]{1,0:T(8,128)S(1)} collective-permute-done((f32[272,128]{1,0:T(8,128)S(1)}, f32[272,128]{1,0:T(8,128)S(1)}, u32[]{:S(2)}, u32[]{:S(2)}) %collective-permute-start.4) | collective-permute-done | bytes 139296 | tf_op jit(solution)/shard_map/ppermute | solution.py:710
  29.8 0.9 %collective-permute-done.7 = bf16[6,8,1024]{2,1,0:T(8,128)(2,1)S(1)} collective-permute-done((bf16[6,8,1024]{2,1,0:T(8,128)(2,1)S(1)}, bf16[6,8,1024]{2,1,0:T(8,128)(2,1)S(1)}, u32[]{:S(2)}, u32[]{:S(2)}) %collective-permute-start.7) | collective-permute-done | bytes 98336 | tf_op jit(solution)/shard_map/ppermute | solution.py:710
  30.8 8.1 %front.1 = (bf16[512,512]{1,0:T(8,128)(2,1)S(1)}, f32[512,128]{1,0:T(8,128)S(1)}, f32[512,128]{1,0:T(8,128)S(1)}, f32[512,128]{1,0:T(8,128)S(1)}, bf16[1024,256]...) custom-call(s32[2]{0:T(128)S(1)} %pad_add_fusion.here_ref.col_ref, ...), custom_call_target="tpu_custom_call" | custom-call | bytes 36000000 | tf_op jit(solution)/shard_map/front/pallas_call | solution.py:515
  39.0 2.1 %collective-permute-start.14 = (bf16[320,512]{1,0:T(8,128)(2,1)S(1)}, bf16[320,512]{1,0:T(8,128)(2,1)S(1)}, u32[]{:S(2)}, u32[]{:S(2)}) collective-permute-start(bf16[320,512]{1,0:T(8,128)(2,1)S(1)} %split.13), channel_id=1, source_target_pairs={{0,2},{2,0},{4,6},{6,4},{8,10},{10,8},{12,14},{14,12},{1,3},{3,1},... | collective-permute-start | bytes 983048 | tf_op jit(solution)/shard_map/ppermute | solution.py:710
  41.1 8.1 %back.1 = (bf16[512,512]{1,0:T(8,128)(2,1)S(1)}, bf16[512,512]{1,0:T(8,128)(2,1)S(1)}, bf16[512,1024]{1,0:T(8,128)(2,1)S(1)}, f32[320,128]{1,0:T(8,128)S(1)}, bf16[320,128]{1,0:T(8,128)(2,1)S(1)}) custom-call(s32[2]{0:T(128)S(1)} %pad_add_fusion.here_ref.col_ref, bf16[512,1024]{1,0:T(8,128)(2,1)S(1)} %bitcast.15, bf16[512,1024]{1,0:T(8,128)(2,1)S(1)} %bitcast.17, ...), custom_call_target="tpu_custom_call" | custom-call | bytes 36000000 | tf_op jit(solution)/shard_map/back/pallas_call | solution.py:540
  49.3 1.3 %collective-permute-done.10.after_ref = bf16[320,128]{1,0:T(8,128)(2,1)S(1)} collective-permute-done((bf16[320,128]{1,0:T(8,128)(2,1)S(1)}, bf16[320,128]{1,0:T(8,128)(2,1)S(1)}, u32[]{:S(2)}, u32[]{:S(2)}) %collective-permute-start.10) | collective-permute-done | bytes 81952 | tf_op jit(solution)/shard_map/ppermute | solution.py:710
  50.6 1.3 %projector.1 = (f32[512,512]{1,0:T(8,128)S(1)}, bf16[512,512]{1,0:T(8,128)(2,1)S(1)}) custom-call(s32[2]{0:T(128)S(1)} %pad_add_fusion.here_ref.col_ref, bf16[800,1024]{1,0:T(8,128)(2,1)S(1)} %get-tuple-element.59.mixed_all, bf16[512,512]{1,0:T(8,128)(2,1)S(1)} %get-tuple-element.72.target_ref, bf16[320,128]{1,0:T(8,128)(2,1)S(1)} %collective-permute-done.10.after_ref), custom_call_target="tpu_custom_call" | custom-call | bytes 7200000 | tf_op jit(solution)/shard_map/projector/pallas_call | solution.py:562
  52.5 0.6 collective-permute-done.14
  53.3 3.6 %collective-permute-done.11 = bf16[320,128]{1,0:T(8,128)(2,1)S(1)} collective-permute-done((bf16[320,128]{1,0:T(8,128)(2,1)S(1)}, bf16[320,128]{1,0:T(8,128)(2,1)S(1)}, u32[]{:S(2)}, u32[]{:S(2)}) %collective-permute-start.11) | collective-permute-done | bytes 81952 | tf_op jit(solution)/shard_map/ppermute | solution.py:710
  57.1 0.7 collective-permute-start.13
  57.9 1.8 %collective-permute-start.16 = (bf16[128,512]{1,0:T(8,128)(2,1)S(1)}, bf16[128,512]{1,0:T(8,128)(2,1)S(1)}, u32[]{:S(2)}, u32[]{:S(2)}) collective-permute-start(bf16[128,512]{1,0:T(8,128)(2,1)S(1)} %get-tuple-element.95), channel_id=1, source_target_pairs={{0,4},{2,6},{4,0},{6,2},{8,12},{10,14},{12,8},{14,10},{1,5},{3,7},... | collective-permute-start | bytes 393224 | tf_op jit(solution)/shard_map/ppermute | solution.py:710
  59.7 1.2 %collective-permute-start.18 = (bf16[128,512]{1,0:T(8,128)(2,1)S(1)}, bf16[128,512]{1,0:T(8,128)(2,1)S(1)}, u32[]{:S(2)}, u32[]{:S(2)}) collective-permute-start(bf16[128,512]{1,0:T(8,128)(2,1)S(1)} %get-tuple-element.96), channel_id=1, source_target_pairs={{0,6},{2,4},{4,2},{6,0},{8,14},{10,12},{12,10},{14,8},{1,7},{3,5},... | collective-permute-start | bytes 393224 | tf_op jit(solution)/shard_map/ppermute | solution.py:710
  61.8 2.9 %collective-permute-start.15 = (bf16[320,128]{1,0:T(8,128)(2,1)S(1)}, bf16[320,128]{1,0:T(8,128)(2,1)S(1)}, u32[]{:S(2)}, u32[]{:S(2)}) collective-permute-start(bf16[320,128]{1,0:T(8,128)(2,1)S(1)} %convert_add_fusion.5), channel_id=1, source_target_pairs={{0,8},{2,10},{4,12},{6,14},{8,0},{10,2},{12,4},{14,6},{1,9},{3,11}... | collective-permute-start | bytes 245768 | tf_op jit(solution)/shard_map/ppermute | solution.py:710
  64.7 1.7 %collective-permute-done.18 = bf16[128,512]{1,0:T(8,128)(2,1)S(1)} collective-permute-done((bf16[128,512]{1,0:T(8,128)(2,1)S(1)}, bf16[128,512]{1,0:T(8,128)(2,1)S(1)}, u32[]{:S(2)}, u32[]{:S(2)}) %collective-permute-start.18) | collective-permute-done | bytes 131104 | tf_op jit(solution)/shard_map/ppermute | solution.py:710
  66.4 1.3 %collective-permute-done.17 = bf16[128,512]{1,0:T(8,128)(2,1)S(1)} collective-permute-done((bf16[128,512]{1,0:T(8,128)(2,1)S(1)}, bf16[128,512]{1,0:T(8,128)(2,1)S(1)}, u32[]{:S(2)}, u32[]{:S(2)}) %collective-permute-start.17) | collective-permute-done | bytes 131104 | tf_op jit(solution)/shard_map/ppermute | solution.py:710
  67.9 0.6 collective-permute-start.21
  68.7 4.3 %collective-permute-done.21 = bf16[128,512]{1,0:T(8,128)(2,1)S(1)} collective-permute-done((bf16[128,512]{1,0:T(8,128)(2,1)S(1)}, bf16[128,512]{1,0:T(8,128)(2,1)S(1)}, u32[]{:S(2)}, u32[]{:S(2)}) %collective-permute-start.21) | collective-permute-done | bytes 131104 | tf_op jit(solution)/shard_map/ppermute | solution.py:710
  73.1 2.2 %collective-permute-start.22 = (bf16[128,512]{1,0:T(8,128)(2,1)S(1)}, bf16[128,512]{1,0:T(8,128)(2,1)S(1)}, u32[]{:S(2)}, u32[]{:S(2)}) collective-permute-start(bf16[128,512]{1,0:T(8,128)(2,1)S(1)} %pad_maximum_fusion.2), channel_id=1, source_target_pairs={{0,8},{2,10},{4,12},{6,14},{8,0},{10,2},{12,4},{14,6},{1,9},{3,11}... | collective-permute-start | bytes 393224 | tf_op jit(solution)/shard_map/ppermute | solution.py:710
  75.3 2.8 %final.1 = (bf16[512,1024]{1,0:T(8,128)(2,1)}, bf16[512,1024]{1,0:T(8,128)(2,1)}, f32[16]{0:T(128)}, f32[9,1024]{1,0:T(8,128)}) custom-call(s32[2]{0:T(128)S(1)} %pad_add_fusion.here_ref.col_ref, f32[16]{0:T(128)S(1)} %copy-done.9, f32[320,128]{1,0:T(8,128)S(1)} %convert_add_fusion.4.own_ref, f32[320,128]{1,0:T(8,128)S(1)} %collective-permute-done.19.far_ref, ...), custom_call_target="tpu_custom_call" | custom-call | bytes 18000000 | tf_op jit(solution)/shard_map/final/pallas_call | solution.py:686
  78.1 0.8 %copy-done.8 = f32[9,1024]{1,0:T(8,128)S(1)} copy-done((f32[9,1024]{1,0:T(8,128)S(1)}, f32[9,1024]{1,0:T(8,128)}, u32[]{:S(2)}) %copy-start.8) | copy-done | bytes 36888
  78.9 1.6 %content.1 = (bf16[512,1024]{1,0:T(8,128)(2,1)}, bf16[512,1024]{1,0:T(8,128)(2,1)}) custom-call(bf16[512,1024]{1,0:T(8,128)(2,1)S(1)} %get-tuple-element.63.grad_ref, bf16[1024,256]{1,0:T(8,128)(2,1)S(1)} %get-tuple-element.64.block_ref, bf16[512,512]{1,0:T(8,128)(2,1)S(1)} %get-tuple-element.65.merged_front, ...), custom_call_target="tpu_custom_call" | custom-call | bytes 7200000 | tf_op jit(solution)/shard_map/content/pallas_call | solution.py:592
  80.6 0.7 pad_maximum_fusion.1
  (78 shorter events, 5.2 us)
Async XLA Ops:
  0.6 8.0 %copy-start = (bf16[16,32,1024]{2,1,0:T(8,128)(2,1)S(1)}, bf16[16,32,1024]{2,1,0:T(8,128)(2,1)}, u32[]{:S(2)}) copy-start(bf16[16,32,1024]{2,1,0:T(8,128)(2,1)} %u_tail.1) | copy-start | bytes 3145732
  0.6 8.0 %copy-start.1 = (bf16[16,32,1024]{2,1,0:T(8,128)(2,1)S(1)}, bf16[16,32,1024]{2,1,0:T(8,128)(2,1)}, u32[]{:S(2)}) copy-start(bf16[16,32,1024]{2,1,0:T(8,128)(2,1)} %v_tail.1) | copy-start | bytes 3145732
  4.2 1.5 %collective-permute-start.1 = (f32[272,128]{1,0:T(8,128)S(1)}, f32[272,128]{1,0:T(8,128)S(1)}, u32[]{:S(2)}, u32[]{:S(2)}) collective-permute-start(f32[272,128]{1,0:T(8,128)S(1)} %get-tuple-element.52), channel_id=1, source_target_pairs={{0,1},{1,0},{2,3},{3,2},{4,5},{5,4},{6,7},{7,6},{8,9},{9,8},{10,11... | collective-permute-start | bytes 417800 | tf_op jit(solution)/shard_map/ppermute | solution.py:710
  5.7 6.9 %collective-permute-start.2 = (f32[272,128]{1,0:T(8,128)S(1)}, f32[272,128]{1,0:T(8,128)S(1)}, u32[]{:S(2)}, u32[]{:S(2)}) collective-permute-start(f32[272,128]{1,0:T(8,128)S(1)} %add.54), channel_id=1, source_target_pairs={{0,2},{2,0},{4,6},{6,4},{8,10},{10,8},{12,14},{14,12},{1,3},{3,1},... | collective-permute-start | bytes 417800 | tf_op jit(solution)/shard_map/ppermute | solution.py:710
  8.8 21.1 %collective-permute-start = (bf16[32,8,1024]{2,1,0:T(8,128)(2,1)S(1)}, bf16[32,8,1024]{2,1,0:T(8,128)(2,1)S(1)}, u32[]{:S(2)}, u32[]{:S(2)}) collective-permute-start(bf16[32,8,1024]{2,1,0:T(8,128)(2,1)S(1)} %pad_maximum_fusion), channel_id=1, source_target_pairs={{0,1},{1,0},{2,3},{3,2},{4,5},{5,4},{6,7},{7,6},{8,9},{9,8},{10,11... | collective-permute-start | bytes 1572872 | tf_op jit(solution)/shard_map/ppermute | solution.py:710
  12.7 9.2 %collective-permute-start.3 = (f32[272,128]{1,0:T(8,128)S(1)}, f32[272,128]{1,0:T(8,128)S(1)}, u32[]{:S(2)}, u32[]{:S(2)}) collective-permute-start(f32[272,128]{1,0:T(8,128)S(1)} %add.55), channel_id=1, source_target_pairs={{0,8},{2,10},{4,12},{6,14},{8,0},{10,2},{12,4},{14,6},{1,9},{3,11}... | collective-permute-start | bytes 417800 | tf_op jit(solution)/shard_map/ppermute | solution.py:710
  15.6 15.2 %copy-start.7 = (f32[9,1024]{1,0:T(8,128)S(1)}, f32[9,1024]{1,0:T(8,128)}, u32[]{:S(2)}) copy-start(f32[9,1024]{1,0:T(8,128)} %taps_ref.3) | copy-start | bytes 110596
  16.2 14.6 %copy-start.2 = (bf16[1024,1024]{1,0:T(8,128)(2,1)S(1)}, bf16[1024,1024]{1,0:T(8,128)(2,1)}, u32[]{:S(2)}) copy-start(bf16[1024,1024]{1,0:T(8,128)(2,1)} %proj_ref.3) | copy-start | bytes 6291460
  16.2 14.6 %copy-start.9 = (f32[16]{0:T(128)S(1)}, f32[16]{0:T(128)}, u32[]{:S(2)}) copy-start(f32[16]{0:T(128)} %sharp_ref.3) | copy-start | bytes 196
  16.2 12.9 %collective-permute-start.5 = (bf16[3,32,1024]{2,1,0:T(8,128)(2,1)S(1)}, bf16[3,32,1024]{2,1,0:T(8,128)(2,1)S(1)}, u32[]{:S(2)}, u32[]{:S(2)}) collective-permute-start(bf16[3,32,1024]{2,1,0:T(8,128)(2,1)S(1)} %get-tuple-element.53), channel_id=1, source_target_pairs={{0,2},{2,0},{4,6},{6,4},{8,10},{10,8},{12,14},{14,12},{1,3},{3,1},... | collective-permute-start | bytes 589832 | tf_op jit(solution)/shard_map/ppermute | solution.py:710
  17.8 11.3 %collective-permute-start.6 = (bf16[3,32,1024]{2,1,0:T(8,128)(2,1)S(1)}, bf16[3,32,1024]{2,1,0:T(8,128)(2,1)S(1)}, u32[]{:S(2)}, u32[]{:S(2)}) collective-permute-start(bf16[3,32,1024]{2,1,0:T(8,128)(2,1)S(1)} %get-tuple-element.56), channel_id=1, source_target_pairs={{2,4},{6,8},{10,12},{4,2},{8,6},{12,10},{3,5},{7,9},{11,13},{5,3},... | collective-permute-start | bytes 589832 | tf_op jit(solution)/shard_map/ppermute | solution.py:787
  21.9 7.1 %collective-permute-start.4 = (f32[272,128]{1,0:T(8,128)S(1)}, f32[272,128]{1,0:T(8,128)S(1)}, u32[]{:S(2)}, u32[]{:S(2)}) collective-permute-start(f32[272,128]{1,0:T(8,128)S(1)} %add.56), channel_id=1, source_target_pairs={{0,4},{2,6},{4,0},{6,2},{8,12},{10,14},{12,8},{14,10},{1,5},{3,7},... | collective-permute-start | bytes 417800 | tf_op jit(solution)/shard_map/ppermute | solution.py:710
  29.2 1.6 %collective-permute-start.8 = (f32[272,128]{1,0:T(8,128)S(1)}, f32[272,128]{1,0:T(8,128)S(1)}, u32[]{:S(2)}, u32[]{:S(2)}) collective-permute-start(f32[272,128]{1,0:T(8,128)S(1)} %add.57.own_ref.energy_own_ref), channel_id=1, source_target_pairs={{0,1},{1,0},{2,3},{3,2},{4,5},{5,4},{6,7},{7,6},{8,9},{9,8},{10,11... | collective-permute-start | bytes 417800 | tf_op jit(solution)/shard_map/ppermute | solution.py:710
  29.3 1.5 %collective-permute-start.7 = (bf16[6,8,1024]{2,1,0:T(8,128)(2,1)S(1)}, bf16[6,8,1024]{2,1,0:T(8,128)(2,1)S(1)}, u32[]{:S(2)}, u32[]{:S(2)}) collective-permute-start(bf16[6,8,1024]{2,1,0:T(8,128)(2,1)S(1)} %fusion.2), channel_id=1, source_target_pairs={{0,1},{1,0},{2,3},{3,2},{4,5},{5,4},{6,7},{7,6},{8,9},{9,8},{10,11... | collective-permute-start | bytes 294920 | tf_op jit(solution)/shard_map/ppermute | solution.py:710
  38.9 10.3 %collective-permute-start.9 = (bf16[192,512]{1,0:T(8,128)(2,1)S(1)}, bf16[192,512]{1,0:T(8,128)(2,1)S(1)}, u32[]{:S(2)}, u32[]{:S(2)}) collective-permute-start(bf16[192,512]{1,0:T(8,128)(2,1)S(1)} %split.12), channel_id=1, source_target_pairs={{0,2},{2,0},{4,6},{6,4},{8,10},{10,8},{12,14},{14,12},{1,3},{3,1},... | collective-permute-start | bytes 589832 | tf_op jit(solution)/shard_map/ppermute | solution.py:710
  39.0 14.1 %collective-permute-start.14 = (bf16[320,512]{1,0:T(8,128)(2,1)S(1)}, bf16[320,512]{1,0:T(8,128)(2,1)S(1)}, u32[]{:S(2)}, u32[]{:S(2)}) collective-permute-start(bf16[320,512]{1,0:T(8,128)(2,1)S(1)} %split.13), channel_id=1, source_target_pairs={{0,2},{2,0},{4,6},{6,4},{8,10},{10,8},{12,14},{14,12},{1,3},{3,1},... | collective-permute-start | bytes 983048 | tf_op jit(solution)/shard_map/ppermute | solution.py:710
  49.2 1.3 %collective-permute-start.10 = (bf16[320,128]{1,0:T(8,128)(2,1)S(1)}, bf16[320,128]{1,0:T(8,128)(2,1)S(1)}, u32[]{:S(2)}, u32[]{:S(2)}) collective-permute-start(bf16[320,128]{1,0:T(8,128)(2,1)S(1)} %get-tuple-element.71), channel_id=1, source_target_pairs={{0,1},{1,0},{2,3},{3,2},{4,5},{5,4},{6,7},{7,6},{8,9},{9,8},{10,11... | collective-permute-start | bytes 245768 | tf_op jit(solution)/shard_map/ppermute | solution.py:710
  51.9 5.1 %collective-permute-start.12 = (bf16[512,512]{1,0:T(8,128)(2,1)S(1)}, bf16[512,512]{1,0:T(8,128)(2,1)S(1)}, u32[]{:S(2)}, u32[]{:S(2)}) collective-permute-start(bf16[512,512]{1,0:T(8,128)(2,1)S(1)} %get-tuple-element.74), channel_id=1, source_target_pairs={{0,1},{1,0},{2,3},{3,2},{4,5},{5,4},{6,7},{7,6},{8,9},{9,8},{10,11... | collective-permute-start | bytes 1572872 | tf_op jit(solution)/shard_map/ppermute | solution.py:710
  52.1 4.8 %collective-permute-start.11 = (bf16[320,128]{1,0:T(8,128)(2,1)S(1)}, bf16[320,128]{1,0:T(8,128)(2,1)S(1)}, u32[]{:S(2)}, u32[]{:S(2)}) collective-permute-start(bf16[320,128]{1,0:T(8,128)(2,1)S(1)} %add_convert_fusion), channel_id=1, source_target_pairs={{0,4},{2,6},{4,0},{6,2},{8,12},{10,14},{12,8},{14,10},{1,5},{3,7},... | collective-permute-start | bytes 245768 | tf_op jit(solution)/shard_map/ppermute | solution.py:710
  57.1 4.5 %collective-permute-start.13 = (bf16[320,128]{1,0:T(8,128)(2,1)S(1)}, bf16[320,128]{1,0:T(8,128)(2,1)S(1)}, u32[]{:S(2)}, u32[]{:S(2)}) collective-permute-start(bf16[320,128]{1,0:T(8,128)(2,1)S(1)} %convert_add_fusion.6), channel_id=1, source_target_pairs={{0,2},{2,0},{4,6},{6,4},{8,10},{10,8},{12,14},{14,12},{1,3},{3,1},... | collective-permute-start | bytes 245768 | tf_op jit(solution)/shard_map/ppermute | solution.py:710
  57.9 6.9 %collective-permute-start.16 = (bf16[128,512]{1,0:T(8,128)(2,1)S(1)}, bf16[128,512]{1,0:T(8,128)(2,1)S(1)}, u32[]{:S(2)}, u32[]{:S(2)}) collective-permute-start(bf16[128,512]{1,0:T(8,128)(2,1)S(1)} %get-tuple-element.95), channel_id=1, source_target_pairs={{0,4},{2,6},{4,0},{6,2},{8,12},{10,14},{12,8},{14,10},{1,5},{3,7},... | collective-permute-start | bytes 393224 | tf_op jit(solution)/shard_map/ppermute | solution.py:710
  59.7 6.8 %collective-permute-start.18 = (bf16[128,512]{1,0:T(8,128)(2,1)S(1)}, bf16[128,512]{1,0:T(8,128)(2,1)S(1)}, u32[]{:S(2)}, u32[]{:S(2)}) collective-permute-start(bf16[128,512]{1,0:T(8,128)(2,1)S(1)} %get-tuple-element.96), channel_id=1, source_target_pairs={{0,6},{2,4},{4,2},{6,0},{8,14},{10,12},{12,10},{14,8},{1,7},{3,5},... | collective-permute-start | bytes 393224 | tf_op jit(solution)/shard_map/ppermute | solution.py:710
  60.8 6.9 %collective-permute-start.17 = (bf16[128,512]{1,0:T(8,128)(2,1)S(1)}, bf16[128,512]{1,0:T(8,128)(2,1)S(1)}, u32[]{:S(2)}, u32[]{:S(2)}) collective-permute-start(bf16[128,512]{1,0:T(8,128)(2,1)S(1)} %get-tuple-element.97), channel_id=1, source_target_pairs={{0,2},{2,0},{4,6},{6,4},{8,10},{10,8},{12,14},{14,12},{1,3},{3,1},... | collective-permute-start | bytes 393224 | tf_op jit(solution)/shard_map/ppermute | solution.py:710
  61.7 13.6 %copy-start.4 = (bf16[16,32,1024]{2,1,0:T(8,128)(2,1)S(1)}, bf16[16,32,1024]{2,1,0:T(8,128)(2,1)}, u32[]{:S(2)}) copy-start(bf16[16,32,1024]{2,1,0:T(8,128)(2,1)} %param.7) | copy-start | bytes 3145732
  61.7 13.6 %copy-start.6 = (bf16[16,32,1024]{2,1,0:T(8,128)(2,1)S(1)}, bf16[16,32,1024]{2,1,0:T(8,128)(2,1)}, u32[]{:S(2)}) copy-start(bf16[16,32,1024]{2,1,0:T(8,128)(2,1)} %param.8) | copy-start | bytes 3145732
  61.7 6.1 %collective-permute-start.20 = (bf16[256,512]{1,0:T(8,128)(2,1)S(1)}, bf16[256,512]{1,0:T(8,128)(2,1)S(1)}, u32[]{:S(2)}, u32[]{:S(2)}) collective-permute-start(bf16[256,512]{1,0:T(8,128)(2,1)S(1)} %slice.87), channel_id=1, source_target_pairs={{0,1},{1,0},{2,3},{3,2},{4,5},{5,4},{6,7},{7,6},{8,9},{9,8},{10,11... | collective-permute-start | bytes 786440 | tf_op jit(solution)/shard_map/ppermute | solution.py:710
  61.8 6.8 %collective-permute-start.15 = (bf16[320,128]{1,0:T(8,128)(2,1)S(1)}, bf16[320,128]{1,0:T(8,128)(2,1)S(1)}, u32[]{:S(2)}, u32[]{:S(2)}) collective-permute-start(bf16[320,128]{1,0:T(8,128)(2,1)S(1)} %convert_add_fusion.5), channel_id=1, source_target_pairs={{0,8},{2,10},{4,12},{6,14},{8,0},{10,2},{12,4},{14,6},{1,9},{3,11}... | collective-permute-start | bytes 245768 | tf_op jit(solution)/shard_map/ppermute | solution.py:710
  67.8 10.3 %copy-start.10 = (f32[128,512]{1,0:T(8,128)}, f32[128,512]{1,0:T(8,128)S(1)}, u32[]{:S(2)}) copy-start(f32[128,512]{1,0:T(8,128)S(1)} %convert_add_fusion.3) | copy-start | bytes 786436
  67.9 5.0 %collective-permute-start.21 = (bf16[128,512]{1,0:T(8,128)(2,1)S(1)}, bf16[128,512]{1,0:T(8,128)(2,1)S(1)}, u32[]{:S(2)}, u32[]{:S(2)}) collective-permute-start(bf16[128,512]{1,0:T(8,128)(2,1)S(1)} %slice.88), channel_id=1, source_target_pairs={{0,4},{2,6},{4,0},{6,2},{8,12},{10,14},{12,8},{14,10},{1,5},{3,7},... | collective-permute-start | bytes 393224 | tf_op jit(solution)/shard_map/ppermute | solution.py:710
  68.6 6.7 %collective-permute-start.19 = (f32[320,128]{1,0:T(8,128)S(1)}, f32[320,128]{1,0:T(8,128)S(1)}, u32[]{:S(2)}, u32[]{:S(2)}) collective-permute-start(f32[320,128]{1,0:T(8,128)S(1)} %convert_add_fusion.4.own_ref), channel_id=1, source_target_pairs={{0,1},{1,0},{2,3},{3,2},{4,5},{5,4},{6,7},{7,6},{8,9},{9,8},{10,11... | collective-permute-start | bytes 491528 | tf_op jit(solution)/shard_map/ppermute | solution.py:710
  73.1 7.5 %collective-permute-start.22 = (bf16[128,512]{1,0:T(8,128)(2,1)S(1)}, bf16[128,512]{1,0:T(8,128)(2,1)S(1)}, u32[]{:S(2)}, u32[]{:S(2)}) collective-permute-start(bf16[128,512]{1,0:T(8,128)(2,1)S(1)} %pad_maximum_fusion.2), channel_id=1, source_target_pairs={{0,8},{2,10},{4,12},{6,14},{8,0},{10,2},{12,4},{14,6},{1,9},{3,11}... | collective-permute-start | bytes 393224 | tf_op jit(solution)/shard_map/ppermute | solution.py:710
  78.9 1.7 %slice-start = ((f32[128,512]{1,0:T(8,128)}), f32[64,512]{1,0:T(8,128)S(1)}, s32[]{:S(2)}) async-start(f32[128,512]{1,0:T(8,128)} %copy-done.10), calls=%async_computation | async-start | bytes 262144 | tf_op jit(solution)/shard_map/slice | solution.py:723
  (3 other events, 3.4 us)
